TPU v7x, 128 devices: a whole 4x4x4 slice. The times are simulated.
128 devices in a mesh: ctx: 32 (over y, z_lo, x), dp: 4 (over z_hi, core).
Axes of the slice: x: 4, y: 4, z: 4 (z_hi: 2, z_lo: 2; z = z_hi * 2 + z_lo), core: 2. Of those that a mesh axis runs over, the one named last changes fastest.
Arguments:
- q_proj: bfloat16 [4, 2, 2048, 1792], P('dp', None, 'ctx'), may hold values from -240 to 240
- k_proj: bfloat16 [4, 2, 2048, 256], P('dp', None, 'ctx'), may hold values from -12 to 12
- v_proj: bfloat16 [4, 2, 2048, 256], P('dp', None, 'ctx'), may hold values from -6 to 6
- q_bias: float32 [1792], replicated, may hold values from -4 to 4
- v_bias: float32 [256], replicated, may hold values from -2.5 to 2.5
- cotangent: bfloat16 [4, 2, 2048, 1792], P('dp', None, 'ctx'), may hold values from -6 to 6
- lengths: int32 [4, 16], P('dp'), may hold values from 1 to 1024, 4096 in all within a row
Outputs:
- attended: bfloat16 [4, 2, 2048, 1792], P('dp', None, 'ctx')
- q_grad: bfloat16 [4, 2, 2048, 1792], P('dp', None, 'ctx')
- k_grad: bfloat16 [4, 2, 2048, 256], P('dp', None, 'ctx')
- v_grad: bfloat16 [4, 2, 2048, 256], P('dp', None, 'ctx')
- q_bias_grad: float32 [1792], replicated
- v_bias_grad: float32 [256], replicated
Inputs may be any that keep to these rules, and one draw needn't show every extreme that they name: `lengths`: each row sums to 4096; the longest document of each row has exactly 1024 tokens.
All inputs are finite; a program needn't handle non-finite values.
Results may differ from a plain program's by a relative error of at most 0.012.
Values may be sent and summed in bfloat16 or wider, within the bound.
No kernel may reach another device: no remote copies, remote signals or barrier semaphores. Data moves between devices by JAX's collectives and lax.ppermute only.
A program may use at most 192 MiB of HBM per device.

v0:
```python
import math

import jax
import jax.numpy as jnp
from jax import lax
from jax.sharding import PartitionSpec as P

HD = 128
KVH = 2
GROUP = 7
HQ = 1792
KW = 256


MASKED = -1e30


def positions(row_count, group_size, block_len, offset):
    row_index = offset + jnp.arange(row_count, dtype=jnp.int32)
    later_pos = (2 * group_size - 1 - row_index // block_len) * block_len + row_index % block_len
    return jnp.stack([row_index, later_pos])


def documents(places, doc_ends):
    return jnp.sum((places[..., None] >= doc_ends).astype(jnp.int32), axis=-1)


def visible_pairs(query_pos, query_doc, key_pos, key_doc):
    return (query_doc[:, None] == key_doc[None, :]) & (key_pos[None, :] <= query_pos[:, None])


def score_tile(queries, key_tile, score_scale):
    return (
        jnp.einsum("tged,jgd->getj", queries, key_tile, preferred_element_type=jnp.float32)
        * score_scale
    )


def update_stats(carry, visible, raw_scores):
    running, totals = carry
    scores = jnp.where(visible, raw_scores, MASKED)
    newest = jnp.maximum(running, jnp.max(scores, axis=-1))
    shifted = jnp.where(visible, jnp.exp(scores - newest[..., None]), 0.0)
    return (newest, totals * jnp.exp(running - newest) + jnp.sum(shifted, axis=-1))


def on_device(q_proj, k_proj, v_proj, q_bias, v_bias, cotangent, lengths):
    group_size = lax.axis_size("ctx")
    my_index = lax.axis_index("ctx")
    block_len = q_proj.shape[2]
    half_len = block_len * group_size
    seq_len = 2 * half_len
    tok_len = 2 * block_len
    tile_len = min(512, seq_len)
    tile_count = seq_len // tile_len
    score_scale = 1.0 / math.sqrt(HD)
    doc_ends = jnp.cumsum(lengths[0])
    query_rows = (q_proj[0].astype(jnp.float32) + q_bias).astype(jnp.bfloat16)
    value_rows = (v_proj[0].astype(jnp.float32) + v_bias).astype(jnp.bfloat16)
    query_pos = positions(block_len, group_size, block_len, my_index * block_len).reshape(tok_len)
    query_doc = documents(query_pos, doc_ends)
    queries = query_rows.reshape(tok_len, KVH, GROUP, HD)
    cot_rows = cotangent[0].reshape(tok_len, KVH, GROUP, HD)
    key_value = jnp.concatenate([k_proj[0], value_rows], axis=-1)[None]
    gathered = lax.all_gather(key_value, "ctx", axis=2, tiled=True).reshape(
        tile_count, tile_len, 2, KVH, HD
    )
    key_pos = positions(half_len, group_size, block_len, 0).reshape(tile_count, tile_len)
    key_doc = documents(key_pos, doc_ends)
    tiles = (gathered[:, :, 0], gathered[:, :, 1], key_pos, key_doc)
    start_top = jnp.full((KVH, GROUP, tok_len), MASKED, jnp.float32)
    zero_sum = jnp.zeros((tok_len, KVH, GROUP, HD), jnp.float32)

    def stats_step(carry, tile):
        key_tile, value_tile, tile_pos, tile_doc = tile
        visible = visible_pairs(query_pos, query_doc, tile_pos, tile_doc)
        return (update_stats(carry, visible, score_tile(queries, key_tile, score_scale)), None)

    (running, totals), _ = lax.scan(stats_step, (start_top, jnp.zeros_like(start_top)), tiles)
    log_total = running + jnp.log(totals)

    def output_step(summed, tile):
        key_tile, value_tile, tile_pos, tile_doc = tile
        visible = visible_pairs(query_pos, query_doc, tile_pos, tile_doc)
        scores = score_tile(queries, key_tile, score_scale)
        weights = jnp.exp(jnp.where(visible, scores - log_total[..., None], MASKED)).astype(
            jnp.bfloat16
        )
        return (
            summed
            + jnp.einsum("getj,jgd->tged", weights, value_tile, preferred_element_type=jnp.float32),
            None,
        )

    summed, _ = lax.scan(output_step, zero_sum, tiles)
    attended = summed.astype(jnp.bfloat16).reshape(1, 2, block_len, HQ)
    row_delta = jnp.einsum("tged,tged->get", cot_rows.astype(jnp.float32), summed)

    def weights_of(visible, key_tile):
        scores = score_tile(queries, key_tile, score_scale)
        return jnp.exp(jnp.where(visible, scores - log_total[..., None], MASKED))

    def tile_grads(visible, key_tile, value_tile):
        weights = weights_of(visible, key_tile)
        grad_weights = jnp.einsum(
            "tged,jgd->getj", cot_rows, value_tile, preferred_element_type=jnp.float32
        )
        grad_scores = (weights * (grad_weights - row_delta[..., None])).astype(jnp.bfloat16)
        return (weights, grad_scores)

    def full_step(query_grad, tile):
        key_tile, value_tile, tile_pos, tile_doc = tile
        visible = visible_pairs(query_pos, query_doc, tile_pos, tile_doc)
        weights, grad_scores = tile_grads(visible, key_tile, value_tile)
        key_part = jnp.einsum(
            "getj,tged->jgd", grad_scores, queries, preferred_element_type=jnp.float32
        )
        value_part = jnp.einsum(
            "getj,tged->jgd",
            weights.astype(jnp.bfloat16),
            cot_rows,
            preferred_element_type=jnp.float32,
        )
        updated = query_grad + jnp.einsum(
            "getj,jgd->tged", grad_scores, key_tile, preferred_element_type=jnp.float32
        )
        return (updated, (key_part, value_part))

    zero_grad = jnp.zeros((tok_len, KVH, GROUP, HD), jnp.float32)
    query_grad, (key_parts, value_parts) = lax.scan(full_step, zero_grad, tiles)
    key_grad, value_grad = (
        lax.psum_scatter(
            key_parts.reshape(1, 2, half_len, KW), "ctx", scatter_dimension=2, tiled=True
        ),
        lax.psum_scatter(
            value_parts.reshape(1, 2, half_len, KW), "ctx", scatter_dimension=2, tiled=True
        ),
    )
    query_grad = query_grad * score_scale
    key_grad = key_grad * score_scale
    query_sum, value_sum = lax.psum(
        (
            jnp.sum(query_grad.reshape(tok_len, HQ), axis=0),
            jnp.sum(value_grad.reshape(tok_len, KW), axis=0),
        ),
        ("ctx", "dp"),
    )
    q_grad = query_grad.astype(jnp.bfloat16).reshape(1, 2, block_len, HQ)
    k_grad = key_grad.astype(jnp.bfloat16)
    v_grad = value_grad.astype(jnp.bfloat16)
    return (attended, q_grad, k_grad, v_grad, query_sum, value_sum)


def solution(mesh):
    placed = (
        P("dp", None, "ctx", None),
        P("dp", None, "ctx", None),
        P("dp", None, "ctx", None),
        P(),
        P(),
        P("dp", None, "ctx", None),
        P("dp", None),
    )
    return jax.shard_map(
        on_device,
        mesh=mesh,
        in_specs=placed,
        out_specs=(
            P("dp", None, "ctx", None),
            P("dp", None, "ctx", None),
            P("dp", None, "ctx", None),
            P("dp", None, "ctx", None),
            P(),
            P(),
        ),
        check_vma=False,
    )
```

profile of v0, /device:TPU:0, one launch (start us, length us, event | category | flops | bytes accessed | tf_op | source)
XLA Modules:
  0.0 699.5 jit_solution(14213324915598847606)
XLA Ops:
  18.5 151.9 %all-gather.3.cloned.1.call-done = bf16[2,2048,512]{2,1,0:T(8,128)(2,1)} async-done(((bf16[2,64,512]{2,1,0:T(8,128)(2,1)}), bf16[2,2048,512]{2,1,0:T(8,128)(2,1)}) %all-gather.3.cloned.1.call-update) | async-done | bytes 4194320 | tf_op jit(solution)/shard_map/all_gather | solution.py:65
  170.3 6.9 reshape.220
  177.2 5.6 slice_bitcast_fusion
  183.3 26.0 %while.42 = (s32[]{:T(128)}, f32[2,7,128]{2,1,0:T(8,128)S(1)}, f32[2,7,128]{2,1,0:T(8,128)S(1)}, s32[128]{0:T(128)}, s32[8,512]{1,0:T(8,128)}, /*index=5*/s32[8,...) while((s32[]{:T(128)}, f32[2,7,128]{2,1,0:T(8,128)S(1)}, ...), condition=%wide.wide.region_6.7_spmd.clone, body=%wide.wide.region_3.6_spmd.clone.sunk | while | flops 242426624 | bytes 8364176 | solution.py:79
  209.9 63.3 %while.43 = (s32[]{:T(128)}, f32[128,2,7,128]{0,3,2,1:T(8,128)}, bf16[8,512,2,128]{3,2,1,0:T(2,128)(2,1)}, s32[128]{0:T(128)}, s32[8,512]{1,0:T(8,128)}, /*index...) while((s32[]{:T(128)}, f32[128,2,7,128]{0,3,2,1:T(8,128)}, ...), condition=%wide.wide.region_8.9_spmd.clone, body=%wide.wide.region_7.8_spmd.clone.sunk | while | flops 474087424 | bytes 20796628 | solution.py:95
  214.1 3.4 fusion.102
  221.7 3.8 fusion.102
  229.7 3.8 fusion.102
  237.6 3.8 fusion.102
  245.6 3.8 fusion.102
  253.5 3.8 fusion.102
  261.5 3.8 fusion.102
  269.5 3.8 fusion.102
  273.2 2.6 copy.69
  275.8 2.4 multiply_reduce_fusion
  279.2 70.3 %while.44 = (s32[]{:T(128)}, f32[128,2,7,128]{0,3,2,1:T(8,128)S(1)}, f32[8,512,2,128]{3,2,1,0:T(2,128)}, f32[8,512,2,128]{3,2,1,0:T(2,128)}, bf16[8,512,2,128]{3...) while((s32[]{:T(128)}, ...), condition=%wide.wide.region_10.11_spmd.clone, body=%wide.wide.region_9.10_spmd.clone.sunk | while | flops 1184235520 | bytes 26708196 | solution.py:130
  295.0 1.8 copy_dynamic-update-slice_fusion.4
  303.8 1.8 copy_dynamic-update-slice_fusion.4
  347.7 1.8 copy_dynamic-update-slice_fusion.4
  349.5 6.4 reshape.227
  356.0 6.6 reshape.226
  367.6 156.4 %reduce-scatter.5.cloned.1.call-done = f32[1,2,64,256]{3,2,1,0:T(8,128)} async-done(((f32[1,2,2048,256]{3,2,1,0:T(8,128)}), f32[1,2,64,256]{3,2,1,0:T(8,128)}) %reduce-scatter.5.cloned.1.call-update) | async-done | bytes 131088 | tf_op jit(solution)/shard_map/reduce_scatter | solution.py:135
  525.6 63.6 %all-reduce = (f32[1792]{0:T(1024)}, f32[256]{0:T(256)}) all-reduce(f32[1792]{0:T(1024)S(1)} %reduce_sum.50, f32[256]{0:T(256)S(1)} %get-tuple-element.450), channel_id=1, replica_groups=mesh['ctx'=32,'dp'=4] {'ctx','dp'}, use_global_device_ids=true, to_apply=%region_14.15 | all-reduce | flops 2048 | bytes 16384 | tf_op jit(solution)/shard_map/psum | solution.py:141
  589.2 102.2 %reduce-scatter.3.cloned.1.call-done = f32[1,2,64,256]{3,2,1,0:T(8,128)} async-done(((f32[1,2,2048,256]{3,2,1,0:T(8,128)}), f32[1,2,64,256]{3,2,1,0:T(8,128)}) %reduce-scatter.3.cloned.1.call-update) | async-done | bytes 131088 | tf_op jit(solution)/shard_map/reduce_scatter | solution.py:132
  (270 shorter events, 144.7 us)
Async XLA Ops:
  7.2 163.2 %all-gather.3.cloned.1.call-start = ((), (), s32[]{:S(2)}) async-start(), calls=%async_computation.4 | async-start | bytes 4325376 | tf_op jit(solution)/shard_map/all_gather | solution.py:65
  9.6 514.4 %reduce-scatter.5.cloned.1.call-start = ((), (), s32[]{:S(2)}) async-start(), calls=%async_computation.3 | async-start | bytes 4325376 | tf_op jit(solution)/shard_map/reduce_scatter | solution.py:135
  9.7 167.5 %copy-start.7 = (s32[2,64]{1,0:T(2,128)}, s32[2,64]{1,0:T(2,128)S(1)}, u32[]{:S(2)}) copy-start(s32[2,64]{1,0:T(2,128)S(1)} %pad_add_fusion.1) | copy-start | bytes 1540
  14.4 2.5 copy-start.2
  214.1 3.4 copy-start.1
  221.7 3.8 copy-start.1
  225.5 1.3 copy-start
  229.7 3.8 copy-start.1
  237.6 3.8 copy-start.1
  245.6 3.8 copy-start.1
  253.5 3.8 copy-start.1
  261.5 3.8 copy-start.1
  269.5 3.8 copy-start.1
  273.2 6.0 copy-start.5
  273.2 6.0 copy-start.6
  279.3 3.5 copy-start.4
  288.0 3.5 copy-start.4
  296.8 3.5 copy-start.4
  305.6 3.5 copy-start.4
  314.4 3.5 copy-start.4
  323.2 3.5 copy-start.4
  332.0 3.5 copy-start.4
  340.7 3.5 copy-start.4
  356.0 335.4 %reduce-scatter.3.cloned.1.call-start = ((), (), s32[]{:S(2)}) async-start(), calls=%async_computation.2 | async-start | bytes 4325376 | tf_op jit(solution)/shard_map/reduce_scatter | solution.py:132
  (8 other events, 10.2 us)
Sparse Core Ops, SparseCore 0:
  10.2 160.0 all-gather.2
  356.1 167.8 reduce-scatter.4
  526.4 164.9 reduce-scatter.2
where the time goes:
time: 702 us; the launch traced here: 699 us
  waiting for transfers between devices  410 us (58%)
  local copies, waits for them, and re-layouts  103 us (15%)
  matrix products  68.5 us (10%)
  blocking collectives  63.6 us (9%)
  other arithmetic  38.8 us (6%)
  between operations  13.9 us (2%)
    reduce_scatter x1, waiting for transfers between devices, on_device(): lax.psum_scatter(value_parts.reshape(1, 2, half_len, KW), 'ctx', scatter_...  156 us
    all_gather x1, waiting for transfers between devices, on_device(): lax.all_gather(key_value, 'ctx', axis=2, tiled=True)  152 us
    reduce_scatter x1, waiting for transfers between devices, on_device(): lax.psum_scatter(key_parts.reshape(1, 2, half_len, KW), 'ctx', scatter_di...  102 us
    psum x1, blocking collectives, on_device(): lax.psum((jnp.sum(query_grad.reshape(tok_len, HQ), axis=0), jnp.sum(value...  63.6 us
    dynamic_slice x56, local copies, waits for them, and re-layouts, on_device(): lax.scan(stats_step, (start_top, jnp.zeros_like(start_top)), tiles)  43.1 us
    dot_general x8, matrix products, output_step(): jnp.einsum('getj,jgd->tged', weights, value_tile, preferred_element_type=...  29.8 us
    and x24, other arithmetic, visible_pairs(): (query_doc[:, None] == key_doc[None, :]) & (key_pos[None, :] <= query_pos...  20.9 us
    dynamic_update_slice x8, local copies, waits for them, and re-layouts, on_device(): query_grad, (key_parts, value_parts) = lax.scan(full_step, zero_grad, tiles)  14.2 us
  transfers between devices with their start and end apart: 3, of which 3 were waited for; matrix products, arithmetic and copies ran while one was open for 3% of the time, Pallas kernels for 0%

commit v1 on v0

v1 whole, which is shorter than its diff:
```python
import functools
import math

import jax
import jax.numpy as jnp
from jax import lax
from jax.experimental import pallas as pl
from jax.experimental.pallas import tpu as pltpu
from jax.sharding import PartitionSpec as P

HD = 128
KVH = 2
GROUP = 7
HQ = 1792
KW = 256
MOST = 1024

MASKED = -1e30
BLOCKS_PER_CHUNK = 4

NT = (((1,), (1,)), ((), ()))
NN = (((1,), (0,)), ((), ()))
TN = (((0,), (0,)), ((), ()))


def dot(a, b, dims):
    return lax.dot_general(a, b, dims, preferred_element_type=jnp.float32)


def attention_kernel(
    group_size,
    where_ref,
    len_ref,
    q_ref,
    ct_ref,
    qb_ref,
    kv_ref,
    att_ref,
    qg_ref,
    gr_ref,
    sum_ref,
    win_ref,
    q_rows,
    d_rows,
    p_ref,
    pb_ref,
    grad_ref,
    acc_ref,
):
    block_len = q_ref.shape[1]
    rows = GROUP * block_len
    chunk = BLOCKS_PER_CHUNK * block_len
    scale = 1.0 / math.sqrt(HD)
    log2e = 1.0 / math.log(2.0)
    last_block = 2 * group_size - 1
    me = where_ref[0]
    n_docs = len_ref.shape[1]

    gr_ref[...] = jnp.zeros_like(gr_ref)
    sum_ref[...] = jnp.zeros_like(sum_ref)

    def place(block):
        early = block < group_size
        return jnp.where(early, block, last_block - block), jnp.where(early, 0, 1)

    def query_block(h, carry):
        own = jnp.where(h == 0, me, last_block - me)
        first_pos = own * block_len
        token = lax.broadcasted_iota(jnp.int32, (1, rows), 1) % block_len
        query_pos = first_pos + token
        query_start = jnp.zeros_like(query_pos)
        end = jnp.int32(0)
        first_start = jnp.int32(0)
        for k in range(n_docs):
            end = end + len_ref[0, k]
            query_start = jnp.where(query_pos >= end, end, query_start)
            first_start = jnp.where(first_pos >= end, end, first_start)
        low = first_start // block_len
        n_blocks = own - low + 1
        n_chunks = (n_blocks + BLOCKS_PER_CHUNK - 1) // BLOCKS_PER_CHUNK

        def load(i, carry):
            c, half = place(jnp.minimum(low + i, own))
            win_ref[pl.ds(i * block_len, block_len), :] = kv_ref[c, half]
            return carry

        lax.fori_loop(0, n_chunks * BLOCKS_PER_CHUNK, load, 0)

        for g in range(KVH):
            for t in range(GROUP):
                f = (g * GROUP + t) * HD
                here = slice(t * block_len, (t + 1) * block_len)
                q_rows[here, :] = (
                    q_ref[h, :, f : f + HD].astype(jnp.float32) + qb_ref[:, f : f + HD]
                ).astype(jnp.bfloat16)
                d_rows[here, :] = ct_ref[h, :, f : f + HD]
            key_cols = slice(g * HD, (g + 1) * HD)
            value_cols = slice(KW + g * HD, KW + (g + 1) * HD)

            def score_step(i, top):
                at = pl.ds(pl.multiple_of(i * chunk, chunk), chunk)
                s = dot(win_ref[at, key_cols], q_rows[...], NT) * (scale * log2e)
                key_pos = (low * block_len + i * chunk) + lax.broadcasted_iota(
                    jnp.int32, (chunk, 1), 0
                )
                visible = (key_pos >= query_start) & (key_pos <= query_pos)
                s = jnp.where(visible, s, MASKED)
                p_ref[at, :] = s
                return jnp.maximum(top, jnp.max(s, axis=0, keepdims=True))

            top = lax.fori_loop(
                0, n_chunks, score_step, jnp.full((1, rows), MASKED, jnp.float32)
            )

            def exp_step(i, total):
                at = pl.ds(pl.multiple_of(i * chunk, chunk), chunk)
                e = jnp.exp2(p_ref[at, :] - top)
                p_ref[at, :] = e
                return total + jnp.sum(e, axis=0, keepdims=True)

            total = lax.fori_loop(0, n_chunks, exp_step, jnp.zeros((1, rows), jnp.float32))
            inverse = 1.0 / total

            acc_ref[...] = jnp.zeros_like(acc_ref)

            def out_step(i, carry):
                at = pl.ds(pl.multiple_of(i * chunk, chunk), chunk)
                p = p_ref[at, :] * inverse
                p_ref[at, :] = p
                low_p = p.astype(jnp.bfloat16)
                pb_ref[at, :] = low_p
                acc_ref[...] += dot(win_ref[at, value_cols], low_p, TN)
                return carry

            lax.fori_loop(0, n_chunks, out_step, 0)
            summed = acc_ref[...]
            delta = jnp.sum(
                summed * jnp.transpose(d_rows[...].astype(jnp.float32)), axis=0, keepdims=True
            )
            out_rows = jnp.transpose(summed).astype(jnp.bfloat16)
            for t in range(GROUP):
                f = (g * GROUP + t) * HD
                att_ref[h, :, f : f + HD] = out_rows[t * block_len : (t + 1) * block_len]

            acc_ref[...] = jnp.zeros_like(acc_ref)

            def grad_step(i, value_total):
                at = pl.ds(pl.multiple_of(i * chunk, chunk), chunk)
                dp = dot(win_ref[at, value_cols], d_rows[...], NT)
                ds = (p_ref[at, :] * (dp - delta)).astype(jnp.bfloat16)
                value_part = dot(pb_ref[at, :], d_rows[...], NN)
                grad_ref[at, value_cols] = value_part
                grad_ref[at, key_cols] = dot(ds, q_rows[...], NN) * scale
                acc_ref[...] += dot(win_ref[at, key_cols], ds, TN)
                return value_total + jnp.sum(value_part, axis=0, keepdims=True)

            value_total = lax.fori_loop(
                0, n_chunks, grad_step, jnp.zeros((1, HD), jnp.float32)
            )
            v_row = KVH * GROUP + g
            sum_ref[v_row : v_row + 1, :] += value_total
            query_grad = jnp.transpose(acc_ref[...] * scale)
            for t in range(GROUP):
                f = (g * GROUP + t) * HD
                part = query_grad[t * block_len : (t + 1) * block_len]
                qg_ref[h, :, f : f + HD] = part.astype(jnp.bfloat16)
                row = g * GROUP + t
                sum_ref[row : row + 1, :] += jnp.sum(part, axis=0, keepdims=True)

        def store(i, carry):
            c, half = place(low + i)
            part = grad_ref[pl.ds(i * block_len, block_len), :]
            gr_ref[c, half] = (gr_ref[c, half].astype(jnp.float32) + part).astype(jnp.bfloat16)
            return carry

        lax.fori_loop(0, n_blocks, store, 0)
        return carry

    lax.fori_loop(0, 2, query_block, 0)


def attention(group_size, me, lengths, q, ct, q_bias, kv):
    block_len = q.shape[1]
    rows = GROUP * block_len
    window = -(-(MOST // block_len + 1) // BLOCKS_PER_CHUNK) * BLOCKS_PER_CHUNK * block_len
    smem = pl.BlockSpec(memory_space=pltpu.SMEM)
    vmem = pl.BlockSpec(memory_space=pltpu.VMEM)
    return pl.pallas_call(
        functools.partial(attention_kernel, group_size),
        out_shape=(
            jax.ShapeDtypeStruct(q.shape, jnp.bfloat16),
            jax.ShapeDtypeStruct(q.shape, jnp.bfloat16),
            jax.ShapeDtypeStruct(kv.shape, jnp.bfloat16),
            jax.ShapeDtypeStruct((KVH * GROUP + KVH, HD), jnp.float32),
        ),
        in_specs=[smem, smem, vmem, vmem, vmem, vmem],
        out_specs=(vmem, vmem, vmem, vmem),
        scratch_shapes=[
            pltpu.VMEM((window, 2 * KW), jnp.bfloat16),
            pltpu.VMEM((rows, HD), jnp.bfloat16),
            pltpu.VMEM((rows, HD), jnp.bfloat16),
            pltpu.VMEM((window, rows), jnp.float32),
            pltpu.VMEM((window, rows), jnp.bfloat16),
            pltpu.VMEM((window, 2 * KW), jnp.float32),
            pltpu.VMEM((HD, rows), jnp.float32),
        ],
        compiler_params=pltpu.CompilerParams(vmem_limit_bytes=48 * 1024 * 1024),
        cost_estimate=pl.CostEstimate(
            flops=3_000_000_000, bytes_accessed=10_000_000, transcendentals=2_000_000
        ),
        name="attention",
    )(me, lengths, q, ct, q_bias, kv)


def all_sum(x, axes):
    for axis in axes:
        size = lax.axis_size(axis)
        step = 1
        while step < size:
            x = x + lax.ppermute(x, axis, [(i, i ^ step) for i in range(size)])
            step *= 2
    return x


def on_device(q_proj, k_proj, v_proj, q_bias, v_bias, cotangent, lengths):
    group_size = lax.axis_size("ctx")
    me = lax.axis_index("ctx").astype(jnp.int32)
    value_rows = (v_proj[0].astype(jnp.float32) + v_bias).astype(jnp.bfloat16)
    key_value = jnp.concatenate([k_proj[0], value_rows], axis=-1)
    sent = jnp.broadcast_to(key_value[None], (group_size, *key_value.shape))
    gathered = lax.all_to_all(sent, "ctx", 0, 0)
    attended, q_grad, parts, sums = attention(
        group_size, me[None], lengths, q_proj[0], cotangent[0], q_bias[None], gathered
    )
    returned = lax.all_to_all(parts, "ctx", 0, 0)
    totals = jnp.sum(returned.astype(jnp.float32), axis=0)
    k_grad = totals[..., :KW].astype(jnp.bfloat16)
    v_grad = totals[..., KW:].astype(jnp.bfloat16)
    sums = all_sum(sums, ("ctx", "dp"))
    return (
        attended[None],
        q_grad[None],
        k_grad[None],
        v_grad[None],
        sums[: KVH * GROUP].reshape(HQ),
        sums[KVH * GROUP :].reshape(KW),
    )


def solution(mesh):
    placed = (
        P("dp", None, "ctx", None),
        P("dp", None, "ctx", None),
        P("dp", None, "ctx", None),
        P(),
        P(),
        P("dp", None, "ctx", None),
        P("dp", None),
    )
    return jax.shard_map(
        on_device,
        mesh=mesh,
        in_specs=placed,
        out_specs=(
            P("dp", None, "ctx", None),
            P("dp", None, "ctx", None),
            P("dp", None, "ctx", None),
            P("dp", None, "ctx", None),
            P(),
            P(),
        ),
        check_vma=False,
    )
```

time: 702 us -> 175 us (0.25)
  waiting for transfers between devices: 410 us -> 105 us
  local copies, waits for them, and re-layouts: 103 us -> 6.29 us
  matrix products: 68.5 us -> 0 us
  blocking collectives: 63.6 us -> 0 us
  starting transfers between devices: 0.12 us -> 50.6 us
  other arithmetic: 38.8 us -> 4.59 us
  between operations: 13.9 us -> 0.71 us
  Pallas kernels: 0 us -> 8.97 us
    reduce_scatter x2 -> x0, waiting for transfers between devices: 259 us -> none  [the longest x1 156 us: on_device(): lax.psum_scatter(value_parts.reshape(1, 2, half_len, KW), 'ctx', scatter_...]
    all_gather x1 -> x0, waiting for transfers between devices: 152 us -> none  [on_device(): lax.all_gather(key_value, 'ctx', axis=2, tiled=True)]
    dot_general x56 -> x0, matrix products: 68.5 us -> none  [the longest x8 29.8 us: output_step(): jnp.einsum('getj,jgd->tged', weights, value_tile, preferred_element_type=...]
    psum x1 -> x0, blocking collectives: 63.6 us -> none  [on_device(): lax.psum((jnp.sum(query_grad.reshape(tok_len, HQ), axis=0), jnp.sum(value...]
    ppermute x0 -> x7, waiting for transfers between devices: none -> 53.4 us  [all_sum(): x = x + lax.ppermute(x, axis, [(i, i ^ step) for i in range(size)])]
    all_to_all x0 -> x2, waiting for transfers between devices: none -> 51.7 us  [the longest x1 51.7 us: on_device(): gathered = lax.all_to_all(sent, 'ctx', 0, 0)]
    dynamic_slice x56 -> x0, local copies, waits for them, and re-layouts: 43.1 us -> none  [on_device(): lax.scan(stats_step, (start_top, jnp.zeros_like(start_top)), tiles)]
    all_to_all x0 -> x2, starting transfers between devices: none -> 28.4 us  [the longest x1 19.4 us: on_device(): returned = lax.all_to_all(parts, 'ctx', 0, 0)]
  transfers between devices with their start and end apart: 3 -> 9, of which waited for: 3 -> 8; matrix products, arithmetic and copies ran while one was open for 3% -> 1% of each run, Pallas kernels for 0% -> 0%
where the time goes in v1:
time: 175 us; the launch traced here: 176 us
  waiting for transfers between devices  105 us (60%)
  starting transfers between devices  50.6 us (29%)
  Pallas kernels  8.97 us (5%)
  local copies, waits for them, and re-layouts  6.29 us (4%)
  other arithmetic  4.59 us (3%)
    ppermute x7, waiting for transfers between devices, all_sum(): x = x + lax.ppermute(x, axis, [(i, i ^ step) for i in range(size)])  53.4 us
    all_to_all x1, waiting for transfers between devices, on_device(): gathered = lax.all_to_all(sent, 'ctx', 0, 0)  51.7 us
    ppermute x7, starting transfers between devices, all_sum(): x = x + lax.ppermute(x, axis, [(i, i ^ step) for i in range(size)])  22.2 us
    all_to_all x1, starting transfers between devices, on_device(): returned = lax.all_to_all(parts, 'ctx', 0, 0)  19.4 us
    all_to_all x1, starting transfers between devices, on_device(): gathered = lax.all_to_all(sent, 'ctx', 0, 0)  9.03 us
    pallas_call x1, Pallas kernels, attention(): pl.pallas_call(functools.partial(attention_kernel, group_size), out_shape...  8.97 us
  transfers between devices with their start and end apart: 9, of which 8 were waited for; matrix products, arithmetic and copies ran while one was open for 1% of the time, Pallas kernels for 0%

profile of v1, /device:TPU:0, one launch (start us, length us, event | category | flops | bytes accessed | tf_op | source)
XLA Modules:
  0.0 176.2 jit_solution(8622637508374467267)
XLA Ops:
  0.6 0.9 fusion
  1.5 0.9 pad_maximum_fusion
  2.3 2.5 %broadcast_in_dim.27 = bf16[32,2,64,512]{3,2,1,0:T(8,128)(2,1)} broadcast(bf16[2,64,512]{2,1,0:T(8,128)(2,1)S(1)} %pad_maximum_fusion), dimensions={1,2,3} | broadcast | bytes 4325376 | tf_op jit(solution)/shard_map/broadcast_in_dim | solution.py:230
  4.8 9.0 %all-to-all-start = ((bf16[32,2,64,512]{3,2,1,0:T(8,128)(2,1)}), bf16[32,2,64,512]{3,2,1,0:T(8,128)(2,1)}, u32[]{:S(2)}, u32[]{:S(2)}) async-start(bf16[32,2,64,512]{3,2,1,0:T(8,128)(2,1)} %broadcast_in_dim.27), calls=%async_computation | async-start | bytes 8388608 | tf_op jit(solution)/shard_map/all_to_all | solution.py:231
  13.9 51.7 %all-to-all-done.kv_ref = bf16[32,2,64,512]{3,2,1,0:T(8,128)(2,1)} async-done(((bf16[32,2,64,512]{3,2,1,0:T(8,128)(2,1)}), bf16[32,2,64,512]{3,2,1,0:T(8,128)(2,1)}, u32[]{:S(2)}, u32[]{:S(2)}) %all-to-all-start) | async-done | bytes 4194336 | tf_op jit(solution)/shard_map/all_to_all | solution.py:231
  65.6 9.0 %attention.1 = (bf16[2,64,1792]{2,1,0:T(8,128)(2,1)}, bf16[2,64,1792]{2,1,0:T(8,128)(2,1)}, bf16[32,2,64,512]{3,2,1,0:T(8,128)(2,1)S(1)}, f32[16,128]{1,0:T(8,128)S(1)}) custom-call(s32[1]{0:T(128)} %bitcast.where_ref, s32[1,16]{1,0:T(1,128)S(1)} %copy-done.3, bf16[2,64,1792]{2,1,0:T(8,128)(2,1)S(1)} %bitcast.17, bf16[2,64,1792]{2,1,0:T(8,128)(2,1)S(1)} %bitcast.18, ...), custom_call_target="tpu_custom_call" | custom-call | flops 3000000000 | bytes 10000000 | tf_op jit(solution)/shard_map/attention/pallas_call | solution.py:188
  74.6 2.0 %copy-done = bf16[32,2,64,512]{3,2,1,0:T(8,128)(2,1)} copy-done((bf16[32,2,64,512]{3,2,1,0:T(8,128)(2,1)}, bf16[32,2,64,512]{3,2,1,0:T(8,128)(2,1)S(1)}, u32[]{:S(2)}) %copy-start) | copy-done | bytes 4194328
  76.5 19.4 %all-to-all-start.1 = ((bf16[32,2,64,512]{3,2,1,0:T(8,128)(2,1)}), bf16[32,2,64,512]{3,2,1,0:T(8,128)(2,1)}, u32[]{:S(2)}, u32[]{:S(2)}) async-start(bf16[32,2,64,512]{3,2,1,0:T(8,128)(2,1)} %copy-done), calls=%async_computation.1 | async-start | bytes 8388608 | tf_op jit(solution)/shard_map/all_to_all | solution.py:235
  95.9 1.8 %collective-permute-start = (f32[16,128]{1,0:T(8,128)S(1)}, f32[16,128]{1,0:T(8,128)S(1)}, u32[]{:S(2)}, u32[]{:S(2)}) collective-permute-start(f32[16,128]{1,0:T(8,128)S(1)} %get-tuple-element.13), channel_id=1, source_target_pairs={{0,4},{4,0},{8,12},{12,8},{16,20},{20,16},{24,28},{28,24},{32,36},... | collective-permute-start | bytes 24584 | tf_op jit(solution)/shard_map/ppermute | solution.py:220
  97.7 42.3 %collective-permute-done = f32[16,128]{1,0:T(8,128)S(1)} collective-permute-done((f32[16,128]{1,0:T(8,128)S(1)}, f32[16,128]{1,0:T(8,128)S(1)}, u32[]{:S(2)}, u32[]{:S(2)}) %collective-permute-start) | collective-permute-done | bytes 8224 | tf_op jit(solution)/shard_map/ppermute | solution.py:220
  140.0 2.8 %collective-permute-start.1 = (f32[16,128]{1,0:T(8,128)S(1)}, f32[16,128]{1,0:T(8,128)S(1)}, u32[]{:S(2)}, u32[]{:S(2)}) collective-permute-start(f32[16,128]{1,0:T(8,128)S(1)} %add.31), channel_id=1, source_target_pairs={{0,8},{4,12},{8,0},{12,4},{16,24},{20,28},{24,16},{28,20},{32,40},... | collective-permute-start | bytes 24584 | tf_op jit(solution)/shard_map/ppermute | solution.py:220
  142.8 2.4 %collective-permute-done.1 = f32[16,128]{1,0:T(8,128)S(1)} collective-permute-done((f32[16,128]{1,0:T(8,128)S(1)}, f32[16,128]{1,0:T(8,128)S(1)}, u32[]{:S(2)}, u32[]{:S(2)}) %collective-permute-start.1) | collective-permute-done | bytes 8224 | tf_op jit(solution)/shard_map/ppermute | solution.py:220
  145.1 1.4 collective-permute-start.2
  146.6 2.2 %collective-permute-done.2 = f32[16,128]{1,0:T(8,128)S(1)} collective-permute-done((f32[16,128]{1,0:T(8,128)S(1)}, f32[16,128]{1,0:T(8,128)S(1)}, u32[]{:S(2)}, u32[]{:S(2)}) %collective-permute-start.2) | collective-permute-done | bytes 8224 | tf_op jit(solution)/shard_map/ppermute | solution.py:220
  148.8 1.8 %collective-permute-start.3 = (f32[16,128]{1,0:T(8,128)S(1)}, f32[16,128]{1,0:T(8,128)S(1)}, u32[]{:S(2)}, u32[]{:S(2)}) collective-permute-start(f32[16,128]{1,0:T(8,128)S(1)} %add.33), channel_id=1, source_target_pairs={{0,32},{4,36},{8,40},{12,44},{16,48},{20,52},{24,56},{28,60},{32,0... | collective-permute-start | bytes 24584 | tf_op jit(solution)/shard_map/ppermute | solution.py:220
  150.6 1.8 %collective-permute-done.3 = f32[16,128]{1,0:T(8,128)S(1)} collective-permute-done((f32[16,128]{1,0:T(8,128)S(1)}, f32[16,128]{1,0:T(8,128)S(1)}, u32[]{:S(2)}, u32[]{:S(2)}) %collective-permute-start.3) | collective-permute-done | bytes 8224 | tf_op jit(solution)/shard_map/ppermute | solution.py:220
  152.4 3.3 %collective-permute-start.4 = (f32[16,128]{1,0:T(8,128)S(1)}, f32[16,128]{1,0:T(8,128)S(1)}, u32[]{:S(2)}, u32[]{:S(2)}) collective-permute-start(f32[16,128]{1,0:T(8,128)S(1)} %add.34), channel_id=1, source_target_pairs={{0,64},{4,68},{8,72},{12,76},{16,80},{20,84},{24,88},{28,92},{32,9... | collective-permute-start | bytes 24584 | tf_op jit(solution)/shard_map/ppermute | solution.py:220
  155.7 1.9 %collective-permute-done.4 = f32[16,128]{1,0:T(8,128)S(1)} collective-permute-done((f32[16,128]{1,0:T(8,128)S(1)}, f32[16,128]{1,0:T(8,128)S(1)}, u32[]{:S(2)}, u32[]{:S(2)}) %collective-permute-start.4) | collective-permute-done | bytes 8224 | tf_op jit(solution)/shard_map/ppermute | solution.py:220
  157.6 1.2 collective-permute-done.5
  158.8 11.1 %collective-permute-start.6 = (f32[16,128]{1,0:T(8,128)S(1)}, f32[16,128]{1,0:T(8,128)S(1)}, u32[]{:S(2)}, u32[]{:S(2)}) collective-permute-start(f32[16,128]{1,0:T(8,128)S(1)} %add.36), channel_id=1, source_target_pairs={{0,2},{1,3},{2,0},{3,1},{4,6},{5,7},{6,4},{7,5},{8,10},{9,11},{10,... | collective-permute-start | bytes 24584 | tf_op jit(solution)/shard_map/ppermute | solution.py:220
  169.9 1.6 collective-permute-done.6
  172.1 0.6 slice_bitcast_fusion.2
  172.7 2.9 %reduce = bf16[2,64,512]{2,1,0:T(8,128)(2,1)S(1)} reduce(bf16[32,2,64,512]{3,2,1,0:T(8,128)(2,1)} %all-to-all-done.1, bf16[]{:T(256)} %constant.13), dimensions={0}, to_apply=%region_0.0.clone | reduce | flops 2031616 | bytes 4325378 | tf_op jit(solution)/shard_map/reduce_sum | solution.py:236
  175.6 0.7 slice_bitcast_fusion
  (20 shorter events, 0.6 us)
Async XLA Ops:
  4.8 9.1 %copy-start.4 = (f32[1792]{0:T(1024)S(1)}, f32[1792]{0:T(1024)}, u32[]{:S(2)}) copy-start(f32[1792]{0:T(1024)} %param.10) | copy-start | bytes 21508
  4.8 60.8 %copy-start.1 = (bf16[1,2,64,1792]{3,2,1,0:T(8,128)(2,1)S(1)}, bf16[1,2,64,1792]{3,2,1,0:T(8,128)(2,1)}, u32[]{:S(2)}) copy-start(bf16[1,2,64,1792]{3,2,1,0:T(8,128)(2,1)} %param.7) | copy-start | bytes 1376260
  4.8 60.8 %copy-start.2 = (bf16[1,2,64,1792]{3,2,1,0:T(8,128)(2,1)S(1)}, bf16[1,2,64,1792]{3,2,1,0:T(8,128)(2,1)}, u32[]{:S(2)}) copy-start(bf16[1,2,64,1792]{3,2,1,0:T(8,128)(2,1)} %param.12) | copy-start | bytes 1376260
  4.8 60.8 %copy-start.3 = (s32[1,16]{1,0:T(1,128)S(1)}, s32[1,16]{1,0:T(1,128)}, u32[]{:S(2)}) copy-start(s32[1,16]{1,0:T(1,128)} %len_ref.1) | copy-start | bytes 196
  4.8 60.7 %all-to-all-start = ((bf16[32,2,64,512]{3,2,1,0:T(8,128)(2,1)}), bf16[32,2,64,512]{3,2,1,0:T(8,128)(2,1)}, u32[]{:S(2)}, u32[]{:S(2)}) async-start(bf16[32,2,64,512]{3,2,1,0:T(8,128)(2,1)} %broadcast_in_dim.27), calls=%async_computation | async-start | bytes 8388608 | tf_op jit(solution)/shard_map/all_to_all | solution.py:231
  74.6 2.0 %copy-start = (bf16[32,2,64,512]{3,2,1,0:T(8,128)(2,1)}, bf16[32,2,64,512]{3,2,1,0:T(8,128)(2,1)S(1)}, u32[]{:S(2)}) copy-start(bf16[32,2,64,512]{3,2,1,0:T(8,128)(2,1)S(1)} %get-tuple-element.12) | copy-start | bytes 12582916
  76.5 96.2 %all-to-all-start.1 = ((bf16[32,2,64,512]{3,2,1,0:T(8,128)(2,1)}), bf16[32,2,64,512]{3,2,1,0:T(8,128)(2,1)}, u32[]{:S(2)}, u32[]{:S(2)}) async-start(bf16[32,2,64,512]{3,2,1,0:T(8,128)(2,1)} %copy-done), calls=%async_computation.1 | async-start | bytes 8388608 | tf_op jit(solution)/shard_map/all_to_all | solution.py:235
  95.9 44.1 %collective-permute-start = (f32[16,128]{1,0:T(8,128)S(1)}, f32[16,128]{1,0:T(8,128)S(1)}, u32[]{:S(2)}, u32[]{:S(2)}) collective-permute-start(f32[16,128]{1,0:T(8,128)S(1)} %get-tuple-element.13), channel_id=1, source_target_pairs={{0,4},{4,0},{8,12},{12,8},{16,20},{20,16},{24,28},{28,24},{32,36},... | collective-permute-start | bytes 24584 | tf_op jit(solution)/shard_map/ppermute | solution.py:220
  140.0 5.2 %collective-permute-start.1 = (f32[16,128]{1,0:T(8,128)S(1)}, f32[16,128]{1,0:T(8,128)S(1)}, u32[]{:S(2)}, u32[]{:S(2)}) collective-permute-start(f32[16,128]{1,0:T(8,128)S(1)} %add.31), channel_id=1, source_target_pairs={{0,8},{4,12},{8,0},{12,4},{16,24},{20,28},{24,16},{28,20},{32,40},... | collective-permute-start | bytes 24584 | tf_op jit(solution)/shard_map/ppermute | solution.py:220
  145.1 3.7 %collective-permute-start.2 = (f32[16,128]{1,0:T(8,128)S(1)}, f32[16,128]{1,0:T(8,128)S(1)}, u32[]{:S(2)}, u32[]{:S(2)}) collective-permute-start(f32[16,128]{1,0:T(8,128)S(1)} %add.32), channel_id=1, source_target_pairs={{0,16},{4,20},{8,24},{12,28},{16,0},{20,4},{24,8},{28,12},{32,48},... | collective-permute-start | bytes 24584 | tf_op jit(solution)/shard_map/ppermute | solution.py:220
  148.8 3.7 %collective-permute-start.3 = (f32[16,128]{1,0:T(8,128)S(1)}, f32[16,128]{1,0:T(8,128)S(1)}, u32[]{:S(2)}, u32[]{:S(2)}) collective-permute-start(f32[16,128]{1,0:T(8,128)S(1)} %add.33), channel_id=1, source_target_pairs={{0,32},{4,36},{8,40},{12,44},{16,48},{20,52},{24,56},{28,60},{32,0... | collective-permute-start | bytes 24584 | tf_op jit(solution)/shard_map/ppermute | solution.py:220
  152.4 5.2 %collective-permute-start.4 = (f32[16,128]{1,0:T(8,128)S(1)}, f32[16,128]{1,0:T(8,128)S(1)}, u32[]{:S(2)}, u32[]{:S(2)}) collective-permute-start(f32[16,128]{1,0:T(8,128)S(1)} %add.34), channel_id=1, source_target_pairs={{0,64},{4,68},{8,72},{12,76},{16,80},{20,84},{24,88},{28,92},{32,9... | collective-permute-start | bytes 24584 | tf_op jit(solution)/shard_map/ppermute | solution.py:220
  157.6 1.2 collective-permute-start.5
  158.8 12.7 %collective-permute-start.6 = (f32[16,128]{1,0:T(8,128)S(1)}, f32[16,128]{1,0:T(8,128)S(1)}, u32[]{:S(2)}, u32[]{:S(2)}) collective-permute-start(f32[16,128]{1,0:T(8,128)S(1)} %add.36), channel_id=1, source_target_pairs={{0,2},{1,3},{2,0},{3,1},{4,6},{5,7},{6,4},{7,5},{8,10},{9,11},{10,... | collective-permute-start | bytes 24584 | tf_op jit(solution)/shard_map/ppermute | solution.py:220

commit v2 on v1

v2 whole, which is shorter than its diff:
```python
import functools
import math

import jax
import jax.numpy as jnp
from jax import lax
from jax.experimental import pallas as pl
from jax.experimental.pallas import tpu as pltpu
from jax.sharding import PartitionSpec as P

HD = 128
KVH = 2
GROUP = 7
HQ = 1792
KW = 256
MOST = 1024

HALF_Q = GROUP * HD
SLOT_W = 2 * HD
SUM_ROWS = 16
MASKED = -1e30
VMEM_BYTES = 60 * 1024 * 1024
GOT_PARTS = 4
BLOCKS_PER_CHUNK = 4

NT = (((1,), (1,)), ((), ()))
NN = (((1,), (0,)), ((), ()))
TN = (((0,), (0,)), ((), ()))

SMEM = pl.BlockSpec(memory_space=pltpu.SMEM)
VMEM = pl.BlockSpec(memory_space=pltpu.VMEM)
HBM = pl.BlockSpec(memory_space=pltpu.HBM)


def dot(a, b, dims):
    return lax.dot_general(a, b, dims, preferred_element_type=jnp.float32)


def lanes(start, size):
    return pl.ds(pl.multiple_of(start, HD), size)


def send_kernel(group_size, me_ref, k_ref, v_ref, vb_ref, q_ref, ct_ref, send_ref, swap_ref, kv_ref, sem, swap_sem):
    block_len = k_ref.shape[1]
    other = 1 - me_ref[0] % 2
    copies = []
    for i, ref in enumerate((q_ref, ct_ref)):
        copies.append(
            pltpu.make_async_copy(
                ref.at[:, :, lanes(other * HALF_Q, HALF_Q)], swap_ref.at[i], swap_sem.at[i]
            )
        )
    for copy in copies:
        copy.start()
    for g in range(KVH):
        cols = slice(g * HD, (g + 1) * HD)
        for h in range(2):
            here = slice(h * block_len, (h + 1) * block_len)
            kv_ref[g, here, :HD] = k_ref[h, :, cols]
            kv_ref[g, here, HD:] = (
                v_ref[h, :, cols].astype(jnp.float32) + vb_ref[:, cols]
            ).astype(jnp.bfloat16)
    for d in range(group_size):
        copy = pltpu.make_async_copy(kv_ref.at[d % 2], send_ref.at[d], sem.at[d])
        copy.start()
        copies.append(copy)
    for copy in copies:
        copy.wait()


def attention_kernel(
    group_size,
    me_ref,
    len_ref,
    q_ref,
    ct_ref,
    other_hbm,
    qb_ref,
    kv_ref,
    mine_hbm,
    back_hbm,
    gr_ref,
    other_ref,
    mine_ref,
    back_ref,
    stage_ref,
    windows_ref,
    q_rows,
    d_rows,
    p_ref,
    grad_ref,
    acc_ref,
    row_ref,
    sum_ref,
    sems,
    load_sems,
):
    block_len = q_ref.shape[1]
    pair_len = 2 * block_len
    rows = GROUP * pair_len
    chunk = BLOCKS_PER_CHUNK * block_len
    scale = 1.0 / math.sqrt(HD)
    log2e = 1.0 / math.log(2.0)
    last_block = 2 * group_size - 1
    me = me_ref[0]
    head = me % 2
    pair = me - head
    n_docs = len_ref.shape[1]

    other_copy = pltpu.make_async_copy(other_hbm, other_ref, sems.at[0])
    other_copy.start()

    def place(block):
        early = block < group_size
        slot = jnp.where(early, block, last_block - block)
        return slot, pl.multiple_of(jnp.where(early, 0, block_len), block_len)

    def reach(h):
        first_block = jnp.where(h == 0, pair, last_block - 1 - pair)
        first_pos = first_block * block_len
        end = jnp.int32(0)
        first_start = jnp.int32(0)
        for k in range(n_docs):
            end = end + len_ref[0, k]
            first_start = jnp.where(first_pos >= end, end, first_start)
        low = first_start // block_len
        n_blocks = first_block + 2 - low
        n_chunks = (n_blocks + BLOCKS_PER_CHUNK - 1) // BLOCKS_PER_CHUNK
        return first_block, low, n_blocks, n_chunks

    def load_copy(h, i, first_block, low):
        slot, at = place(jnp.minimum(low + i, first_block + 1))
        into = pl.ds(pl.multiple_of(i * block_len, block_len), block_len)
        return pltpu.make_async_copy(
            kv_ref.at[slot, pl.ds(at, block_len), :],
            windows_ref.at[h, into, :],
            load_sems.at[h, i],
        )

    for h in range(2):
        first_block, low, n_blocks, n_chunks = reach(h)

        def start_load(i, carry, h=h, first_block=first_block, low=low):
            load_copy(h, i, first_block, low).start()
            return carry

        lax.fori_loop(0, n_chunks * BLOCKS_PER_CHUNK, start_load, 0)

    stage_ref[...] = jnp.zeros_like(stage_ref)
    sum_ref[...] = jnp.zeros_like(sum_ref)
    other_copy.wait()

    def query_unit(h, carry):
        first_block, low, n_blocks, n_chunks = reach(h)
        first_pos = first_block * block_len
        win_ref = windows_ref.at[h]
        own_at = pl.multiple_of(jnp.where(h == 0, head, 1 - head) * block_len, block_len)
        partner_at = pl.multiple_of(block_len - own_at, block_len)
        lane = lax.broadcasted_iota(jnp.int32, (1, rows), 1)
        query_pos = first_pos + lane % pair_len
        query_start = jnp.zeros_like(query_pos)
        end = jnp.int32(0)
        for k in range(n_docs):
            end = end + len_ref[0, k]
            query_start = jnp.where(query_pos >= end, end, query_start)

        def wait_load(i, carry):
            load_copy(h, i, first_block, low).wait()
            return carry

        lax.fori_loop(0, n_chunks * BLOCKS_PER_CHUNK, wait_load, 0)

        for t in range(GROUP):
            f = t * HD
            bias = qb_ref[:, lanes(head * HALF_Q + f, HD)]
            own_rows = pl.ds(t * pair_len + own_at, block_len)
            partner_rows = pl.ds(t * pair_len + partner_at, block_len)
            own_lanes = lanes(head * HALF_Q + f, HD)
            q_rows[own_rows, :] = (q_ref[h, :, own_lanes].astype(jnp.float32) + bias).astype(
                jnp.bfloat16
            )
            q_rows[partner_rows, :] = (
                other_ref[0, h, :, f : f + HD].astype(jnp.float32) + bias
            ).astype(jnp.bfloat16)
            d_rows[own_rows, :] = ct_ref[h, :, own_lanes]
            d_rows[partner_rows, :] = other_ref[1, h, :, f : f + HD]

        def window(i):
            return pl.ds(pl.multiple_of(i * chunk, chunk), chunk)

        def score_step(i, top):
            at = window(i)
            s = dot(win_ref[at, :HD], q_rows[...], NT) * (scale * log2e)
            key_pos = (low * block_len + i * chunk) + lax.broadcasted_iota(
                jnp.int32, (chunk, 1), 0
            )
            visible = (key_pos >= query_start) & (key_pos <= query_pos)
            s = jnp.where(visible, s, MASKED)
            p_ref[at, :] = s
            return jnp.maximum(top, jnp.max(s, axis=0, keepdims=True))

        top = lax.fori_loop(0, n_chunks, score_step, jnp.full((1, rows), MASKED, jnp.float32))

        acc_ref[...] = jnp.zeros_like(acc_ref)

        def out_step(i, total):
            at = window(i)
            e = jnp.exp2(p_ref[at, :] - top)
            p_ref[at, :] = e
            acc_ref[...] += dot(win_ref[at, HD:], e.astype(jnp.bfloat16), TN)
            return total + jnp.sum(e, axis=0, keepdims=True)

        total = lax.fori_loop(0, n_chunks, out_step, jnp.zeros((1, rows), jnp.float32))
        inverse = 1.0 / total
        summed = acc_ref[...] * inverse
        delta = jnp.sum(
            summed * jnp.transpose(d_rows[...].astype(jnp.float32)), axis=0, keepdims=True
        )
        row_ref[...] = jnp.transpose(summed)
        for t in range(GROUP):
            f = t * HD
            mine_ref[0, h, :, f : f + HD] = row_ref[
                pl.ds(t * pair_len + own_at, block_len), :
            ].astype(jnp.bfloat16)
            back_ref[0, h, :, f : f + HD] = row_ref[
                pl.ds(t * pair_len + partner_at, block_len), :
            ].astype(jnp.bfloat16)

        acc_ref[...] = jnp.zeros_like(acc_ref)

        def grad_step(i, value_total):
            at = window(i)
            p = p_ref[at, :] * inverse
            dp = dot(win_ref[at, HD:], d_rows[...], NT)
            ds = (p * (dp - delta)).astype(jnp.bfloat16)
            value_part = dot(p.astype(jnp.bfloat16), d_rows[...], NN)
            grad_ref[at, HD:] = value_part
            grad_ref[at, :HD] = dot(ds, q_rows[...], NN) * scale
            acc_ref[...] += dot(win_ref[at, :HD], ds, TN)
            return value_total + jnp.sum(value_part, axis=0, keepdims=True)

        value_total = lax.fori_loop(0, n_chunks, grad_step, jnp.zeros((1, HD), jnp.float32))
        sum_ref[GROUP : GROUP + 1, :] += value_total
        row_ref[...] = jnp.transpose(acc_ref[...] * scale)
        for t in range(GROUP):
            f = t * HD
            mine_ref[1, h, :, f : f + HD] = row_ref[
                pl.ds(t * pair_len + own_at, block_len), :
            ].astype(jnp.bfloat16)
            back_ref[1, h, :, f : f + HD] = row_ref[
                pl.ds(t * pair_len + partner_at, block_len), :
            ].astype(jnp.bfloat16)
            sum_ref[t : t + 1, :] += jnp.sum(
                row_ref[t * pair_len : (t + 1) * pair_len, :], axis=0, keepdims=True
            )

        def store(i, carry):
            slot, at = place(low + i)
            part = grad_ref[pl.ds(pl.multiple_of(i * block_len, block_len), block_len), :]
            into = pl.ds(at, block_len)
            stage_ref[slot, into, :] = (
                stage_ref[slot, into, :].astype(jnp.float32) + part
            ).astype(jnp.bfloat16)
            return carry

        lax.fori_loop(0, n_blocks, store, 0)
        return carry

    lax.fori_loop(0, 2, query_unit, 0)

    sums = sum_ref[...]
    high = sums.astype(jnp.bfloat16).astype(jnp.float32)
    middle = (sums - high).astype(jnp.bfloat16).astype(jnp.float32)
    lowest = sums - high - middle
    pieces = jnp.concatenate(
        [
            jnp.concatenate([high, middle], axis=1),
            jnp.concatenate([lowest, jnp.zeros_like(lowest)], axis=1),
        ],
        axis=0,
    ).astype(jnp.bfloat16)
    for d in range(group_size):
        stage_ref[d, pair_len:, :] = pieces
    copies = [
        pltpu.make_async_copy(back_ref, back_hbm, sems.at[1]),
        pltpu.make_async_copy(stage_ref, gr_ref, sems.at[2]),
        pltpu.make_async_copy(mine_ref, mine_hbm, sems.at[3]),
    ]
    for copy in copies:
        copy.start()
    for copy in copies:
        copy.wait()


def sums_kernel(got_ref, out_ref):
    for g in range(KVH):
        total = got_ref[g].astype(jnp.float32)
        for d in range(g + 2, got_ref.shape[0], 2):
            total += got_ref[d].astype(jnp.float32)
        half = SUM_ROWS // 2
        out_ref[g * half : (g + 1) * half, :] = (
            total[:half, :HD] + total[:half, HD:] + total[half:, :HD]
        )


def finish_kernel(
    group_size, me_ref, got_hbm, mine_ref, theirs_ref, att_ref, qg_ref, kg_ref, vg_ref, got_ref, sems, out_sems
):
    block_len = att_ref.shape[1]
    pair_len = 2 * block_len
    head = me_ref[0] % 2
    part = group_size // GOT_PARTS
    loads = []
    for i in range(GOT_PARTS):
        some = slice(i * part, (i + 1) * part)
        loads.append(
            pltpu.make_async_copy(got_hbm.at[some, :pair_len], got_ref.at[some], sems.at[i])
        )
        loads[i].start()
    copies = []
    for i, ref in enumerate((att_ref, qg_ref)):
        for j, (source, at) in enumerate(((mine_ref, head), (theirs_ref, 1 - head))):
            copies.append(
                pltpu.make_async_copy(
                    source.at[i], ref.at[:, :, lanes(at * HALF_Q, HALF_Q)], out_sems.at[2 * i + j]
                )
            )
            copies[-1].start()
    for load in loads:
        load.wait()
    for h in range(2):
        here = slice(h * block_len, (h + 1) * block_len)
        for g in range(KVH):
            total = got_ref[g, here, :].astype(jnp.float32)
            for d in range(g + 2, group_size, 2):
                total += got_ref[d, here, :].astype(jnp.float32)
            total = total.astype(jnp.bfloat16)
            kg_ref[h, :, g * HD : (g + 1) * HD] = total[:, :HD]
            vg_ref[h, :, g * HD : (g + 1) * HD] = total[:, HD:]
    for copy in copies:
        copy.wait()


def on_device(q_proj, k_proj, v_proj, q_bias, v_bias, cotangent, lengths):
    group_size = lax.axis_size("ctx")
    me = lax.axis_index("ctx").astype(jnp.int32)[None]
    q, ct, k, v = q_proj[0], cotangent[0], k_proj[0], v_proj[0]
    block_len = q.shape[1]
    pair_len = 2 * block_len
    rows = GROUP * pair_len
    most_blocks = MOST // block_len + 2
    window = -(-most_blocks // BLOCKS_PER_CHUNK) * BLOCKS_PER_CHUNK * block_len
    bf16, f32 = jnp.bfloat16, jnp.float32
    halves = jax.ShapeDtypeStruct((2, 2, block_len, HALF_Q), bf16)

    sent, swap = pl.pallas_call(
        functools.partial(send_kernel, group_size),
        out_shape=(jax.ShapeDtypeStruct((group_size, pair_len, SLOT_W), bf16), halves),
        in_specs=[SMEM, VMEM, VMEM, VMEM, HBM, HBM],
        out_specs=(HBM, HBM),
        scratch_shapes=[
            pltpu.VMEM((KVH, pair_len, SLOT_W), bf16),
            pltpu.SemaphoreType.DMA((group_size,)),
            pltpu.SemaphoreType.DMA((2,)),
        ],
        compiler_params=pltpu.CompilerParams(vmem_limit_bytes=VMEM_BYTES),
        name="send",
    )(me, k, v, v_bias[None], q, ct)
    partners = [(i, i ^ 1) for i in range(group_size)]
    other = lax.ppermute(swap, "ctx", partners)
    gathered = lax.all_to_all(sent, "ctx", 0, 0)

    slot_len = pair_len + SUM_ROWS
    slots = (group_size, slot_len, SLOT_W)
    mine, back, parts = pl.pallas_call(
        functools.partial(attention_kernel, group_size),
        out_shape=(halves, halves, jax.ShapeDtypeStruct(slots, bf16)),
        in_specs=[SMEM, SMEM, VMEM, VMEM, HBM, VMEM, HBM],
        out_specs=(HBM, HBM, HBM),
        scratch_shapes=[
            pltpu.VMEM(halves.shape, bf16),
            pltpu.VMEM(halves.shape, bf16),
            pltpu.VMEM(halves.shape, bf16),
            pltpu.VMEM(slots, bf16),
            pltpu.VMEM((2, window, SLOT_W), bf16),
            pltpu.VMEM((rows, HD), bf16),
            pltpu.VMEM((rows, HD), bf16),
            pltpu.VMEM((window, rows), f32),
            pltpu.VMEM((window, SLOT_W), f32),
            pltpu.VMEM((HD, rows), f32),
            pltpu.VMEM((rows, HD), f32),
            pltpu.VMEM((SUM_ROWS // 2, HD), f32),
            pltpu.SemaphoreType.DMA((4,)),
            pltpu.SemaphoreType.DMA((2, window // block_len)),
        ],
        compiler_params=pltpu.CompilerParams(vmem_limit_bytes=VMEM_BYTES),
        cost_estimate=pl.CostEstimate(
            flops=3_000_000_000, bytes_accessed=10_000_000, transcendentals=2_000_000
        ),
        name="attention",
    )(me, lengths, q, ct, other, q_bias[None], gathered)

    theirs = lax.ppermute(back, "ctx", partners)
    got = lax.all_to_all(parts, "ctx", 0, 0)
    sums = pl.pallas_call(
        sums_kernel,
        out_shape=jax.ShapeDtypeStruct((SUM_ROWS, HD), f32),
        grid=(1,),
        in_specs=[
            pl.BlockSpec((group_size, SUM_ROWS, SLOT_W), lambda i: (0, pair_len // SUM_ROWS, 0))
        ],
        out_specs=pl.BlockSpec((SUM_ROWS, HD), lambda i: (0, 0)),
        compiler_params=pltpu.CompilerParams(vmem_limit_bytes=VMEM_BYTES),
        name="sums",
    )(got)
    for axis_step in (1, 2):
        size = lax.axis_size("dp")
        sums = sums + lax.ppermute(sums, "dp", [(i, i ^ axis_step) for i in range(size)])
    wide = jax.ShapeDtypeStruct(q.shape, bf16)
    narrow = jax.ShapeDtypeStruct(k.shape, bf16)
    attended, q_grad, k_grad, v_grad = pl.pallas_call(
        functools.partial(finish_kernel, group_size),
        out_shape=(wide, wide, narrow, narrow),
        in_specs=[SMEM, HBM, HBM, HBM],
        out_specs=(HBM, HBM, VMEM, VMEM),
        scratch_shapes=[
            pltpu.VMEM((group_size, pair_len, SLOT_W), bf16),
            pltpu.SemaphoreType.DMA((GOT_PARTS,)),
            pltpu.SemaphoreType.DMA((4,)),
        ],
        cost_estimate=pl.CostEstimate(flops=1_000_000, bytes_accessed=6_000_000, transcendentals=0),
        compiler_params=pltpu.CompilerParams(vmem_limit_bytes=VMEM_BYTES),
        name="finish",
    )(me, got, mine, theirs)
    by_head = sums.reshape(KVH, SUM_ROWS // 2, HD)
    return (
        attended[None],
        q_grad[None],
        k_grad[None],
        v_grad[None],
        by_head[:, :GROUP].reshape(HQ),
        by_head[:, GROUP].reshape(KW),
    )


def solution(mesh):
    placed = (
        P("dp", None, "ctx", None),
        P("dp", None, "ctx", None),
        P("dp", None, "ctx", None),
        P(),
        P(),
        P("dp", None, "ctx", None),
        P("dp", None),
    )
    return jax.shard_map(
        on_device,
        mesh=mesh,
        in_specs=placed,
        out_specs=(
            P("dp", None, "ctx", None),
            P("dp", None, "ctx", None),
            P("dp", None, "ctx", None),
            P("dp", None, "ctx", None),
            P(),
            P(),
        ),
        check_vma=False,
    )
```

time: 175 us -> 158 us (0.903); the launches traced: 176 us -> 156 us
  Pallas kernels: 8.97 us -> 57.2 us
  waiting for transfers between devices: 105 us -> 63.8 us
  starting transfers between devices: 50.6 us -> 27.3 us
  other arithmetic: 4.59 us -> 0.7 us
    all_to_all x1, waiting for transfers between devices: 51.7 us -> 0.01 us  [on_device(): gathered = lax.all_to_all(sent, 'ctx', 0, 0)]
    pallas_call x1 -> x4, Pallas kernels: 8.97 us -> 57.2 us  [the longest x1 29.6 us: on_device(): pl.pallas_call(functools.partial(finish_kernel, group_size), out_shape=(w...]
    all_to_all x1, waiting for transfers between devices: 0.01 us -> 30.3 us  [on_device(): got = lax.all_to_all(parts, 'ctx', 0, 0)]
    ppermute x7 -> x4, waiting for transfers between devices: 53.4 us -> 33.5 us  [the longest x1 32.1 us: on_device(): other = lax.ppermute(swap, 'ctx', partners)]
    ppermute x7 -> x4, starting transfers between devices: 22.2 us -> 7.63 us  [the longest x2 3.89 us: on_device(): lax.ppermute(sums, 'dp', [(i, i ^ axis_step) for i in range(size)])]
    all_to_all x1, starting transfers between devices: 19.4 us -> 10.8 us  [on_device(): got = lax.all_to_all(parts, 'ctx', 0, 0)]
    broadcast_in_dim x2 -> x0, local copies, waits for them, and re-layouts: 3.13 us -> none  [the longest x1 2.47 us: on_device(): sent = jnp.broadcast_to(key_value[None], (group_size, *key_value.shape))]
    reduce_sum x1 -> x0, other arithmetic: 2.86 us -> none  [on_device(): totals = jnp.sum(returned.astype(jnp.float32), axis=0)]
  transfers between devices with their start and end apart: 9 -> 6, of which waited for: 8 -> 3; matrix products, arithmetic and copies ran while one was open for 1% -> 1% of each run, Pallas kernels for 0% -> 20%
where the time goes in v2:
time: 158 us; the launch traced here: 156 us
  waiting for transfers between devices  63.8 us (40%)
  Pallas kernels  57.2 us (36%)
  starting transfers between devices  27.3 us (17%)
  local copies, waits for them, and re-layouts  6.08 us (4%)
    ppermute x1, waiting for transfers between devices, on_device(): other = lax.ppermute(swap, 'ctx', partners)  32.1 us
    all_to_all x1, waiting for transfers between devices, on_device(): got = lax.all_to_all(parts, 'ctx', 0, 0)  30.3 us
    pallas_call x1, Pallas kernels, on_device(): pl.pallas_call(functools.partial(finish_kernel, group_size), out_shape=(w...  29.6 us
    pallas_call x1, Pallas kernels, on_device(): pl.pallas_call(functools.partial(send_kernel, group_size), out_shape=(jax...  16.2 us
    all_to_all x1, starting transfers between devices, on_device(): got = lax.all_to_all(parts, 'ctx', 0, 0)  10.8 us
    pallas_call x1, Pallas kernels, on_device(): pl.pallas_call(functools.partial(attention_kernel, group_size), out_shape...  9.78 us
    all_to_all x1, starting transfers between devices, on_device(): gathered = lax.all_to_all(sent, 'ctx', 0, 0)  8.9 us
    unnamed x14, local copies, waits for them, and re-layouts  4.32 us
  transfers between devices with their start and end apart: 6, of which 3 were waited for; matrix products, arithmetic and copies ran while one was open for 1% of the time, Pallas kernels for 20%

profile of v2, /device:TPU:0, one launch (start us, length us, event | category | flops | bytes accessed | tf_op | source)
XLA Modules:
  0.0 155.9 jit_solution(12280891104223434701)
XLA Ops:
  0.6 16.2 %send.1 = (bf16[32,128,256]{2,1,0:T(8,128)(2,1)}, bf16[2,2,64,896]{3,2,1,0:T(8,128)(2,1)}) custom-call(s32[1]{0:T(128)} %bitcast.me_ref, bf16[2,64,256]{2,1,0:T(8,128)(2,1)} %bitcast.18, bf16[2,64,256]{2,1,0:T(8,128)(2,1)} %bitcast.19, f32[1,256]{1,0:T(1,128)} %bitcast.21, bf16[2,64,1792]{2,1,0:T(8,128)(2,1)} %bitcast.14, bf16[2,64,1792]{2,1,0:T(8,128)(2,1)} %bitcast.16), custom_call_target="tpu_custom_call" | custom-call | tf_op jit(solution)/shard_map/send/pallas_call | solution.py:356
  16.9 0.0 copy-start.6
  16.9 0.0 copy-start.3
  16.9 8.9 %all-to-all-start = ((bf16[32,128,256]{2,1,0:T(8,128)(2,1)}), bf16[32,128,256]{2,1,0:T(8,128)(2,1)S(1)}, u32[]{:S(2)}, u32[]{:S(2)}) async-start(bf16[32,128,256]{2,1,0:T(8,128)(2,1)} %get-tuple-element.16), calls=%async_computation | async-start | bytes 4194304 | tf_op jit(solution)/shard_map/all_to_all | solution.py:371
  25.8 1.9 %collective-permute-start = (bf16[2,2,64,896]{3,2,1,0:T(8,128)(2,1)S(1)}, bf16[2,2,64,896]{3,2,1,0:T(8,128)(2,1)S(1)}, u32[]{:S(2)}, u32[]{:S(2)}) collective-permute-start(bf16[2,2,64,896]{3,2,1,0:T(8,128)(2,1)S(1)} %copy-done.6), channel_id=1, source_target_pairs={{0,4},{4,0},{8,12},{12,8},{16,20},{20,16},{24,28},{28,24},{32,36},... | collective-permute-start | bytes 1376264 | tf_op jit(solution)/shard_map/ppermute | solution.py:370
  27.7 0.6 broadcast_in_dim.23.qb_ref
  28.3 32.1 %collective-permute-done.other_hbm = bf16[2,2,64,896]{3,2,1,0:T(8,128)(2,1)S(1)} collective-permute-done((bf16[2,2,64,896]{3,2,1,0:T(8,128)(2,1)S(1)}, bf16[2,2,64,896]{3,2,1,0:T(8,128)(2,1)S(1)}, u32[]{:S(2)}, u32[]{:S(2)}) %collective-permute-start) | collective-permute-done | bytes 458784 | tf_op jit(solution)/shard_map/ppermute | solution.py:370
  60.4 0.8 copy-done.5
  61.2 1.3 copy-done.1
  62.5 9.8 %attention.1 = (bf16[2,2,64,896]{3,2,1,0:T(8,128)(2,1)}, bf16[2,2,64,896]{3,2,1,0:T(8,128)(2,1)}, bf16[32,144,256]{2,1,0:T(8,128)(2,1)}) custom-call(s32[1]{0:T(128)} %bitcast.me_ref, s32[1,16]{1,0:T(1,128)} %len_ref.1, bf16[2,64,1792]{2,1,0:T(8,128)(2,1)} %bitcast.15, bf16[2,64,1792]{2,1,0:T(8,128)(2,1)} %bitcast.17, bf16[2,2,64,896]{3,2,1,0:T(8,128)(2,1)} %copy-done.5, ...), custom_call_target="tpu_custom_call" | custom-call | flops 3000000000 | bytes 10000000 | tf_op jit(solution)/shard_map/attention/pallas_call | solution.py:375
  72.3 0.0 copy-start.4
  72.3 10.8 %all-to-all-start.1 = ((bf16[32,144,256]{2,1,0:T(8,128)(2,1)}), bf16[32,144,256]{2,1,0:T(8,128)(2,1)S(1)}, u32[]{:S(2)}, u32[]{:S(2)}) async-start(bf16[32,144,256]{2,1,0:T(8,128)(2,1)} %get-tuple-element.17), calls=%async_computation.1 | async-start | bytes 4718592 | tf_op jit(solution)/shard_map/all_to_all | solution.py:404
  83.1 1.9 %collective-permute-start.1 = (bf16[2,2,64,896]{3,2,1,0:T(8,128)(2,1)S(1)}, bf16[2,2,64,896]{3,2,1,0:T(8,128)(2,1)S(1)}, u32[]{:S(2)}, u32[]{:S(2)}) collective-permute-start(bf16[2,2,64,896]{3,2,1,0:T(8,128)(2,1)S(1)} %copy-done.4), channel_id=1, source_target_pairs={{0,4},{4,0},{8,12},{12,8},{16,20},{20,16},{24,28},{28,24},{32,36},... | collective-permute-start | bytes 1376264 | tf_op jit(solution)/shard_map/ppermute | solution.py:403
  85.0 30.3 %all-to-all-done.1.got_hbm.got_ref = bf16[32,144,256]{2,1,0:T(8,128)(2,1)S(1)} async-done(((bf16[32,144,256]{2,1,0:T(8,128)(2,1)}), bf16[32,144,256]{2,1,0:T(8,128)(2,1)S(1)}, u32[]{:S(2)}, u32[]{:S(2)}) %all-to-all-start.1) | async-done | bytes 2359328 | tf_op jit(solution)/shard_map/all_to_all | solution.py:404
  115.3 1.4 copy-done
  116.7 1.6 %sums.1 = f32[16,128]{1,0:T(8,128)} custom-call(bf16[32,144,256]{2,1,0:T(8,128)(2,1)} %copy-done), custom_call_target="tpu_custom_call" | custom-call | tf_op jit(solution)/shard_map/sums/pallas_call | solution.py:405
  118.3 1.4 collective-permute-done.2
  119.7 0.7 add.6
  120.4 3.9 %collective-permute-start.3 = (f32[16,128]{1,0:T(8,128)S(1)}, f32[16,128]{1,0:T(8,128)S(1)}, u32[]{:S(2)}, u32[]{:S(2)}) collective-permute-start(f32[16,128]{1,0:T(8,128)S(1)} %add.6), channel_id=1, source_target_pairs={{0,2},{1,3},{2,0},{3,1},{4,6},{5,7},{6,4},{7,5},{8,10},{9,11},{10,... | collective-permute-start | bytes 24584 | tf_op jit(solution)/shard_map/ppermute | solution.py:418
  124.3 0.0 collective-permute-done.1.theirs_ref
  124.3 0.8 copy-done.2
  125.1 29.6 %finish.1 = (bf16[2,64,1792]{2,1,0:T(8,128)(2,1)}, bf16[2,64,1792]{2,1,0:T(8,128)(2,1)}, bf16[2,64,256]{2,1,0:T(8,128)(2,1)}, bf16[2,64,256]{2,1,0:T(8,128)(2,1)}) custom-call(s32[1]{0:T(128)} %bitcast.me_ref, bf16[32,144,256]{2,1,0:T(8,128)(2,1)} %copy-done, bf16[2,2,64,896]{3,2,1,0:T(8,128)(2,1)} %get-tuple-element.18.mine_ref, ...), custom_call_target="tpu_custom_call" | custom-call | flops 1000000 | bytes 6000000 | tf_op jit(solution)/shard_map/finish/pallas_call | solution.py:421
  154.7 0.6 slice.9
  155.3 0.6 reshape.19
  (11 shorter events, 0.0 us)
Async XLA Ops:
  16.9 8.9 %copy-start.6 = (bf16[2,2,64,896]{3,2,1,0:T(8,128)(2,1)S(1)}, bf16[2,2,64,896]{3,2,1,0:T(8,128)(2,1)}, u32[]{:S(2)}) copy-start(bf16[2,2,64,896]{3,2,1,0:T(8,128)(2,1)} %get-tuple-element.15) | copy-start | bytes 1376260
  16.9 10.8 %copy-start.3 = (f32[1792]{0:T(1024)S(1)}, f32[1792]{0:T(1024)}, u32[]{:S(2)}) copy-start(f32[1792]{0:T(1024)} %param.10) | copy-start | bytes 21508
  16.9 43.5 %all-to-all-start = ((bf16[32,128,256]{2,1,0:T(8,128)(2,1)}), bf16[32,128,256]{2,1,0:T(8,128)(2,1)S(1)}, u32[]{:S(2)}, u32[]{:S(2)}) async-start(bf16[32,128,256]{2,1,0:T(8,128)(2,1)} %get-tuple-element.16), calls=%async_computation | async-start | bytes 4194304 | tf_op jit(solution)/shard_map/all_to_all | solution.py:371
  25.8 34.6 %collective-permute-start = (bf16[2,2,64,896]{3,2,1,0:T(8,128)(2,1)S(1)}, bf16[2,2,64,896]{3,2,1,0:T(8,128)(2,1)S(1)}, u32[]{:S(2)}, u32[]{:S(2)}) collective-permute-start(bf16[2,2,64,896]{3,2,1,0:T(8,128)(2,1)S(1)} %copy-done.6), channel_id=1, source_target_pairs={{0,4},{4,0},{8,12},{12,8},{16,20},{20,16},{24,28},{28,24},{32,36},... | collective-permute-start | bytes 1376264 | tf_op jit(solution)/shard_map/ppermute | solution.py:370
  60.4 0.8 copy-start.5
  61.2 1.3 copy-start.1
  72.3 10.8 %copy-start.4 = (bf16[2,2,64,896]{3,2,1,0:T(8,128)(2,1)S(1)}, bf16[2,2,64,896]{3,2,1,0:T(8,128)(2,1)}, u32[]{:S(2)}) copy-start(bf16[2,2,64,896]{3,2,1,0:T(8,128)(2,1)} %get-tuple-element.19) | copy-start | bytes 1376260
  72.3 43.0 %all-to-all-start.1 = ((bf16[32,144,256]{2,1,0:T(8,128)(2,1)}), bf16[32,144,256]{2,1,0:T(8,128)(2,1)S(1)}, u32[]{:S(2)}, u32[]{:S(2)}) async-start(bf16[32,144,256]{2,1,0:T(8,128)(2,1)} %get-tuple-element.17), calls=%async_computation.1 | async-start | bytes 4718592 | tf_op jit(solution)/shard_map/all_to_all | solution.py:404
  83.1 41.2 %collective-permute-start.1 = (bf16[2,2,64,896]{3,2,1,0:T(8,128)(2,1)S(1)}, bf16[2,2,64,896]{3,2,1,0:T(8,128)(2,1)S(1)}, u32[]{:S(2)}, u32[]{:S(2)}) collective-permute-start(bf16[2,2,64,896]{3,2,1,0:T(8,128)(2,1)S(1)} %copy-done.4), channel_id=1, source_target_pairs={{0,4},{4,0},{8,12},{12,8},{16,20},{20,16},{24,28},{28,24},{32,36},... | collective-permute-start | bytes 1376264 | tf_op jit(solution)/shard_map/ppermute | solution.py:403
  115.3 1.4 copy-start
  118.3 1.4 collective-permute-start.2
  120.4 34.3 %collective-permute-start.3 = (f32[16,128]{1,0:T(8,128)S(1)}, f32[16,128]{1,0:T(8,128)S(1)}, u32[]{:S(2)}, u32[]{:S(2)}) collective-permute-start(f32[16,128]{1,0:T(8,128)S(1)} %add.6), channel_id=1, source_target_pairs={{0,2},{1,3},{2,0},{3,1},{4,6},{5,7},{6,4},{7,5},{8,10},{9,11},{10,... | collective-permute-start | bytes 24584 | tf_op jit(solution)/shard_map/ppermute | solution.py:418
  124.3 0.8 copy-start.2

commit v3 on v2

--- a/solution.py
+++ b/solution.py
@@ -19,8 +19,8 @@
 SLOT_W = 2 * HD
 SUM_ROWS = 16
 MASKED = -1e30
-VMEM_BYTES = 60 * 1024 * 1024
-GOT_PARTS = 4
+VMEM_BYTES = 59 * 1024 * 1024
+SMALL_BYTES = 16 * 1024 * 1024
 BLOCKS_PER_CHUNK = 4
 
 NT = (((1,), (1,)), ((), ()))
@@ -29,7 +29,7 @@
 
 SMEM = pl.BlockSpec(memory_space=pltpu.SMEM)
 VMEM = pl.BlockSpec(memory_space=pltpu.VMEM)
-HBM = pl.BlockSpec(memory_space=pltpu.HBM)
+ANY = pl.BlockSpec(memory_space=pl.ANY)
 
 
 def dot(a, b, dims):
@@ -40,18 +40,16 @@
     return pl.ds(pl.multiple_of(start, HD), size)
 
 
-def send_kernel(group_size, me_ref, k_ref, v_ref, vb_ref, q_ref, ct_ref, send_ref, swap_ref, kv_ref, sem, swap_sem):
+def swap_kernel(me_ref, q_ref, ct_ref, swap_ref):
+    other = 1 - me_ref[0] % 2
+    for i, ref in enumerate((q_ref, ct_ref)):
+        for h in range(2):
+            swap_ref[i, h] = ref[h, :, lanes(other * HALF_Q, HALF_Q)]
+
+
+def send_kernel(group_size, k_ref, v_ref, vb_ref, send_ref, kv_ref, sem):
     block_len = k_ref.shape[1]
-    other = 1 - me_ref[0] % 2
     copies = []
-    for i, ref in enumerate((q_ref, ct_ref)):
-        copies.append(
-            pltpu.make_async_copy(
-                ref.at[:, :, lanes(other * HALF_Q, HALF_Q)], swap_ref.at[i], swap_sem.at[i]
-            )
-        )
-    for copy in copies:
-        copy.start()
     for g in range(KVH):
         cols = slice(g * HD, (g + 1) * HD)
         for h in range(2):
@@ -60,10 +58,10 @@
             kv_ref[g, here, HD:] = (
                 v_ref[h, :, cols].astype(jnp.float32) + vb_ref[:, cols]
             ).astype(jnp.bfloat16)
-    for d in range(group_size):
-        copy = pltpu.make_async_copy(kv_ref.at[d % 2], send_ref.at[d], sem.at[d])
-        copy.start()
-        copies.append(copy)
+        for d in range(g, group_size, KVH):
+            copy = pltpu.make_async_copy(kv_ref.at[g], send_ref.at[d], sem.at[d])
+            copy.start()
+            copies.append(copy)
     for copy in copies:
         copy.wait()
 
@@ -292,53 +290,33 @@
         copy.wait()
 
 
-def sums_kernel(got_ref, out_ref):
+def join_kernel(me_ref, mine_ref, theirs_ref, att_ref, qg_ref):
+    head = me_ref[0] % 2
+    for i, ref in enumerate((att_ref, qg_ref)):
+        for h in range(2):
+            ref[h, :, lanes(head * HALF_Q, HALF_Q)] = mine_ref[i, h]
+            ref[h, :, lanes((1 - head) * HALF_Q, HALF_Q)] = theirs_ref[i, h]
+
+
+def total_kernel(got_ref, kg_ref, vg_ref, sum_ref):
+    block_len = kg_ref.shape[1]
+
+    def total_of(g, here):
+        total = got_ref[g, here, :].astype(jnp.float32)
+        for d in range(g + KVH, got_ref.shape[0], KVH):
+            total += got_ref[d, here, :].astype(jnp.float32)
+        return total
+
     for g in range(KVH):
-        total = got_ref[g].astype(jnp.float32)
-        for d in range(g + 2, got_ref.shape[0], 2):
-            total += got_ref[d].astype(jnp.float32)
-        half = SUM_ROWS // 2
-        out_ref[g * half : (g + 1) * half, :] = (
-            total[:half, :HD] + total[:half, HD:] + total[half:, :HD]
-        )
-
-
-def finish_kernel(
-    group_size, me_ref, got_hbm, mine_ref, theirs_ref, att_ref, qg_ref, kg_ref, vg_ref, got_ref, sems, out_sems
-):
-    block_len = att_ref.shape[1]
-    pair_len = 2 * block_len
-    head = me_ref[0] % 2
-    part = group_size // GOT_PARTS
-    loads = []
-    for i in range(GOT_PARTS):
-        some = slice(i * part, (i + 1) * part)
-        loads.append(
-            pltpu.make_async_copy(got_hbm.at[some, :pair_len], got_ref.at[some], sems.at[i])
-        )
-        loads[i].start()
-    copies = []
-    for i, ref in enumerate((att_ref, qg_ref)):
-        for j, (source, at) in enumerate(((mine_ref, head), (theirs_ref, 1 - head))):
-            copies.append(
-                pltpu.make_async_copy(
-                    source.at[i], ref.at[:, :, lanes(at * HALF_Q, HALF_Q)], out_sems.at[2 * i + j]
-                )
-            )
-            copies[-1].start()
-    for load in loads:
-        load.wait()
-    for h in range(2):
-        here = slice(h * block_len, (h + 1) * block_len)
-        for g in range(KVH):
-            total = got_ref[g, here, :].astype(jnp.float32)
-            for d in range(g + 2, group_size, 2):
-                total += got_ref[d, here, :].astype(jnp.float32)
-            total = total.astype(jnp.bfloat16)
+        for h in range(2):
+            total = total_of(g, slice(h * block_len, (h + 1) * block_len)).astype(jnp.bfloat16)
             kg_ref[h, :, g * HD : (g + 1) * HD] = total[:, :HD]
             vg_ref[h, :, g * HD : (g + 1) * HD] = total[:, HD:]
-    for copy in copies:
-        copy.wait()
+        pieces = total_of(g, slice(2 * block_len, 2 * block_len + SUM_ROWS))
+        half = SUM_ROWS // 2
+        sum_ref[g * half : (g + 1) * half, :] = (
+            pieces[:half, :HD] + pieces[:half, HD:] + pieces[half:, :HD]
+        )
 
 
 def on_device(q_proj, k_proj, v_proj, q_bias, v_bias, cotangent, lengths):
@@ -353,19 +331,26 @@
     bf16, f32 = jnp.bfloat16, jnp.float32
     halves = jax.ShapeDtypeStruct((2, 2, block_len, HALF_Q), bf16)
 
-    sent, swap = pl.pallas_call(
+    swap = pl.pallas_call(
+        swap_kernel,
+        out_shape=halves,
+        in_specs=[SMEM, VMEM, VMEM],
+        out_specs=VMEM,
+        compiler_params=pltpu.CompilerParams(vmem_limit_bytes=SMALL_BYTES),
+        name="swap",
+    )(me, q, ct)
+    sent = pl.pallas_call(
         functools.partial(send_kernel, group_size),
-        out_shape=(jax.ShapeDtypeStruct((group_size, pair_len, SLOT_W), bf16), halves),
-        in_specs=[SMEM, VMEM, VMEM, VMEM, HBM, HBM],
-        out_specs=(HBM, HBM),
+        out_shape=jax.ShapeDtypeStruct((group_size, pair_len, SLOT_W), bf16),
+        in_specs=[VMEM, VMEM, VMEM],
+        out_specs=ANY,
         scratch_shapes=[
             pltpu.VMEM((KVH, pair_len, SLOT_W), bf16),
             pltpu.SemaphoreType.DMA((group_size,)),
-            pltpu.SemaphoreType.DMA((2,)),
         ],
         compiler_params=pltpu.CompilerParams(vmem_limit_bytes=VMEM_BYTES),
         name="send",
-    )(me, k, v, v_bias[None], q, ct)
+    )(k, v, v_bias[None])
     partners = [(i, i ^ 1) for i in range(group_size)]
     other = lax.ppermute(swap, "ctx", partners)
     gathered = lax.all_to_all(sent, "ctx", 0, 0)
@@ -375,8 +360,8 @@
     mine, back, parts = pl.pallas_call(
         functools.partial(attention_kernel, group_size),
         out_shape=(halves, halves, jax.ShapeDtypeStruct(slots, bf16)),
-        in_specs=[SMEM, SMEM, VMEM, VMEM, HBM, VMEM, HBM],
-        out_specs=(HBM, HBM, HBM),
+        in_specs=[SMEM, SMEM, VMEM, VMEM, ANY, VMEM, ANY],
+        out_specs=(ANY, ANY, ANY),
         scratch_shapes=[
             pltpu.VMEM(halves.shape, bf16),
             pltpu.VMEM(halves.shape, bf16),
@@ -402,36 +387,28 @@
 
     theirs = lax.ppermute(back, "ctx", partners)
     got = lax.all_to_all(parts, "ctx", 0, 0)
-    sums = pl.pallas_call(
-        sums_kernel,
-        out_shape=jax.ShapeDtypeStruct((SUM_ROWS, HD), f32),
-        grid=(1,),
-        in_specs=[
-            pl.BlockSpec((group_size, SUM_ROWS, SLOT_W), lambda i: (0, pair_len // SUM_ROWS, 0))
-        ],
-        out_specs=pl.BlockSpec((SUM_ROWS, HD), lambda i: (0, 0)),
-        compiler_params=pltpu.CompilerParams(vmem_limit_bytes=VMEM_BYTES),
-        name="sums",
+    wide = jax.ShapeDtypeStruct(q.shape, bf16)
+    narrow = jax.ShapeDtypeStruct(k.shape, bf16)
+    attended, q_grad = pl.pallas_call(
+        join_kernel,
+        out_shape=(wide, wide),
+        in_specs=[SMEM, VMEM, VMEM],
+        out_specs=(VMEM, VMEM),
+        cost_estimate=pl.CostEstimate(flops=1_000_000, bytes_accessed=4_000_000, transcendentals=0),
+        compiler_params=pltpu.CompilerParams(vmem_limit_bytes=SMALL_BYTES),
+        name="join",
+    )(me, mine, theirs)
+    k_grad, v_grad, sums = pl.pallas_call(
+        total_kernel,
+        out_shape=(narrow, narrow, jax.ShapeDtypeStruct((SUM_ROWS, HD), f32)),
+        in_specs=[VMEM],
+        out_specs=(VMEM, VMEM, VMEM),
+        compiler_params=pltpu.CompilerParams(vmem_limit_bytes=SMALL_BYTES),
+        name="total",
     )(got)
     for axis_step in (1, 2):
         size = lax.axis_size("dp")
         sums = sums + lax.ppermute(sums, "dp", [(i, i ^ axis_step) for i in range(size)])
-    wide = jax.ShapeDtypeStruct(q.shape, bf16)
-    narrow = jax.ShapeDtypeStruct(k.shape, bf16)
-    attended, q_grad, k_grad, v_grad = pl.pallas_call(
-        functools.partial(finish_kernel, group_size),
-        out_shape=(wide, wide, narrow, narrow),
-        in_specs=[SMEM, HBM, HBM, HBM],
-        out_specs=(HBM, HBM, VMEM, VMEM),
-        scratch_shapes=[
-            pltpu.VMEM((group_size, pair_len, SLOT_W), bf16),
-            pltpu.SemaphoreType.DMA((GOT_PARTS,)),
-            pltpu.SemaphoreType.DMA((4,)),
-        ],
-        cost_estimate=pl.CostEstimate(flops=1_000_000, bytes_accessed=6_000_000, transcendentals=0),
-        compiler_params=pltpu.CompilerParams(vmem_limit_bytes=VMEM_BYTES),
-        name="finish",
-    )(me, got, mine, theirs)
     by_head = sums.reshape(KVH, SUM_ROWS // 2, HD)
     return (
         attended[None],

time: 158 us -> 113 us (0.72)
  Pallas kernels: 57.2 us -> 12.9 us
  starting transfers between devices: 27.3 us -> 29.9 us
  local copies, waits for them, and re-layouts: 6.08 us -> 3.88 us
    pallas_call x3 -> x4, Pallas kernels: 47.4 us -> 4.5 us  [the longest x1 2.53 us: on_device(): pl.pallas_call(functools.partial(send_kernel, group_size), out_shape=jax....]
    all_to_all x1, starting transfers between devices: 10.8 us -> 13.1 us  [on_device(): got = lax.all_to_all(parts, 'ctx', 0, 0)]
    unnamed x14 -> x12, local copies, waits for them, and re-layouts: 4.32 us -> 2.11 us
  transfers between devices with their start and end apart: 6 -> 6, of which waited for: 3 -> 4; matrix products, arithmetic and copies ran while one was open for 1% -> 1% of each run, Pallas kernels for 20% -> 2%
where the time goes in v3:
time: 113 us; the launch traced here: 111 us
  waiting for transfers between devices  63.6 us (56%)
  starting transfers between devices  29.9 us (26%)
  Pallas kernels  12.9 us (11%)
  local copies, waits for them, and re-layouts  3.88 us (3%)
    ppermute x1, waiting for transfers between devices, on_device(): other = lax.ppermute(swap, 'ctx', partners)  32.1 us
    all_to_all x1, waiting for transfers between devices, on_device(): got = lax.all_to_all(parts, 'ctx', 0, 0)  29.7 us
    all_to_all x1, starting transfers between devices, on_device(): got = lax.all_to_all(parts, 'ctx', 0, 0)  13.1 us
    all_to_all x1, starting transfers between devices, on_device(): gathered = lax.all_to_all(sent, 'ctx', 0, 0)  8.9 us
    pallas_call x1, Pallas kernels, on_device(): pl.pallas_call(functools.partial(attention_kernel, group_size), out_shape...  8.41 us
    ppermute x2, starting transfers between devices, on_device(): lax.ppermute(sums, 'dp', [(i, i ^ axis_step) for i in range(size)])  4.17 us
    pallas_call x1, Pallas kernels, on_device(): pl.pallas_call(functools.partial(send_kernel, group_size), out_shape=jax....  2.53 us
  transfers between devices with their start and end apart: 6, of which 4 were waited for; matrix products, arithmetic and copies ran while one was open for 1% of the time, Pallas kernels for 2%

profile of v3, /device:TPU:0, one launch (start us, length us, event | category | flops | bytes accessed | tf_op | source)
XLA Modules:
  0.0 111.0 jit_solution(13696108181655226559)
XLA Ops:
  0.6 2.5 %send.1 = bf16[32,128,256]{2,1,0:T(8,128)(2,1)} custom-call(bf16[2,64,256]{2,1,0:T(8,128)(2,1)} %bitcast.18, bf16[2,64,256]{2,1,0:T(8,128)(2,1)} %bitcast.19, f32[1,256]{1,0:T(1,128)} %bitcast.21), custom_call_target="tpu_custom_call" | custom-call | tf_op jit(solution)/shard_map/send/pallas_call | solution.py:342
  3.2 0.0 copy-start.1
  3.2 0.0 copy-start.2
  3.2 0.0 copy-start.4
  3.2 8.9 %all-to-all-start = ((bf16[32,128,256]{2,1,0:T(8,128)(2,1)}), bf16[32,128,256]{2,1,0:T(8,128)(2,1)S(1)}, u32[]{:S(2)}, u32[]{:S(2)}) async-start(bf16[32,128,256]{2,1,0:T(8,128)(2,1)} %send.1), calls=%async_computation | async-start | bytes 4194304 | tf_op jit(solution)/shard_map/all_to_all | solution.py:356
  12.2 1.9 %collective-permute-start = (bf16[2,2,64,896]{3,2,1,0:T(8,128)(2,1)S(1)}, bf16[2,2,64,896]{3,2,1,0:T(8,128)(2,1)S(1)}, u32[]{:S(2)}, u32[]{:S(2)}) collective-permute-start(bf16[2,2,64,896]{3,2,1,0:T(8,128)(2,1)S(1)} %swap.1), channel_id=1, source_target_pairs={{0,4},{4,0},{8,12},{12,8},{16,20},{20,16},{24,28},{28,24},{32,36},... | collective-permute-start | bytes 1376264 | tf_op jit(solution)/shard_map/ppermute | solution.py:355
  14.1 0.6 broadcast_in_dim.22.qb_ref
  14.7 32.1 %collective-permute-done.other_hbm = bf16[2,2,64,896]{3,2,1,0:T(8,128)(2,1)S(1)} collective-permute-done((bf16[2,2,64,896]{3,2,1,0:T(8,128)(2,1)S(1)}, bf16[2,2,64,896]{3,2,1,0:T(8,128)(2,1)S(1)}, u32[]{:S(2)}, u32[]{:S(2)}) %collective-permute-start) | collective-permute-done | bytes 458784 | tf_op jit(solution)/shard_map/ppermute | solution.py:355
  46.7 0.0 all-to-all-done.kv_ref
  46.7 0.8 copy-done.5
  47.5 1.3 %copy-done.3 = bf16[32,128,256]{2,1,0:T(8,128)(2,1)} copy-done((bf16[32,128,256]{2,1,0:T(8,128)(2,1)}, bf16[32,128,256]{2,1,0:T(8,128)(2,1)S(1)}, u32[]{:S(2)}) %copy-start.3) | copy-done | bytes 2097176
  48.8 8.4 %attention.1 = (bf16[2,2,64,896]{3,2,1,0:T(8,128)(2,1)}, bf16[2,2,64,896]{3,2,1,0:T(8,128)(2,1)}, bf16[32,144,256]{2,1,0:T(8,128)(2,1)}) custom-call(s32[1]{0:T(128)} %bitcast.me_ref, s32[1,16]{1,0:T(1,128)} %len_ref.1, bf16[2,64,1792]{2,1,0:T(8,128)(2,1)} %bitcast.14, bf16[2,64,1792]{2,1,0:T(8,128)(2,1)} %bitcast.16, bf16[2,2,64,896]{3,2,1,0:T(8,128)(2,1)} %copy-done.5, ...), custom_call_target="tpu_custom_call" | custom-call | flops 3000000000 | bytes 10000000 | tf_op jit(solution)/shard_map/attention/pallas_call | solution.py:360
  57.3 13.1 %all-to-all-start.1 = ((bf16[32,144,256]{2,1,0:T(8,128)(2,1)}), bf16[32,144,256]{2,1,0:T(8,128)(2,1)S(1)}, u32[]{:S(2)}, u32[]{:S(2)}) async-start(bf16[32,144,256]{2,1,0:T(8,128)(2,1)} %get-tuple-element.18), calls=%async_computation.1 | async-start | bytes 4718592 | tf_op jit(solution)/shard_map/all_to_all | solution.py:389
  70.4 0.0 copy-start
  70.4 1.9 %collective-permute-start.1 = (bf16[2,2,64,896]{3,2,1,0:T(8,128)(2,1)}, bf16[2,2,64,896]{3,2,1,0:T(8,128)(2,1)S(1)}, u32[]{:S(2)}, u32[]{:S(2)}) collective-permute-start(bf16[2,2,64,896]{3,2,1,0:T(8,128)(2,1)} %get-tuple-element.15), channel_id=1, source_target_pairs={{0,4},{4,0},{8,12},{12,8},{16,20},{20,16},{24,28},{28,24},{32,36},... | collective-permute-start | bytes 1376264 | tf_op jit(solution)/shard_map/ppermute | solution.py:388
  72.3 29.7 %all-to-all-done.1.got_ref = bf16[32,144,256]{2,1,0:T(8,128)(2,1)S(1)} async-done(((bf16[32,144,256]{2,1,0:T(8,128)(2,1)}), bf16[32,144,256]{2,1,0:T(8,128)(2,1)S(1)}, u32[]{:S(2)}, u32[]{:S(2)}) %all-to-all-start.1) | async-done | bytes 2359328 | tf_op jit(solution)/shard_map/all_to_all | solution.py:389
  101.9 0.9 total.1
  102.9 0.0 collective-permute-start.2
  102.9 1.2 %collective-permute-done.2 = f32[16,128]{1,0:T(8,128)S(1)} collective-permute-done((f32[16,128]{1,0:T(8,128)S(1)}, f32[16,128]{1,0:T(8,128)S(1)}, u32[]{:S(2)}, u32[]{:S(2)}) %collective-permute-start.2) | collective-permute-done | bytes 8224 | tf_op jit(solution)/shard_map/ppermute | solution.py:411
  104.1 4.2 %collective-permute-start.3 = (f32[16,128]{1,0:T(8,128)S(1)}, f32[16,128]{1,0:T(8,128)S(1)}, u32[]{:S(2)}, u32[]{:S(2)}) collective-permute-start(f32[16,128]{1,0:T(8,128)S(1)} %add.6), channel_id=1, source_target_pairs={{0,2},{1,3},{2,0},{3,1},{4,6},{5,7},{6,4},{7,5},{8,10},{9,11},{10,... | collective-permute-start | bytes 24584 | tf_op jit(solution)/shard_map/ppermute | solution.py:411
  108.2 1.0 join.1
  109.2 0.6 collective-permute-done.3
  109.9 0.6 slice.9
  110.4 0.6 reshape.19
  (10 shorter events, 0.1 us)
Async XLA Ops:
  3.2 9.0 %copy-start.1 = (bf16[1,2,64,1792]{3,2,1,0:T(8,128)(2,1)S(1)}, bf16[1,2,64,1792]{3,2,1,0:T(8,128)(2,1)}, u32[]{:S(2)}) copy-start(bf16[1,2,64,1792]{3,2,1,0:T(8,128)(2,1)} %param.7) | copy-start | bytes 1376260
  3.2 8.9 %copy-start.2 = (bf16[1,2,64,1792]{3,2,1,0:T(8,128)(2,1)S(1)}, bf16[1,2,64,1792]{3,2,1,0:T(8,128)(2,1)}, u32[]{:S(2)}) copy-start(bf16[1,2,64,1792]{3,2,1,0:T(8,128)(2,1)} %param.12) | copy-start | bytes 1376260
  3.2 10.9 %copy-start.4 = (f32[1792]{0:T(1024)S(1)}, f32[1792]{0:T(1024)}, u32[]{:S(2)}) copy-start(f32[1792]{0:T(1024)} %param.10) | copy-start | bytes 21508
  3.2 43.5 %all-to-all-start = ((bf16[32,128,256]{2,1,0:T(8,128)(2,1)}), bf16[32,128,256]{2,1,0:T(8,128)(2,1)S(1)}, u32[]{:S(2)}, u32[]{:S(2)}) async-start(bf16[32,128,256]{2,1,0:T(8,128)(2,1)} %send.1), calls=%async_computation | async-start | bytes 4194304 | tf_op jit(solution)/shard_map/all_to_all | solution.py:356
  12.2 34.6 %collective-permute-start = (bf16[2,2,64,896]{3,2,1,0:T(8,128)(2,1)S(1)}, bf16[2,2,64,896]{3,2,1,0:T(8,128)(2,1)S(1)}, u32[]{:S(2)}, u32[]{:S(2)}) collective-permute-start(bf16[2,2,64,896]{3,2,1,0:T(8,128)(2,1)S(1)} %swap.1), channel_id=1, source_target_pairs={{0,4},{4,0},{8,12},{12,8},{16,20},{20,16},{24,28},{28,24},{32,36},... | collective-permute-start | bytes 1376264 | tf_op jit(solution)/shard_map/ppermute | solution.py:355
  46.7 0.8 copy-start.5
  47.5 1.3 %copy-start.3 = (bf16[32,128,256]{2,1,0:T(8,128)(2,1)}, bf16[32,128,256]{2,1,0:T(8,128)(2,1)S(1)}, u32[]{:S(2)}) copy-start(bf16[32,128,256]{2,1,0:T(8,128)(2,1)S(1)} %all-to-all-done.kv_ref) | copy-start | bytes 6291460
  57.3 44.7 %all-to-all-start.1 = ((bf16[32,144,256]{2,1,0:T(8,128)(2,1)}), bf16[32,144,256]{2,1,0:T(8,128)(2,1)S(1)}, u32[]{:S(2)}, u32[]{:S(2)}) async-start(bf16[32,144,256]{2,1,0:T(8,128)(2,1)} %get-tuple-element.18), calls=%async_computation.1 | async-start | bytes 4718592 | tf_op jit(solution)/shard_map/all_to_all | solution.py:389
  70.4 37.8 %copy-start = (bf16[2,2,64,896]{3,2,1,0:T(8,128)(2,1)S(1)}, bf16[2,2,64,896]{3,2,1,0:T(8,128)(2,1)}, u32[]{:S(2)}) copy-start(bf16[2,2,64,896]{3,2,1,0:T(8,128)(2,1)} %get-tuple-element.14.mine_ref) | copy-start | bytes 1376260
  70.4 37.8 %collective-permute-start.1 = (bf16[2,2,64,896]{3,2,1,0:T(8,128)(2,1)}, bf16[2,2,64,896]{3,2,1,0:T(8,128)(2,1)S(1)}, u32[]{:S(2)}, u32[]{:S(2)}) collective-permute-start(bf16[2,2,64,896]{3,2,1,0:T(8,128)(2,1)} %get-tuple-element.15), channel_id=1, source_target_pairs={{0,4},{4,0},{8,12},{12,8},{16,20},{20,16},{24,28},{28,24},{32,36},... | collective-permute-start | bytes 1376264 | tf_op jit(solution)/shard_map/ppermute | solution.py:388
  102.9 1.2 %collective-permute-start.2 = (f32[16,128]{1,0:T(8,128)S(1)}, f32[16,128]{1,0:T(8,128)S(1)}, u32[]{:S(2)}, u32[]{:S(2)}) collective-permute-start(f32[16,128]{1,0:T(8,128)S(1)} %get-tuple-element.21), channel_id=1, source_target_pairs={{0,1},{1,0},{2,3},{3,2},{4,5},{5,4},{6,7},{7,6},{8,9},{9,8},{10,11... | collective-permute-start | bytes 24584 | tf_op jit(solution)/shard_map/ppermute | solution.py:411
  104.1 5.8 %collective-permute-start.3 = (f32[16,128]{1,0:T(8,128)S(1)}, f32[16,128]{1,0:T(8,128)S(1)}, u32[]{:S(2)}, u32[]{:S(2)}) collective-permute-start(f32[16,128]{1,0:T(8,128)S(1)} %add.6), channel_id=1, source_target_pairs={{0,2},{1,3},{2,0},{3,1},{4,6},{5,7},{6,4},{7,5},{8,10},{9,11},{10,... | collective-permute-start | bytes 24584 | tf_op jit(solution)/shard_map/ppermute | solution.py:411

commit v4 on v3

v4 whole, which is shorter than its diff:
```python
import functools
import math

import jax
import jax.numpy as jnp
from jax import lax
from jax.experimental import pallas as pl
from jax.experimental.pallas import tpu as pltpu
from jax.sharding import PartitionSpec as P

HD = 128
KVH = 2
GROUP = 7
HQ = 1792
KW = 256
MOST = 1024

HALF_Q = GROUP * HD
SLOT_W = 2 * HD
SUM_ROWS = 16
MASKED = -1e30
PREP_FLOPS = 5_600_000_000
SWAP_FLOPS = 1_000_000
JOIN_FLOPS = 40_000_000_000
FINISH_FLOPS = 1_000_000
VMEM_BYTES = 59 * 1024 * 1024
SMALL_BYTES = 16 * 1024 * 1024
BLOCKS_PER_CHUNK = 4

NT = (((1,), (1,)), ((), ()))
NN = (((1,), (0,)), ((), ()))
TN = (((0,), (0,)), ((), ()))

SMEM = pl.BlockSpec(memory_space=pltpu.SMEM)
VMEM = pl.BlockSpec(memory_space=pltpu.VMEM)
ANY = pl.BlockSpec(memory_space=pl.ANY)


def dot(a, b, dims):
    return lax.dot_general(a, b, dims, preferred_element_type=jnp.float32)


def lanes(start, size):
    return pl.ds(pl.multiple_of(start, HD), size)


def route(c, d, group_size, reach):
    pair = d - d % 2
    late = (c > pair + 1) & (c <= pair + reach + 1)
    relay = (c < pair - reach) & (c <= group_size - 3 - pair)
    return jnp.where(late, 1, jnp.where(relay, 2, 0))


def blocks_kernel(me_ref, k_hbm, v_hbm, vb_hbm, early_ref, late_ref, near_ref, far_ref, k_ref, v_ref, vb_ref, sems):
    head = me_ref[0] % 2
    pairs = ((k_hbm, k_ref), (v_hbm, v_ref), (vb_hbm, vb_ref))
    loads = [
        pltpu.make_async_copy(source, into, sems.at[i]) for i, (source, into) in enumerate(pairs)
    ]
    for load in loads:
        load.start()
    for load in loads:
        load.wait()
    for h, ref in enumerate((early_ref, late_ref)):
        for g in range(KVH):
            cols = slice(g * HD, (g + 1) * HD)
            ref[g, :, :HD] = k_ref[h, :, cols]
            ref[g, :, HD:] = (v_ref[h, :, cols].astype(jnp.float32) + vb_ref[:, cols]).astype(
                jnp.bfloat16
            )
    near_ref[...] = early_ref[head]
    far_ref[...] = early_ref[1 - head]


def swap_kernel(me_ref, q_hbm, ct_hbm, late_hbm, swap_ref, q_ref, ct_ref, late_ref, sems):
    other = 1 - me_ref[0] % 2
    cols = lanes(other * HALF_Q, HALF_Q)
    pairs = ((q_hbm.at[:, :, cols], q_ref), (ct_hbm.at[:, :, cols], ct_ref), (late_hbm.at[other], late_ref))
    loads = [
        pltpu.make_async_copy(source, into, sems.at[i]) for i, (source, into) in enumerate(pairs)
    ]
    for load in loads:
        load.start()
    for i, ref in enumerate((q_ref, ct_ref)):
        loads[i].wait()
        for h in range(2):
            for t in range(GROUP):
                swap_ref[(2 * i + h) * GROUP + t] = ref[h, :, t * HD : (t + 1) * HD]
    loads[2].wait()
    swap_ref[4 * GROUP] = late_ref[:, :HD]
    swap_ref[4 * GROUP + 1] = late_ref[:, HD:]


def prepare_kernel(
    me_ref, q_ref, ct_ref, other_ref, qb_ref, q_rows, d_rows
):
    block_len = q_ref.shape[1]
    pair_len = 2 * block_len
    head = me_ref[0] % 2
    for h in range(2):
        own_at = pl.multiple_of((head if h == 0 else 1 - head) * block_len, block_len)
        partner_at = pl.multiple_of(block_len - own_at, block_len)
        for t in range(GROUP):
            own_lanes = lanes(head * HALF_Q + t * HD, HD)
            bias = qb_ref[:, own_lanes]
            own_rows = pl.ds(t * pair_len + own_at, block_len)
            partner_rows = pl.ds(t * pair_len + partner_at, block_len)
            q_rows[h, own_rows, :] = (q_ref[h, :, own_lanes].astype(jnp.float32) + bias).astype(
                jnp.bfloat16
            )
            q_rows[h, partner_rows, :] = (
                other_ref[h * GROUP + t].astype(jnp.float32) + bias
            ).astype(jnp.bfloat16)
            d_rows[h, own_rows, :] = ct_ref[h, :, own_lanes]
            d_rows[h, partner_rows, :] = other_ref[(2 + h) * GROUP + t]


def send_kernel(
    group_size, reach, me_ref, early_hbm, late_hbm, relay_hbm, near_hbm, far_hbm, send_ref, all_ref, sem, load_sems
):
    me = me_ref[0]
    loads = [
        pltpu.make_async_copy(source, all_ref.at[i], load_sems.at[i])
        for i, source in enumerate((early_hbm, late_hbm, relay_hbm))
    ]
    for load in loads:
        load.start()
    for load in loads:
        load.wait()
    copies = []
    for d in range(group_size):
        kind = route(me, jnp.int32(d), group_size, reach)
        copy = pltpu.make_async_copy(all_ref.at[kind, d % KVH], send_ref.at[d], sem.at[d])
        copy.start()
        copies.append(copy)
    for copy in copies:
        copy.wait()


def attention_kernel(
    group_size,
    reach,
    me_ref,
    len_ref,
    q_hbm,
    d_hbm,
    other_hbm,
    kv_hbm,
    late_hbm,
    near_hbm,
    far_hbm,
    mine_hbm,
    back_hbm,
    parts_hbm,
    own_hbm,
    near_grad_hbm,
    far_grad_hbm,
    other_ref,
    mine_ref,
    back_ref,
    all_ref,
    stage_ref,
    win_ref,
    q_both,
    d_both,
    p_ref,
    grad_ref,
    acc_ref,
    row_ref,
    sum_ref,
    in_sems,
    out_sems,
):
    block_len = mine_ref.shape[1]
    pair_len = 2 * block_len
    rows = GROUP * pair_len
    chunk = BLOCKS_PER_CHUNK * block_len
    scale = 1.0 / math.sqrt(HD)
    log2e = 1.0 / math.log(2.0)
    last_block = 2 * group_size - 1
    me = me_ref[0]
    head = me % 2
    pair = me - head
    n_docs = len_ref.shape[1]
    own_late, other_late, near, far = range(group_size, group_size + 4)

    loads = [
        pltpu.make_async_copy(source, into, in_sems.at[i])
        for i, (source, into) in enumerate(
            (
                (other_hbm.at[4 * GROUP :], other_ref),
                (q_hbm, q_both),
                (d_hbm, d_both),
                (kv_hbm, all_ref.at[:group_size]),
                (late_hbm.at[head], all_ref.at[own_late]),
                (near_hbm, all_ref.at[near]),
                (far_hbm, all_ref.at[far]),
            )
        )
    ]
    for load in loads:
        load.start()

    def place(block):
        lowest_late = last_block - 1 - pair - reach
        doubled = jnp.where(
            group_size - 1 - block < pair - reach,
            group_size - 1 - block,
            jnp.where(block == lowest_late + head, near, far),
        )
        early = jnp.where(block <= pair + 1, block, doubled)
        c = last_block - block
        late = jnp.where(c == me, own_late, jnp.where(c == pair + 1 - head, other_late, c))
        return jnp.where(block < group_size, early, late)

    stage_ref[...] = jnp.zeros_like(stage_ref)
    sum_ref[...] = jnp.zeros_like(sum_ref)
    for load in loads:
        load.wait()
    all_ref[other_late, :, :HD] = other_ref[0]
    all_ref[other_late, :, HD:] = other_ref[1]

    def query_unit(h, carry):
        first_block = jnp.where(h == 0, pair, last_block - 1 - pair)
        first_pos = first_block * block_len
        own_at = pl.multiple_of(jnp.where(h == 0, head, 1 - head) * block_len, block_len)
        partner_at = pl.multiple_of(block_len - own_at, block_len)
        lane = lax.broadcasted_iota(jnp.int32, (1, rows), 1)
        query_pos = first_pos + lane % pair_len
        query_start = jnp.zeros_like(query_pos)
        end = jnp.int32(0)
        first_start = jnp.int32(0)
        for k in range(n_docs):
            end = end + len_ref[0, k]
            query_start = jnp.where(query_pos >= end, end, query_start)
            first_start = jnp.where(first_pos >= end, end, first_start)
        low = first_start // block_len
        n_blocks = first_block + 2 - low
        n_chunks = (n_blocks + BLOCKS_PER_CHUNK - 1) // BLOCKS_PER_CHUNK

        def load(i, carry):
            win_ref[pl.ds(pl.multiple_of(i * block_len, block_len), block_len), :] = all_ref[
                place(jnp.minimum(low + i, first_block + 1))
            ]
            return carry

        lax.fori_loop(0, n_chunks * BLOCKS_PER_CHUNK, load, 0)

        q_rows, d_rows = q_both.at[h], d_both.at[h]

        def window(i):
            return pl.ds(pl.multiple_of(i * chunk, chunk), chunk)

        def score_step(i, top):
            at = window(i)
            s = dot(win_ref[at, :HD], q_rows[...], NT) * (scale * log2e)
            key_pos = (low * block_len + i * chunk) + lax.broadcasted_iota(
                jnp.int32, (chunk, 1), 0
            )
            visible = (key_pos >= query_start) & (key_pos <= query_pos)
            s = jnp.where(visible, s, MASKED)
            p_ref[at, :] = s
            return jnp.maximum(top, jnp.max(s, axis=0, keepdims=True))

        top = lax.fori_loop(0, n_chunks, score_step, jnp.full((1, rows), MASKED, jnp.float32))

        acc_ref[...] = jnp.zeros_like(acc_ref)

        def out_step(i, total):
            at = window(i)
            e = jnp.exp2(p_ref[at, :] - top)
            p_ref[at, :] = e
            acc_ref[...] += dot(win_ref[at, HD:], e.astype(jnp.bfloat16), TN)
            return total + jnp.sum(e, axis=0, keepdims=True)

        total = lax.fori_loop(0, n_chunks, out_step, jnp.zeros((1, rows), jnp.float32))
        inverse = 1.0 / total
        summed = acc_ref[...] * inverse
        delta = jnp.sum(
            summed * jnp.transpose(d_rows[...].astype(jnp.float32)), axis=0, keepdims=True
        )
        row_ref[...] = jnp.transpose(summed)
        for t in range(GROUP):
            mine_ref[h * GROUP + t] = row_ref[
                pl.ds(t * pair_len + own_at, block_len), :
            ].astype(jnp.bfloat16)
            back_ref[h * GROUP + t] = row_ref[
                pl.ds(t * pair_len + partner_at, block_len), :
            ].astype(jnp.bfloat16)

        acc_ref[...] = jnp.zeros_like(acc_ref)

        def grad_step(i, value_total):
            at = window(i)
            p = p_ref[at, :] * inverse
            dp = dot(win_ref[at, HD:], d_rows[...], NT)
            ds = (p * (dp - delta)).astype(jnp.bfloat16)
            value_part = dot(p.astype(jnp.bfloat16), d_rows[...], NN)
            grad_ref[at, HD:] = value_part
            grad_ref[at, :HD] = dot(ds, q_rows[...], NN) * scale
            acc_ref[...] += dot(win_ref[at, :HD], ds, TN)
            return value_total + jnp.sum(value_part, axis=0, keepdims=True)

        value_total = lax.fori_loop(0, n_chunks, grad_step, jnp.zeros((1, HD), jnp.float32))
        sum_ref[GROUP : GROUP + 1, :] += value_total
        row_ref[...] = jnp.transpose(acc_ref[...] * scale)
        for t in range(GROUP):
            mine_ref[(2 + h) * GROUP + t] = row_ref[
                pl.ds(t * pair_len + own_at, block_len), :
            ].astype(jnp.bfloat16)
            back_ref[(2 + h) * GROUP + t] = row_ref[
                pl.ds(t * pair_len + partner_at, block_len), :
            ].astype(jnp.bfloat16)
            sum_ref[t : t + 1, :] += jnp.sum(
                row_ref[t * pair_len : (t + 1) * pair_len, :], axis=0, keepdims=True
            )

        def store(i, carry):
            slot = place(low + i)
            part = grad_ref[pl.ds(pl.multiple_of(i * block_len, block_len), block_len), :]
            stage_ref[slot, :block_len, :] = (
                stage_ref[slot, :block_len, :].astype(jnp.float32) + part
            ).astype(jnp.bfloat16)
            return carry

        lax.fori_loop(0, n_blocks, store, 0)
        return carry

    lax.fori_loop(0, 2, query_unit, 0)

    sums = sum_ref[...]
    high = sums.astype(jnp.bfloat16).astype(jnp.float32)
    middle = (sums - high).astype(jnp.bfloat16).astype(jnp.float32)
    lowest = sums - high - middle
    pieces = jnp.concatenate(
        [
            jnp.concatenate([high, middle], axis=1),
            jnp.concatenate([lowest, jnp.zeros_like(lowest)], axis=1),
        ],
        axis=0,
    ).astype(jnp.bfloat16)
    for d in range(group_size):
        stage_ref[d, block_len:, :] = pieces
    back_ref[4 * GROUP] = stage_ref[other_late, :block_len, :HD]
    back_ref[4 * GROUP + 1] = stage_ref[other_late, :block_len, HD:]
    stores = [
        pltpu.make_async_copy(source, into, out_sems.at[i])
        for i, (source, into) in enumerate(
            (
                (back_ref, back_hbm),
                (stage_ref.at[near, :block_len], near_grad_hbm),
                (stage_ref.at[far, :block_len], far_grad_hbm),
                (stage_ref.at[:group_size], parts_hbm),
                (mine_ref, mine_hbm),
                (stage_ref.at[own_late, :block_len], own_hbm),
            )
        )
    ]
    for store in stores:
        store.start()
    for store in stores:
        store.wait()


def join_kernel(me_ref, mine_ref, theirs_ref, near_hbm, far_hbm, att_ref, qg_ref):
    head = me_ref[0] % 2
    for i, ref in enumerate((att_ref, qg_ref)):
        for h in range(2):
            for t in range(GROUP):
                tile = (2 * i + h) * GROUP + t
                ref[h, :, lanes(head * HALF_Q + t * HD, HD)] = mine_ref[tile]
                ref[h, :, lanes((1 - head) * HALF_Q + t * HD, HD)] = theirs_ref[tile]


def total_kernel(
    group_size,
    reach,
    me_ref,
    got_ref,
    near_ref,
    far_ref,
    own_ref,
    theirs_ref,
    joined_hbm,
    relay_ref,
    total_ref,
    sum_ref,
    acc_ref,
):
    block_len = total_ref.shape[2]
    me = me_ref[0]
    head = me % 2
    half = SUM_ROWS // 2
    acc_ref[2] = jnp.zeros_like(acc_ref[2])
    acc_ref[0, head] = near_ref[...].astype(jnp.float32)
    acc_ref[0, 1 - head] = far_ref[...].astype(jnp.float32)
    acc_ref[1, head] = own_ref[...].astype(jnp.float32)
    acc_ref[1, 1 - head, :, :HD] = theirs_ref[4 * GROUP].astype(jnp.float32)
    acc_ref[1, 1 - head, :, HD:] = theirs_ref[4 * GROUP + 1].astype(jnp.float32)
    for d in range(group_size):
        kind = route(me, jnp.int32(d), group_size, reach)
        acc_ref[kind, d % KVH] += got_ref[d, :block_len, :].astype(jnp.float32)
    total_ref[...] = acc_ref[:2]
    relay_ref[...] = acc_ref[2].astype(jnp.bfloat16)
    for g in range(KVH):
        pieces = got_ref[g, block_len:, :].astype(jnp.float32)
        for d in range(g + KVH, group_size, KVH):
            pieces += got_ref[d, block_len:, :].astype(jnp.float32)
        sum_ref[g * half : (g + 1) * half, :] = (
            pieces[:half, :HD] + pieces[:half, HD:] + pieces[half:, :HD]
        )


def finish_kernel(total_ref, relay_ref, kg_ref, vg_ref):
    for g in range(KVH):
        cols = slice(g * HD, (g + 1) * HD)
        early = total_ref[0, g] + relay_ref[g].astype(jnp.float32)
        for h, total in enumerate((early, total_ref[1, g])):
            total = total.astype(jnp.bfloat16)
            kg_ref[h, :, cols] = total[:, :HD]
            vg_ref[h, :, cols] = total[:, HD:]


def bias_kernel(a_ref, b_ref, finished_hbm, q_sum_ref, v_sum_ref):
    total = a_ref[...] + b_ref[...]
    half = SUM_ROWS // 2
    for g in range(KVH):
        for t in range(GROUP):
            at = (g * GROUP + t) * HD
            q_sum_ref[:, at : at + HD] = total[g * half + t : g * half + t + 1]
        v_sum_ref[:, g * HD : (g + 1) * HD] = total[g * half + GROUP : (g + 1) * half]


def on_device(q_proj, k_proj, v_proj, q_bias, v_bias, cotangent, lengths):
    group_size = lax.axis_size("ctx")
    me = lax.axis_index("ctx").astype(jnp.int32)[None]
    q, ct, k, v = q_proj[0], cotangent[0], k_proj[0], v_proj[0]
    block_len = q.shape[1]
    reach = MOST // block_len
    rows = GROUP * 2 * block_len
    window = -(-(reach + 2) // BLOCKS_PER_CHUNK) * BLOCKS_PER_CHUNK * block_len
    bf16, f32 = jnp.bfloat16, jnp.float32
    tiles = jax.ShapeDtypeStruct((4 * GROUP, block_len, HD), bf16)
    more_tiles = jax.ShapeDtypeStruct((4 * GROUP + 2, block_len, HD), bf16)
    block = jax.ShapeDtypeStruct((block_len, SLOT_W), bf16)
    by_head = jax.ShapeDtypeStruct((KVH, block_len, SLOT_W), bf16)
    small = pltpu.CompilerParams(vmem_limit_bytes=SMALL_BYTES)
    large = pltpu.CompilerParams(vmem_limit_bytes=VMEM_BYTES)

    partners = [(i, i ^ 1) for i in range(group_size)]
    relays = [(i, group_size - 1 - i) for i in range(group_size - group_size // 4, group_size)]
    to_near, to_far = [], []
    for p in range(group_size // 2, group_size - group_size // 4, 2):
        lowest_late = 2 * group_size - 2 - p - reach
        for g in range(2):
            to_near.append((lowest_late + g, p + g))
            to_far.append((lowest_late + 1 - g, p + g))

    half_cols = (2, block_len, HALF_Q)
    row_pairs = jax.ShapeDtypeStruct((2, rows, HD), bf16)
    early, late, near, far = pl.pallas_call(
        blocks_kernel,
        out_shape=(by_head, by_head, block, block),
        in_specs=[SMEM] + [ANY] * 3,
        out_specs=(VMEM,) * 4,
        scratch_shapes=[
            pltpu.VMEM(k.shape, bf16),
            pltpu.VMEM(k.shape, bf16),
            pltpu.VMEM((1, KW), f32),
            pltpu.SemaphoreType.DMA((3,)),
        ],
        compiler_params=large,
        name="blocks",
    )(me, k, v, v_bias[None])
    relayed = lax.ppermute(early, "ctx", relays)
    near = lax.ppermute(near, "ctx", to_near)
    far = lax.ppermute(far, "ctx", to_far)
    swap = pl.pallas_call(
        swap_kernel,
        out_shape=more_tiles,
        in_specs=[SMEM, ANY, ANY, ANY],
        out_specs=VMEM,
        scratch_shapes=[
            pltpu.VMEM(half_cols, bf16),
            pltpu.VMEM(half_cols, bf16),
            pltpu.VMEM(block.shape, bf16),
            pltpu.SemaphoreType.DMA((3,)),
        ],
        compiler_params=large,
        cost_estimate=pl.CostEstimate(
            flops=SWAP_FLOPS, bytes_accessed=2_000_000, transcendentals=0
        ),
        name="swap",
    )(me, q, ct, late)
    other = lax.ppermute(swap, "ctx", partners)
    sent = pl.pallas_call(
        functools.partial(send_kernel, group_size, reach),
        out_shape=jax.ShapeDtypeStruct((group_size, block_len, SLOT_W), bf16),
        in_specs=[SMEM] + [ANY] * 5,
        out_specs=ANY,
        scratch_shapes=[
            pltpu.VMEM((3, KVH, block_len, SLOT_W), bf16),
            pltpu.SemaphoreType.DMA((group_size,)),
            pltpu.SemaphoreType.DMA((3,)),
        ],
        compiler_params=large,
        name="send",
    )(me, early, late, relayed, near, far)
    gathered = lax.all_to_all(sent, "ctx", 0, 0)
    q_rows, d_rows = pl.pallas_call(
        prepare_kernel,
        out_shape=(row_pairs, row_pairs),
        in_specs=[SMEM] + [VMEM] * 4,
        out_specs=(VMEM, VMEM),
        cost_estimate=pl.CostEstimate(
            flops=PREP_FLOPS, bytes_accessed=4_000_000, transcendentals=0
        ),
        compiler_params=small,
        name="prepare",
    )(me, q, ct, other, q_bias[None])

    slot_len = block_len + SUM_ROWS
    mine, back, parts, own, near_grad, far_grad = pl.pallas_call(
        functools.partial(attention_kernel, group_size, reach),
        out_shape=(
            tiles,
            more_tiles,
            jax.ShapeDtypeStruct((group_size, slot_len, SLOT_W), bf16),
            block,
            block,
            block,
        ),
        in_specs=[SMEM, SMEM] + [ANY] * 7,
        out_specs=(ANY,) * 6,
        scratch_shapes=[
            pltpu.VMEM((2, block_len, HD), bf16),
            pltpu.VMEM(tiles.shape, bf16),
            pltpu.VMEM(more_tiles.shape, bf16),
            pltpu.VMEM((group_size + 4, block_len, SLOT_W), bf16),
            pltpu.VMEM((group_size + 4, slot_len, SLOT_W), bf16),
            pltpu.VMEM((window, SLOT_W), bf16),
            pltpu.VMEM(row_pairs.shape, bf16),
            pltpu.VMEM(row_pairs.shape, bf16),
            pltpu.VMEM((window, rows), f32),
            pltpu.VMEM((window, SLOT_W), f32),
            pltpu.VMEM((HD, rows), f32),
            pltpu.VMEM((rows, HD), f32),
            pltpu.VMEM((SUM_ROWS // 2, HD), f32),
            pltpu.SemaphoreType.DMA((7,)),
            pltpu.SemaphoreType.DMA((6,)),
        ],
        compiler_params=large,
        cost_estimate=pl.CostEstimate(
            flops=3_000_000_000, bytes_accessed=10_000_000, transcendentals=2_000_000
        ),
        name="attention",
    )(me, lengths, q_rows, d_rows, other, gathered, late, near, far)

    def back_along(pairs):
        return [(target, source) for source, target in pairs]

    theirs = lax.ppermute(back, "ctx", partners)
    near_grad = lax.ppermute(near_grad, "ctx", back_along(to_near))
    far_grad = lax.ppermute(far_grad, "ctx", back_along(to_far))
    got = lax.all_to_all(parts, "ctx", 0, 0)
    wide = jax.ShapeDtypeStruct(q.shape, bf16)
    narrow = jax.ShapeDtypeStruct(k.shape, bf16)
    attended, q_grad = pl.pallas_call(
        join_kernel,
        out_shape=(wide, wide),
        in_specs=[SMEM, VMEM, VMEM, ANY, ANY],
        out_specs=(VMEM, VMEM),
        cost_estimate=pl.CostEstimate(
            flops=JOIN_FLOPS, bytes_accessed=4_000_000, transcendentals=0
        ),
        compiler_params=small,
        name="join",
    )(me, mine, theirs, near_grad, far_grad)
    relay_total, total, sums = pl.pallas_call(
        functools.partial(total_kernel, group_size, reach),
        out_shape=(
            by_head,
            jax.ShapeDtypeStruct((2, KVH, block_len, SLOT_W), f32),
            jax.ShapeDtypeStruct((SUM_ROWS, HD), f32),
        ),
        in_specs=[SMEM] + [VMEM] * 5 + [ANY],
        out_specs=(VMEM, VMEM, VMEM),
        scratch_shapes=[pltpu.VMEM((3, KVH, block_len, SLOT_W), f32)],
        compiler_params=small,
        name="total",
    )(me, got, near_grad, far_grad, own, theirs, q_grad)
    relay_grad = lax.ppermute(relay_total, "ctx", back_along(relays))
    dp_size = lax.axis_size("dp")
    sums = sums + lax.ppermute(sums, "dp", [(i, i ^ 1) for i in range(dp_size)])
    other_sums = lax.ppermute(sums, "dp", [(i, i ^ 2) for i in range(dp_size)])
    k_grad, v_grad = pl.pallas_call(
        finish_kernel,
        out_shape=(narrow, narrow),
        in_specs=[VMEM, VMEM],
        out_specs=(VMEM, VMEM),
        cost_estimate=pl.CostEstimate(
            flops=FINISH_FLOPS, bytes_accessed=1_000_000, transcendentals=0
        ),
        compiler_params=small,
        name="finish",
    )(total, relay_grad)
    q_sum, v_sum = pl.pallas_call(
        bias_kernel,
        out_shape=(jax.ShapeDtypeStruct((1, HQ), f32), jax.ShapeDtypeStruct((1, KW), f32)),
        in_specs=[VMEM, VMEM, ANY],
        out_specs=(VMEM, VMEM),
        compiler_params=small,
        name="bias",
    )(sums, other_sums, k_grad)
    return (
        attended[None],
        q_grad[None],
        k_grad[None],
        v_grad[None],
        q_sum.reshape(HQ),
        v_sum.reshape(KW),
    )


def solution(mesh):
    placed = (
        P("dp", None, "ctx", None),
        P("dp", None, "ctx", None),
        P("dp", None, "ctx", None),
        P(),
        P(),
        P("dp", None, "ctx", None),
        P("dp", None),
    )
    return jax.shard_map(
        on_device,
        mesh=mesh,
        in_specs=placed,
        out_specs=(
            P("dp", None, "ctx", None),
            P("dp", None, "ctx", None),
            P("dp", None, "ctx", None),
            P("dp", None, "ctx", None),
            P(),
            P(),
        ),
        check_vma=False,
    )
```

time: 113 us -> 99.3 us (0.88)
  waiting for transfers between devices: 63.6 us -> 35.9 us
  starting transfers between devices: 29.9 us -> 37.5 us
  Pallas kernels: 12.9 us -> 17.5 us
  local copies, waits for them, and re-layouts: 3.88 us -> 5.73 us
    ppermute x1, waiting for transfers between devices: 32.1 us -> 0.01 us  [on_device(): other = lax.ppermute(swap, 'ctx', partners)]
    all_to_all x1, waiting for transfers between devices: 29.7 us -> 15.7 us  [on_device(): got = lax.all_to_all(parts, 'ctx', 0, 0)]
    all_to_all x1, waiting for transfers between devices: 0.01 us -> 13.4 us  [on_device(): gathered = lax.all_to_all(sent, 'ctx', 0, 0)]
    ppermute x2 -> x8, starting transfers between devices: 4.17 us -> 13.5 us  [the longest x1 4.91 us: on_device(): other_sums = lax.ppermute(sums, 'dp', [(i, i ^ 2) for i in range(dp_size)])]
    ppermute x2 -> x8, waiting for transfers between devices: 1.8 us -> 6.8 us  [the longest x1 4.68 us: on_device(): relayed = lax.ppermute(early, 'ctx', relays)]
    pallas_call x4 -> x8, Pallas kernels: 11.9 us -> 16.4 us  [the longest x1 9.07 us: on_device(): pl.pallas_call(functools.partial(attention_kernel, group_size, reach), ou...]
    unnamed x12 -> x28, local copies, waits for them, and re-layouts: 2.11 us -> 5.72 us
    all_to_all x1, starting transfers between devices: 13.1 us -> 11.4 us  [on_device(): got = lax.all_to_all(parts, 'ctx', 0, 0)]
  transfers between devices with their start and end apart: 6 -> 12, of which waited for: 4 -> 5; matrix products, arithmetic and copies ran while one was open for 1% -> 0% of each run, Pallas kernels for 2% -> 4%
where the time goes in v4:
time: 99.3 us; the launch traced here: 98.1 us
  starting transfers between devices  37.5 us (38%)
  waiting for transfers between devices  35.9 us (36%)
  Pallas kernels  17.5 us (18%)
  local copies, waits for them, and re-layouts  5.73 us (6%)
    all_to_all x1, waiting for transfers between devices, on_device(): got = lax.all_to_all(parts, 'ctx', 0, 0)  15.7 us
    all_to_all x1, waiting for transfers between devices, on_device(): gathered = lax.all_to_all(sent, 'ctx', 0, 0)  13.4 us
    all_to_all x1, starting transfers between devices, on_device(): got = lax.all_to_all(parts, 'ctx', 0, 0)  11.4 us
    all_to_all x1, starting transfers between devices, on_device(): gathered = lax.all_to_all(sent, 'ctx', 0, 0)  9.56 us
    pallas_call x1, Pallas kernels, on_device(): pl.pallas_call(functools.partial(attention_kernel, group_size, reach), ou...  9.07 us
    unnamed x28, local copies, waits for them, and re-layouts  5.72 us
    ppermute x1, starting transfers between devices, on_device(): other_sums = lax.ppermute(sums, 'dp', [(i, i ^ 2) for i in range(dp_size)])  4.91 us
    ppermute x1, waiting for transfers between devices, on_device(): relayed = lax.ppermute(early, 'ctx', relays)  4.68 us
  transfers between devices with their start and end apart: 12, of which 5 were waited for; matrix products, arithmetic and copies ran while one was open for 0% of the time, Pallas kernels for 4%

profile of v4, /device:TPU:0, one launch (start us, length us, event | category | flops | bytes accessed | tf_op | source)
XLA Modules:
  0.0 98.1 jit_solution(17187299105651844290)
XLA Ops:
  0.6 1.6 %blocks.1 = (bf16[2,64,256]{2,1,0:T(8,128)(2,1)}, bf16[2,64,256]{2,1,0:T(8,128)(2,1)}, bf16[64,256]{1,0:T(8,128)(2,1)}, bf16[64,256]{1,0:T(8,128)(2,1)}) custom-call(s32[1]{0:T(128)} %bitcast.me_ref, bf16[2,64,256]{2,1,0:T(8,128)(2,1)} %bitcast.17, bf16[2,64,256]{2,1,0:T(8,128)(2,1)} %bitcast.18, f32[1,256]{1,0:T(1,128)} %bitcast.19), custom_call_target="tpu_custom_call" | custom-call | tf_op jit(solution)/shard_map/blocks/pallas_call | solution.py:461
  2.2 1.3 %collective-permute-start.1 = (bf16[2,64,256]{2,1,0:T(8,128)(2,1)}, bf16[2,64,256]{2,1,0:T(8,128)(2,1)S(1)}, u32[]{:S(2)}, u32[]{:S(2)}) collective-permute-start(bf16[2,64,256]{2,1,0:T(8,128)(2,1)} %get-tuple-element.30.early_hbm), channel_id=1, source_target_pairs={{96,28},{100,24},{104,20},{108,16},{112,12},{116,8},{120,4},{124,0... | collective-permute-start | bytes 196616 | tf_op jit(solution)/shard_map/ppermute | solution.py:475
  3.5 0.7 collective-permute-start.2
  4.9 1.9 %swap.1 = bf16[30,64,128]{2,1,0:T(8,128)(2,1)} custom-call(s32[1]{0:T(128)} %bitcast.me_ref, bf16[2,64,1792]{2,1,0:T(8,128)(2,1)} %bitcast.12, bf16[2,64,1792]{2,1,0:T(8,128)(2,1)} %bitcast.14, bf16[2,64,256]{2,1,0:T(8,128)(2,1)} %get-tuple-element.27.late_hbm), custom_call_target="tpu_custom_call" | custom-call | flops 1000000 | bytes 2000000 | tf_op jit(solution)/shard_map/swap/pallas_call | solution.py:478
  6.8 1.7 %collective-permute-start = (bf16[30,64,128]{2,1,0:T(8,128)(2,1)}, bf16[30,64,128]{2,1,0:T(8,128)(2,1)S(1)}, u32[]{:S(2)}, u32[]{:S(2)}) collective-permute-start(bf16[30,64,128]{2,1,0:T(8,128)(2,1)} %swap.1), channel_id=1, source_target_pairs={{0,4},{4,0},{8,12},{12,8},{16,20},{20,16},{24,28},{28,24},{32,36},... | collective-permute-start | bytes 1474568 | tf_op jit(solution)/shard_map/ppermute | solution.py:495
  8.5 4.7 %collective-permute-done.1.relay_hbm = bf16[2,64,256]{2,1,0:T(8,128)(2,1)S(1)} collective-permute-done((bf16[2,64,256]{2,1,0:T(8,128)(2,1)}, bf16[2,64,256]{2,1,0:T(8,128)(2,1)S(1)}, u32[]{:S(2)}, u32[]{:S(2)}) %collective-permute-start.1) | collective-permute-done | bytes 65568 | tf_op jit(solution)/shard_map/ppermute | solution.py:475
  13.8 2.2 %send.1 = bf16[32,64,256]{2,1,0:T(8,128)(2,1)} custom-call(s32[1]{0:T(128)} %bitcast.me_ref, bf16[2,64,256]{2,1,0:T(8,128)(2,1)} %get-tuple-element.30.early_hbm, bf16[2,64,256]{2,1,0:T(8,128)(2,1)} %get-tuple-element.27.late_hbm, bf16[2,64,256]{2,1,0:T(8,128)(2,1)} %copy-done.10, bf16[64,256]{1,0:T(8,128)(2,1)} %copy-done.11, bf16[64,256]{1,0:T(8,128)(2,1)} %copy-done.12), custom_call_target="tpu_custom_call" | custom-call | tf_op jit(solution)/shard_map/send/pallas_call | solution.py:496
  16.0 9.6 %all-to-all-start = ((bf16[32,64,256]{2,1,0:T(8,128)(2,1)}), bf16[32,64,256]{2,1,0:T(8,128)(2,1)S(1)}, u32[]{:S(2)}, u32[]{:S(2)}) async-start(bf16[32,64,256]{2,1,0:T(8,128)(2,1)} %send.1), calls=%async_computation | async-start | bytes 2097152 | tf_op jit(solution)/shard_map/all_to_all | solution.py:509
  26.5 0.8 copy-done.7
  27.2 0.8 copy-done.8
  28.0 13.4 %all-to-all-done.kv_hbm = bf16[32,64,256]{2,1,0:T(8,128)(2,1)S(1)} async-done(((bf16[32,64,256]{2,1,0:T(8,128)(2,1)}), bf16[32,64,256]{2,1,0:T(8,128)(2,1)S(1)}, u32[]{:S(2)}, u32[]{:S(2)}) %all-to-all-start) | async-done | bytes 1048608 | tf_op jit(solution)/shard_map/all_to_all | solution.py:509
  41.4 1.0 %copy-done.9 = bf16[32,64,256]{2,1,0:T(8,128)(2,1)} copy-done((bf16[32,64,256]{2,1,0:T(8,128)(2,1)}, bf16[32,64,256]{2,1,0:T(8,128)(2,1)S(1)}, u32[]{:S(2)}) %copy-start.9) | copy-done | bytes 1048600
  42.4 9.1 %attention.1 = (bf16[28,64,128]{2,1,0:T(8,128)(2,1)}, bf16[30,64,128]{2,1,0:T(8,128)(2,1)}, bf16[32,80,256]{2,1,0:T(8,128)(2,1)}, bf16[64,256]{1,0:T(8,128)(2,1)...) custom-call(s32[1]{0:T(128)} %bitcast.me_ref, s32[1,16]{1,0:T(1,128)} %len_ref.1, bf16[2,896,128]{2,1,0:T(8,128)(2,1)} %copy-done.7, ...), custom_call_target="tpu_custom_call" | custom-call | flops 3000000000 | bytes 10000000 | tf_op jit(solution)/shard_map/attention/pallas_call | solution.py:523
  51.5 1.3 %collective-permute-start.4 = (bf16[30,64,128]{2,1,0:T(8,128)(2,1)}, bf16[30,64,128]{2,1,0:T(8,128)(2,1)S(1)}, u32[]{:S(2)}, u32[]{:S(2)}) collective-permute-start(bf16[30,64,128]{2,1,0:T(8,128)(2,1)} %get-tuple-element.34), channel_id=1, source_target_pairs={{0,4},{4,0},{8,12},{12,8},{16,20},{20,16},{24,28},{28,24},{32,36},... | collective-permute-start | bytes 1474568 | tf_op jit(solution)/shard_map/ppermute | solution.py:562
  54.2 11.4 %all-to-all-start.1 = ((bf16[32,80,256]{2,1,0:T(8,128)(2,1)}), bf16[32,80,256]{2,1,0:T(8,128)(2,1)S(1)}, u32[]{:S(2)}, u32[]{:S(2)}) async-start(bf16[32,80,256]{2,1,0:T(8,128)(2,1)} %get-tuple-element.39), calls=%async_computation.1 | async-start | bytes 2621440 | tf_op jit(solution)/shard_map/all_to_all | solution.py:565
  65.6 1.1 %join.1 = (bf16[2,64,1792]{2,1,0:T(8,128)(2,1)}, bf16[2,64,1792]{2,1,0:T(8,128)(2,1)}) custom-call(s32[1]{0:T(128)} %bitcast.me_ref, bf16[28,64,128]{2,1,0:T(8,128)(2,1)S(1)} %copy-done.6, bf16[30,64,128]{2,1,0:T(8,128)(2,1)S(1)} %collective-permute-done.4.theirs_ref, bf16[64,256]{1,0:T(8,128)(2,1)S(1)} %collective-permute-done.5.near_hbm.near_ref, ...), custom_call_target="tpu_custom_call" | custom-call | flops 40000000000 | bytes 4000000 | tf_op jit(solution)/shard_map/join/pallas_call | solution.py:568
  66.7 15.7 %all-to-all-done.1.got_ref = bf16[32,80,256]{2,1,0:T(8,128)(2,1)S(1)} async-done(((bf16[32,80,256]{2,1,0:T(8,128)(2,1)}), bf16[32,80,256]{2,1,0:T(8,128)(2,1)S(1)}, u32[]{:S(2)}, u32[]{:S(2)}) %all-to-all-start.1) | async-done | bytes 1310752 | tf_op jit(solution)/shard_map/all_to_all | solution.py:565
  82.4 1.0 %copy-done = bf16[2,64,1792]{2,1,0:T(8,128)(2,1)S(1)} copy-done((bf16[2,64,1792]{2,1,0:T(8,128)(2,1)S(1)}, bf16[2,64,1792]{2,1,0:T(8,128)(2,1)}, u32[]{:S(2)}) %copy-start) | copy-done | bytes 458776
  83.7 4.6 %collective-permute-start.7 = (bf16[2,64,256]{2,1,0:T(8,128)(2,1)S(1)}, bf16[2,64,256]{2,1,0:T(8,128)(2,1)S(1)}, u32[]{:S(2)}, u32[]{:S(2)}) collective-permute-start(bf16[2,64,256]{2,1,0:T(8,128)(2,1)S(1)} %get-tuple-element.42), channel_id=1, source_target_pairs={{28,96},{24,100},{20,104},{16,108},{12,112},{8,116},{4,120},{0,124... | collective-permute-start | bytes 196616 | tf_op jit(solution)/shard_map/ppermute | solution.py:592
  88.4 1.2 %collective-permute-done.8 = f32[16,128]{1,0:T(8,128)S(1)} collective-permute-done((f32[16,128]{1,0:T(8,128)S(1)}, f32[16,128]{1,0:T(8,128)S(1)}, u32[]{:S(2)}, u32[]{:S(2)}) %collective-permute-start.8) | collective-permute-done | bytes 8224 | tf_op jit(solution)/shard_map/ppermute | solution.py:594
  89.6 4.9 %collective-permute-start.9 = (f32[16,128]{1,0:T(8,128)S(1)}, f32[16,128]{1,0:T(8,128)S(1)}, u32[]{:S(2)}, u32[]{:S(2)}) collective-permute-start(f32[16,128]{1,0:T(8,128)S(1)} %add.3.a_ref), channel_id=1, source_target_pairs={{0,2},{1,3},{2,0},{3,1},{4,6},{5,7},{6,4},{7,5},{8,10},{9,11},{10,... | collective-permute-start | bytes 24584 | tf_op jit(solution)/shard_map/ppermute | solution.py:595
  94.5 0.7 finish.1
  95.2 1.0 collective-permute-done.9.b_ref
  96.1 0.8 copy-done.3
  (40 shorter events, 5.0 us)
Async XLA Ops:
  2.2 10.9 %collective-permute-start.1 = (bf16[2,64,256]{2,1,0:T(8,128)(2,1)}, bf16[2,64,256]{2,1,0:T(8,128)(2,1)S(1)}, u32[]{:S(2)}, u32[]{:S(2)}) collective-permute-start(bf16[2,64,256]{2,1,0:T(8,128)(2,1)} %get-tuple-element.30.early_hbm), channel_id=1, source_target_pairs={{96,28},{100,24},{104,20},{108,16},{112,12},{116,8},{120,4},{124,0... | collective-permute-start | bytes 196616 | tf_op jit(solution)/shard_map/ppermute | solution.py:475
  3.5 4.9 %collective-permute-start.2 = (bf16[64,256]{1,0:T(8,128)(2,1)}, bf16[64,256]{1,0:T(8,128)(2,1)S(1)}, u32[]{:S(2)}, u32[]{:S(2)}) collective-permute-start(bf16[64,256]{1,0:T(8,128)(2,1)} %get-tuple-element.31), channel_id=1, source_target_pairs={{120,64},{124,68},{112,72},{116,76},{104,80},{108,84},{96,88},{100... | collective-permute-start | bytes 98312 | tf_op jit(solution)/shard_map/ppermute | solution.py:476
  4.2 4.3 %collective-permute-start.3 = (bf16[64,256]{1,0:T(8,128)(2,1)}, bf16[64,256]{1,0:T(8,128)(2,1)S(1)}, u32[]{:S(2)}, u32[]{:S(2)}) collective-permute-start(bf16[64,256]{1,0:T(8,128)(2,1)} %get-tuple-element.32), channel_id=1, source_target_pairs={{124,64},{120,68},{116,72},{112,76},{108,80},{104,84},{100,88},{96... | collective-permute-start | bytes 98312 | tf_op jit(solution)/shard_map/ppermute | solution.py:477
  6.8 18.8 %collective-permute-start = (bf16[30,64,128]{2,1,0:T(8,128)(2,1)}, bf16[30,64,128]{2,1,0:T(8,128)(2,1)S(1)}, u32[]{:S(2)}, u32[]{:S(2)}) collective-permute-start(bf16[30,64,128]{2,1,0:T(8,128)(2,1)} %swap.1), channel_id=1, source_target_pairs={{0,4},{4,0},{8,12},{12,8},{16,20},{20,16},{24,28},{28,24},{32,36},... | collective-permute-start | bytes 1474568 | tf_op jit(solution)/shard_map/ppermute | solution.py:495
  8.5 4.7 %copy-start.11 = (bf16[64,256]{1,0:T(8,128)(2,1)}, bf16[64,256]{1,0:T(8,128)(2,1)S(1)}, u32[]{:S(2)}) copy-start(bf16[64,256]{1,0:T(8,128)(2,1)S(1)} %collective-permute-done.2.near_hbm) | copy-start | bytes 98308
  8.5 4.7 %copy-start.12 = (bf16[64,256]{1,0:T(8,128)(2,1)}, bf16[64,256]{1,0:T(8,128)(2,1)S(1)}, u32[]{:S(2)}) copy-start(bf16[64,256]{1,0:T(8,128)(2,1)S(1)} %collective-permute-done.3.far_hbm) | copy-start | bytes 98308
  16.0 9.6 %copy-start.13 = (f32[1792]{0:T(1024)S(1)}, f32[1792]{0:T(1024)}, u32[]{:S(2)}) copy-start(f32[1792]{0:T(1024)} %param.10) | copy-start | bytes 21508
  16.0 9.6 %copy-start.1 = (bf16[1,2,64,1792]{3,2,1,0:T(8,128)(2,1)S(1)}, bf16[1,2,64,1792]{3,2,1,0:T(8,128)(2,1)}, u32[]{:S(2)}) copy-start(bf16[1,2,64,1792]{3,2,1,0:T(8,128)(2,1)} %param.7) | copy-start | bytes 1376260
  16.0 9.6 %copy-start.2 = (bf16[1,2,64,1792]{3,2,1,0:T(8,128)(2,1)S(1)}, bf16[1,2,64,1792]{3,2,1,0:T(8,128)(2,1)}, u32[]{:S(2)}) copy-start(bf16[1,2,64,1792]{3,2,1,0:T(8,128)(2,1)} %param.12) | copy-start | bytes 1376260
  16.0 25.4 %all-to-all-start = ((bf16[32,64,256]{2,1,0:T(8,128)(2,1)}), bf16[32,64,256]{2,1,0:T(8,128)(2,1)S(1)}, u32[]{:S(2)}, u32[]{:S(2)}) async-start(bf16[32,64,256]{2,1,0:T(8,128)(2,1)} %send.1), calls=%async_computation | async-start | bytes 2097152 | tf_op jit(solution)/shard_map/all_to_all | solution.py:509
  25.7 0.8 copy-start.5
  26.5 0.8 copy-start.7
  41.4 1.0 %copy-start.9 = (bf16[32,64,256]{2,1,0:T(8,128)(2,1)}, bf16[32,64,256]{2,1,0:T(8,128)(2,1)S(1)}, u32[]{:S(2)}) copy-start(bf16[32,64,256]{2,1,0:T(8,128)(2,1)S(1)} %all-to-all-done.kv_hbm) | copy-start | bytes 3145732
  51.5 14.1 %collective-permute-start.4 = (bf16[30,64,128]{2,1,0:T(8,128)(2,1)}, bf16[30,64,128]{2,1,0:T(8,128)(2,1)S(1)}, u32[]{:S(2)}, u32[]{:S(2)}) collective-permute-start(bf16[30,64,128]{2,1,0:T(8,128)(2,1)} %get-tuple-element.34), channel_id=1, source_target_pairs={{0,4},{4,0},{8,12},{12,8},{16,20},{20,16},{24,28},{28,24},{32,36},... | collective-permute-start | bytes 1474568 | tf_op jit(solution)/shard_map/ppermute | solution.py:562
  52.8 12.7 %collective-permute-start.5 = (bf16[64,256]{1,0:T(8,128)(2,1)}, bf16[64,256]{1,0:T(8,128)(2,1)S(1)}, u32[]{:S(2)}, u32[]{:S(2)}) collective-permute-start(bf16[64,256]{1,0:T(8,128)(2,1)} %get-tuple-element.35), channel_id=1, source_target_pairs={{64,120},{68,124},{72,112},{76,116},{80,104},{84,108},{88,96},{92,... | collective-permute-start | bytes 98312 | tf_op jit(solution)/shard_map/ppermute | solution.py:563
  53.5 12.1 %collective-permute-start.6 = (bf16[64,256]{1,0:T(8,128)(2,1)}, bf16[64,256]{1,0:T(8,128)(2,1)S(1)}, u32[]{:S(2)}, u32[]{:S(2)}) collective-permute-start(bf16[64,256]{1,0:T(8,128)(2,1)} %get-tuple-element.36), channel_id=1, source_target_pairs={{64,124},{68,120},{72,116},{76,112},{80,108},{84,104},{88,100},{92... | collective-permute-start | bytes 98312 | tf_op jit(solution)/shard_map/ppermute | solution.py:564
  54.2 11.4 %copy-start.6 = (bf16[28,64,128]{2,1,0:T(8,128)(2,1)S(1)}, bf16[28,64,128]{2,1,0:T(8,128)(2,1)}, u32[]{:S(2)}) copy-start(bf16[28,64,128]{2,1,0:T(8,128)(2,1)} %get-tuple-element.33.mine_ref) | copy-start | bytes 1376260
  54.2 28.2 %all-to-all-start.1 = ((bf16[32,80,256]{2,1,0:T(8,128)(2,1)}), bf16[32,80,256]{2,1,0:T(8,128)(2,1)S(1)}, u32[]{:S(2)}, u32[]{:S(2)}) async-start(bf16[32,80,256]{2,1,0:T(8,128)(2,1)} %get-tuple-element.39), calls=%async_computation.1 | async-start | bytes 2621440 | tf_op jit(solution)/shard_map/all_to_all | solution.py:565
  65.6 16.8 %copy-start.4 = (bf16[64,256]{1,0:T(8,128)(2,1)S(1)}, bf16[64,256]{1,0:T(8,128)(2,1)}, u32[]{:S(2)}) copy-start(bf16[64,256]{1,0:T(8,128)(2,1)} %get-tuple-element.40.own_ref) | copy-start | bytes 98308
  82.4 1.0 %copy-start = (bf16[2,64,1792]{2,1,0:T(8,128)(2,1)S(1)}, bf16[2,64,1792]{2,1,0:T(8,128)(2,1)}, u32[]{:S(2)}) copy-start(bf16[2,64,1792]{2,1,0:T(8,128)(2,1)} %get-tuple-element.38.joined_hbm) | copy-start | bytes 1376260
  83.7 10.8 %collective-permute-start.7 = (bf16[2,64,256]{2,1,0:T(8,128)(2,1)S(1)}, bf16[2,64,256]{2,1,0:T(8,128)(2,1)S(1)}, u32[]{:S(2)}, u32[]{:S(2)}) collective-permute-start(bf16[2,64,256]{2,1,0:T(8,128)(2,1)S(1)} %get-tuple-element.42), channel_id=1, source_target_pairs={{28,96},{24,100},{20,104},{16,108},{12,112},{8,116},{4,120},{0,124... | collective-permute-start | bytes 196616 | tf_op jit(solution)/shard_map/ppermute | solution.py:592
  88.3 1.3 %collective-permute-start.8 = (f32[16,128]{1,0:T(8,128)S(1)}, f32[16,128]{1,0:T(8,128)S(1)}, u32[]{:S(2)}, u32[]{:S(2)}) collective-permute-start(f32[16,128]{1,0:T(8,128)S(1)} %get-tuple-element.45), channel_id=1, source_target_pairs={{0,1},{1,0},{2,3},{3,2},{4,5},{5,4},{6,7},{7,6},{8,9},{9,8},{10,11... | collective-permute-start | bytes 24584 | tf_op jit(solution)/shard_map/ppermute | solution.py:594
  89.6 6.5 %collective-permute-start.9 = (f32[16,128]{1,0:T(8,128)S(1)}, f32[16,128]{1,0:T(8,128)S(1)}, u32[]{:S(2)}, u32[]{:S(2)}) collective-permute-start(f32[16,128]{1,0:T(8,128)S(1)} %add.3.a_ref), channel_id=1, source_target_pairs={{0,2},{1,3},{2,0},{3,1},{4,6},{5,7},{6,4},{7,5},{8,10},{9,11},{10,... | collective-permute-start | bytes 24584 | tf_op jit(solution)/shard_map/ppermute | solution.py:595
  96.1 0.8 copy-start.3
  (2 other events, 1.4 us)

commit v5 on v4

--- a/solution.py
+++ b/solution.py
@@ -23,6 +23,7 @@
 SWAP_FLOPS = 1_000_000
 JOIN_FLOPS = 40_000_000_000
 FINISH_FLOPS = 1_000_000
+BIAS_FLOPS = 10_000_000_000
 VMEM_BYTES = 59 * 1024 * 1024
 SMALL_BYTES = 16 * 1024 * 1024
 BLOCKS_PER_CHUNK = 4
@@ -92,7 +93,7 @@
 
 
 def prepare_kernel(
-    me_ref, q_ref, ct_ref, other_ref, qb_ref, q_rows, d_rows
+    me_ref, q_ref, ct_ref, other_ref, qb_ref, q_rows, d_rows, d_cols
 ):
     block_len = q_ref.shape[1]
     pair_len = 2 * block_len
@@ -113,20 +114,16 @@
             ).astype(jnp.bfloat16)
             d_rows[h, own_rows, :] = ct_ref[h, :, own_lanes]
             d_rows[h, partner_rows, :] = other_ref[(2 + h) * GROUP + t]
+        d_cols[h] = jnp.transpose(d_rows[h].astype(jnp.float32)).astype(jnp.bfloat16)
 
 
 def send_kernel(
-    group_size, reach, me_ref, early_hbm, late_hbm, relay_hbm, near_hbm, far_hbm, send_ref, all_ref, sem, load_sems
+    group_size, reach, me_ref, early_ref, late_ref, relay_ref, near_hbm, far_hbm, send_ref, all_ref, sem
 ):
     me = me_ref[0]
-    loads = [
-        pltpu.make_async_copy(source, all_ref.at[i], load_sems.at[i])
-        for i, source in enumerate((early_hbm, late_hbm, relay_hbm))
-    ]
-    for load in loads:
-        load.start()
-    for load in loads:
-        load.wait()
+    all_ref[0] = early_ref[...]
+    all_ref[1] = late_ref[...]
+    all_ref[2] = relay_ref[...]
     copies = []
     for d in range(group_size):
         kind = route(me, jnp.int32(d), group_size, reach)
@@ -144,6 +141,7 @@
     len_ref,
     q_hbm,
     d_hbm,
+    dt_hbm,
     other_hbm,
     kv_hbm,
     late_hbm,
@@ -152,7 +150,6 @@
     mine_hbm,
     back_hbm,
     parts_hbm,
-    own_hbm,
     near_grad_hbm,
     far_grad_hbm,
     other_ref,
@@ -163,6 +160,7 @@
     win_ref,
     q_both,
     d_both,
+    dt_both,
     p_ref,
     grad_ref,
     acc_ref,
@@ -191,6 +189,7 @@
                 (other_hbm.at[4 * GROUP :], other_ref),
                 (q_hbm, q_both),
                 (d_hbm, d_both),
+                (dt_hbm, dt_both),
                 (kv_hbm, all_ref.at[:group_size]),
                 (late_hbm.at[head], all_ref.at[own_late]),
                 (near_hbm, all_ref.at[near]),
@@ -276,9 +275,7 @@
         total = lax.fori_loop(0, n_chunks, out_step, jnp.zeros((1, rows), jnp.float32))
         inverse = 1.0 / total
         summed = acc_ref[...] * inverse
-        delta = jnp.sum(
-            summed * jnp.transpose(d_rows[...].astype(jnp.float32)), axis=0, keepdims=True
-        )
+        delta = jnp.sum(summed * dt_both[h].astype(jnp.float32), axis=0, keepdims=True)
         row_ref[...] = jnp.transpose(summed)
         for t in range(GROUP):
             mine_ref[h * GROUP + t] = row_ref[
@@ -341,8 +338,9 @@
     ).astype(jnp.bfloat16)
     for d in range(group_size):
         stage_ref[d, block_len:, :] = pieces
-    back_ref[4 * GROUP] = stage_ref[other_late, :block_len, :HD]
-    back_ref[4 * GROUP + 1] = stage_ref[other_late, :block_len, HD:]
+    for ref, late in ((mine_ref, own_late), (back_ref, other_late)):
+        ref[4 * GROUP] = stage_ref[late, :block_len, :HD]
+        ref[4 * GROUP + 1] = stage_ref[late, :block_len, HD:]
     stores = [
         pltpu.make_async_copy(source, into, out_sems.at[i])
         for i, (source, into) in enumerate(
@@ -352,7 +350,6 @@
                 (stage_ref.at[far, :block_len], far_grad_hbm),
                 (stage_ref.at[:group_size], parts_hbm),
                 (mine_ref, mine_hbm),
-                (stage_ref.at[own_late, :block_len], own_hbm),
             )
         )
     ]
@@ -362,7 +359,9 @@
         store.wait()
 
 
-def join_kernel(me_ref, mine_ref, theirs_ref, near_hbm, far_hbm, att_ref, qg_ref):
+def join_kernel(
+    me_ref, mine_ref, theirs_ref, near_hbm, far_hbm, att_ref, qg_ref, own_ref, theirs_late_ref
+):
     head = me_ref[0] % 2
     for i, ref in enumerate((att_ref, qg_ref)):
         for h in range(2):
@@ -370,6 +369,9 @@
                 tile = (2 * i + h) * GROUP + t
                 ref[h, :, lanes(head * HALF_Q + t * HD, HD)] = mine_ref[tile]
                 ref[h, :, lanes((1 - head) * HALF_Q + t * HD, HD)] = theirs_ref[tile]
+    for ref, late_ref in ((mine_ref, own_ref), (theirs_ref, theirs_late_ref)):
+        late_ref[:, :HD] = ref[4 * GROUP]
+        late_ref[:, HD:] = ref[4 * GROUP + 1]
 
 
 def total_kernel(
@@ -381,7 +383,6 @@
     far_ref,
     own_ref,
     theirs_ref,
-    joined_hbm,
     relay_ref,
     total_ref,
     sum_ref,
@@ -395,8 +396,7 @@
     acc_ref[0, head] = near_ref[...].astype(jnp.float32)
     acc_ref[0, 1 - head] = far_ref[...].astype(jnp.float32)
     acc_ref[1, head] = own_ref[...].astype(jnp.float32)
-    acc_ref[1, 1 - head, :, :HD] = theirs_ref[4 * GROUP].astype(jnp.float32)
-    acc_ref[1, 1 - head, :, HD:] = theirs_ref[4 * GROUP + 1].astype(jnp.float32)
+    acc_ref[1, 1 - head] = theirs_ref[...].astype(jnp.float32)
     for d in range(group_size):
         kind = route(me, jnp.int32(d), group_size, reach)
         acc_ref[kind, d % KVH] += got_ref[d, :block_len, :].astype(jnp.float32)
@@ -421,8 +421,14 @@
             vg_ref[h, :, cols] = total[:, HD:]
 
 
-def bias_kernel(a_ref, b_ref, finished_hbm, q_sum_ref, v_sum_ref):
-    total = a_ref[...] + b_ref[...]
+def bias_kernel(dp_ref, own_ref, *refs):
+    *others, q_sum_ref, v_sum_ref, all_ref = refs
+    me = dp_ref[0]
+    for step, ref in enumerate((own_ref, *others)):
+        all_ref[me ^ step] = ref[...]
+    total = all_ref[0]
+    for i in range(1, all_ref.shape[0]):
+        total = total + all_ref[i]
     half = SUM_ROWS // 2
     for g in range(KVH):
         for t in range(GROUP):
@@ -440,7 +446,6 @@
     rows = GROUP * 2 * block_len
     window = -(-(reach + 2) // BLOCKS_PER_CHUNK) * BLOCKS_PER_CHUNK * block_len
     bf16, f32 = jnp.bfloat16, jnp.float32
-    tiles = jax.ShapeDtypeStruct((4 * GROUP, block_len, HD), bf16)
     more_tiles = jax.ShapeDtypeStruct((4 * GROUP + 2, block_len, HD), bf16)
     block = jax.ShapeDtypeStruct((block_len, SLOT_W), bf16)
     by_head = jax.ShapeDtypeStruct((KVH, block_len, SLOT_W), bf16)
@@ -496,22 +501,21 @@
     sent = pl.pallas_call(
         functools.partial(send_kernel, group_size, reach),
         out_shape=jax.ShapeDtypeStruct((group_size, block_len, SLOT_W), bf16),
-        in_specs=[SMEM] + [ANY] * 5,
+        in_specs=[SMEM] + [VMEM] * 3 + [ANY] * 2,
         out_specs=ANY,
         scratch_shapes=[
             pltpu.VMEM((3, KVH, block_len, SLOT_W), bf16),
             pltpu.SemaphoreType.DMA((group_size,)),
-            pltpu.SemaphoreType.DMA((3,)),
         ],
-        compiler_params=large,
+        compiler_params=small,
         name="send",
     )(me, early, late, relayed, near, far)
     gathered = lax.all_to_all(sent, "ctx", 0, 0)
-    q_rows, d_rows = pl.pallas_call(
+    q_rows, d_rows, d_cols = pl.pallas_call(
         prepare_kernel,
-        out_shape=(row_pairs, row_pairs),
+        out_shape=(row_pairs, row_pairs, jax.ShapeDtypeStruct((2, HD, rows), bf16)),
         in_specs=[SMEM] + [VMEM] * 4,
-        out_specs=(VMEM, VMEM),
+        out_specs=(VMEM,) * 3,
         cost_estimate=pl.CostEstimate(
             flops=PREP_FLOPS, bytes_accessed=4_000_000, transcendentals=0
         ),
@@ -520,41 +524,41 @@
     )(me, q, ct, other, q_bias[None])
 
     slot_len = block_len + SUM_ROWS
-    mine, back, parts, own, near_grad, far_grad = pl.pallas_call(
+    mine, back, parts, near_grad, far_grad = pl.pallas_call(
         functools.partial(attention_kernel, group_size, reach),
         out_shape=(
-            tiles,
+            more_tiles,
             more_tiles,
             jax.ShapeDtypeStruct((group_size, slot_len, SLOT_W), bf16),
             block,
             block,
-            block,
-        ),
-        in_specs=[SMEM, SMEM] + [ANY] * 7,
-        out_specs=(ANY,) * 6,
+        ),
+        in_specs=[SMEM, SMEM] + [ANY] * 8,
+        out_specs=(ANY,) * 5,
         scratch_shapes=[
             pltpu.VMEM((2, block_len, HD), bf16),
-            pltpu.VMEM(tiles.shape, bf16),
+            pltpu.VMEM(more_tiles.shape, bf16),
             pltpu.VMEM(more_tiles.shape, bf16),
             pltpu.VMEM((group_size + 4, block_len, SLOT_W), bf16),
             pltpu.VMEM((group_size + 4, slot_len, SLOT_W), bf16),
             pltpu.VMEM((window, SLOT_W), bf16),
             pltpu.VMEM(row_pairs.shape, bf16),
             pltpu.VMEM(row_pairs.shape, bf16),
+            pltpu.VMEM((2, HD, rows), bf16),
             pltpu.VMEM((window, rows), f32),
             pltpu.VMEM((window, SLOT_W), f32),
             pltpu.VMEM((HD, rows), f32),
             pltpu.VMEM((rows, HD), f32),
             pltpu.VMEM((SUM_ROWS // 2, HD), f32),
-            pltpu.SemaphoreType.DMA((7,)),
-            pltpu.SemaphoreType.DMA((6,)),
+            pltpu.SemaphoreType.DMA((8,)),
+            pltpu.SemaphoreType.DMA((5,)),
         ],
         compiler_params=large,
         cost_estimate=pl.CostEstimate(
             flops=3_000_000_000, bytes_accessed=10_000_000, transcendentals=2_000_000
         ),
         name="attention",
-    )(me, lengths, q_rows, d_rows, other, gathered, late, near, far)
+    )(me, lengths, q_rows, d_rows, d_cols, other, gathered, late, near, far)
 
     def back_along(pairs):
         return [(target, source) for source, target in pairs]
@@ -565,11 +569,11 @@
     got = lax.all_to_all(parts, "ctx", 0, 0)
     wide = jax.ShapeDtypeStruct(q.shape, bf16)
     narrow = jax.ShapeDtypeStruct(k.shape, bf16)
-    attended, q_grad = pl.pallas_call(
+    attended, q_grad, own, theirs_late = pl.pallas_call(
         join_kernel,
-        out_shape=(wide, wide),
+        out_shape=(wide, wide, block, block),
         in_specs=[SMEM, VMEM, VMEM, ANY, ANY],
-        out_specs=(VMEM, VMEM),
+        out_specs=(VMEM,) * 4,
         cost_estimate=pl.CostEstimate(
             flops=JOIN_FLOPS, bytes_accessed=4_000_000, transcendentals=0
         ),
@@ -583,16 +587,19 @@
             jax.ShapeDtypeStruct((2, KVH, block_len, SLOT_W), f32),
             jax.ShapeDtypeStruct((SUM_ROWS, HD), f32),
         ),
-        in_specs=[SMEM] + [VMEM] * 5 + [ANY],
+        in_specs=[SMEM] + [VMEM] * 5,
         out_specs=(VMEM, VMEM, VMEM),
         scratch_shapes=[pltpu.VMEM((3, KVH, block_len, SLOT_W), f32)],
         compiler_params=small,
         name="total",
-    )(me, got, near_grad, far_grad, own, theirs, q_grad)
+    )(me, got, near_grad, far_grad, own, theirs_late)
     relay_grad = lax.ppermute(relay_total, "ctx", back_along(relays))
     dp_size = lax.axis_size("dp")
-    sums = sums + lax.ppermute(sums, "dp", [(i, i ^ 1) for i in range(dp_size)])
-    other_sums = lax.ppermute(sums, "dp", [(i, i ^ 2) for i in range(dp_size)])
+    dp_me = lax.axis_index("dp").astype(jnp.int32)[None]
+    other_sums = [
+        lax.ppermute(sums, "dp", [(i, i ^ step) for i in range(dp_size)])
+        for step in range(1, dp_size)
+    ]
     k_grad, v_grad = pl.pallas_call(
         finish_kernel,
         out_shape=(narrow, narrow),
@@ -607,11 +614,15 @@
     q_sum, v_sum = pl.pallas_call(
         bias_kernel,
         out_shape=(jax.ShapeDtypeStruct((1, HQ), f32), jax.ShapeDtypeStruct((1, KW), f32)),
-        in_specs=[VMEM, VMEM, ANY],
+        in_specs=[SMEM] + [VMEM] * dp_size,
         out_specs=(VMEM, VMEM),
+        scratch_shapes=[pltpu.VMEM((dp_size, SUM_ROWS, HD), f32)],
+        cost_estimate=pl.CostEstimate(
+            flops=BIAS_FLOPS, bytes_accessed=100_000, transcendentals=0
+        ),
         compiler_params=small,
         name="bias",
-    )(sums, other_sums, k_grad)
+    )(dp_me, sums, *other_sums)
     return (
         attended[None],
         q_grad[None],

time: 99.3 us -> 95.9 us (0.966)
  the two profiles are of different devices: /device:TPU:0 before, /device:TPU:24 now
where the time goes in v5:
time: 95.9 us; the launch traced here: 95.8 us
  starting transfers between devices  36.8 us (38%)
  waiting for transfers between devices  34 us (35%)
  Pallas kernels  19.7 us (21%)
  local copies, waits for them, and re-layouts  3.83 us (4%)
    all_to_all x1, waiting for transfers between devices, on_device(): got = lax.all_to_all(parts, 'ctx', 0, 0)  13.8 us
    pallas_call x1, Pallas kernels, on_device(): pl.pallas_call(functools.partial(attention_kernel, group_size, reach), ou...  11.9 us
    all_to_all x1, starting transfers between devices, on_device(): got = lax.all_to_all(parts, 'ctx', 0, 0)  10.5 us
    all_to_all x1, starting transfers between devices, on_device(): gathered = lax.all_to_all(sent, 'ctx', 0, 0)  8.76 us
    all_to_all x1, waiting for transfers between devices, on_device(): gathered = lax.all_to_all(sent, 'ctx', 0, 0)  7.71 us
    ppermute x1, waiting for transfers between devices, on_device(): relay_grad = lax.ppermute(relay_total, 'ctx', back_along(relays))  7.28 us
    ppermute x1, starting transfers between devices, on_device(): relayed = lax.ppermute(early, 'ctx', relays)  5.81 us
    unnamed x26, local copies, waits for them, and re-layouts  3.82 us
  transfers between devices with their start and end apart: 13, of which 6 were waited for; matrix products, arithmetic and copies ran while one was open for 1% of the time, Pallas kernels for 4%

profile of v5, /device:TPU:24, one launch (start us, length us, event | category | flops | bytes accessed | tf_op | source)
XLA Modules:
  0.0 95.8 jit_solution(9771176315832099726)
XLA Ops:
  0.6 1.6 %blocks.1 = (bf16[2,64,256]{2,1,0:T(8,128)(2,1)}, bf16[2,64,256]{2,1,0:T(8,128)(2,1)}, bf16[64,256]{1,0:T(8,128)(2,1)}, bf16[64,256]{1,0:T(8,128)(2,1)}) custom-call(s32[1]{0:T(128)} %bitcast.me_ref, bf16[2,64,256]{2,1,0:T(8,128)(2,1)} %bitcast.16, bf16[2,64,256]{2,1,0:T(8,128)(2,1)} %bitcast.17, f32[1,256]{1,0:T(1,128)} %bitcast.18), custom_call_target="tpu_custom_call" | custom-call | tf_op jit(solution)/shard_map/blocks/pallas_call | solution.py:466
  2.3 5.8 %collective-permute-start.1 = (bf16[2,64,256]{2,1,0:T(8,128)(2,1)}, bf16[2,64,256]{2,1,0:T(8,128)(2,1)S(1)}, u32[]{:S(2)}, u32[]{:S(2)}) collective-permute-start(bf16[2,64,256]{2,1,0:T(8,128)(2,1)} %get-tuple-element.33.early_ref), channel_id=1, source_target_pairs={{96,28},{100,24},{104,20},{108,16},{112,12},{116,8},{120,4},{124,0... | collective-permute-start | bytes 196616 | tf_op jit(solution)/shard_map/ppermute | solution.py:480
  8.1 1.4 %collective-permute-start.2 = (bf16[64,256]{1,0:T(8,128)(2,1)}, bf16[64,256]{1,0:T(8,128)(2,1)S(1)}, u32[]{:S(2)}, u32[]{:S(2)}) collective-permute-start(bf16[64,256]{1,0:T(8,128)(2,1)} %get-tuple-element.34), channel_id=1, source_target_pairs={{120,64},{124,68},{112,72},{116,76},{104,80},{108,84},{96,88},{100... | collective-permute-start | bytes 98312 | tf_op jit(solution)/shard_map/ppermute | solution.py:481
  9.5 1.3 %collective-permute-start.3 = (bf16[64,256]{1,0:T(8,128)(2,1)}, bf16[64,256]{1,0:T(8,128)(2,1)S(1)}, u32[]{:S(2)}, u32[]{:S(2)}) collective-permute-start(bf16[64,256]{1,0:T(8,128)(2,1)} %get-tuple-element.35), channel_id=1, source_target_pairs={{124,64},{120,68},{116,72},{112,76},{108,80},{104,84},{100,88},{96... | collective-permute-start | bytes 98312 | tf_op jit(solution)/shard_map/ppermute | solution.py:482
  10.8 1.9 %swap.1 = bf16[30,64,128]{2,1,0:T(8,128)(2,1)} custom-call(s32[1]{0:T(128)} %bitcast.me_ref, bf16[2,64,1792]{2,1,0:T(8,128)(2,1)} %bitcast.12, bf16[2,64,1792]{2,1,0:T(8,128)(2,1)} %bitcast.14, bf16[2,64,256]{2,1,0:T(8,128)(2,1)} %get-tuple-element.29.late_hbm.late_ref), custom_call_target="tpu_custom_call" | custom-call | flops 1000000 | bytes 2000000 | tf_op jit(solution)/shard_map/swap/pallas_call | solution.py:483
  13.5 1.3 %send.1 = bf16[32,64,256]{2,1,0:T(8,128)(2,1)} custom-call(s32[1]{0:T(128)} %bitcast.me_ref, bf16[2,64,256]{2,1,0:T(8,128)(2,1)S(1)} %copy-done.3, bf16[2,64,256]{2,1,0:T(8,128)(2,1)S(1)} %copy-done.2, bf16[2,64,256]{2,1,0:T(8,128)(2,1)S(1)} %collective-permute-done.1.relay_ref, bf16[64,256]{1,0:T(8,128)(2,1)S(1)} %collective-permute-done.2.near_hbm, ...), custom_call_target="tpu_custom_call" | custom-call | tf_op jit(solution)/shard_map/send/pallas_call | solution.py:501
  14.8 8.8 %all-to-all-start = ((bf16[32,64,256]{2,1,0:T(8,128)(2,1)}), bf16[32,64,256]{2,1,0:T(8,128)(2,1)S(1)}, u32[]{:S(2)}, u32[]{:S(2)}) async-start(bf16[32,64,256]{2,1,0:T(8,128)(2,1)} %send.1), calls=%async_computation | async-start | bytes 2097152 | tf_op jit(solution)/shard_map/all_to_all | solution.py:513
  23.6 3.4 %collective-permute-done.other_ref.other_hbm = bf16[30,64,128]{2,1,0:T(8,128)(2,1)S(1)} collective-permute-done((bf16[30,64,128]{2,1,0:T(8,128)(2,1)}, bf16[30,64,128]{2,1,0:T(8,128)(2,1)S(1)}, u32[]{:S(2)}, u32[]{:S(2)}) %collective-permute-start) | collective-permute-done | bytes 491552 | tf_op jit(solution)/shard_map/ppermute | solution.py:500
  27.9 0.8 copy-done.8
  29.4 0.8 copy-done.10
  30.2 7.7 %all-to-all-done.kv_hbm = bf16[32,64,256]{2,1,0:T(8,128)(2,1)S(1)} async-done(((bf16[32,64,256]{2,1,0:T(8,128)(2,1)}), bf16[32,64,256]{2,1,0:T(8,128)(2,1)S(1)}, u32[]{:S(2)}, u32[]{:S(2)}) %all-to-all-start) | async-done | bytes 1048608 | tf_op jit(solution)/shard_map/all_to_all | solution.py:513
  37.9 1.0 %copy-done.11 = bf16[32,64,256]{2,1,0:T(8,128)(2,1)} copy-done((bf16[32,64,256]{2,1,0:T(8,128)(2,1)}, bf16[32,64,256]{2,1,0:T(8,128)(2,1)S(1)}, u32[]{:S(2)}) %copy-start.11) | copy-done | bytes 1048600
  38.9 11.9 %attention.1 = (bf16[30,64,128]{2,1,0:T(8,128)(2,1)}, bf16[30,64,128]{2,1,0:T(8,128)(2,1)}, bf16[32,80,256]{2,1,0:T(8,128)(2,1)}, bf16[64,256]{1,0:T(8,128)(2,1)}, bf16[64,256]{1,0:T(8,128)(2,1)}) custom-call(s32[1]{0:T(128)} %bitcast.me_ref, s32[1,16]{1,0:T(1,128)} %len_ref.1, bf16[2,896,128]{2,1,0:T(8,128)(2,1)} %copy-done.8, ...), custom_call_target="tpu_custom_call" | custom-call | flops 3000000000 | bytes 10000000 | tf_op jit(solution)/shard_map/attention/pallas_call | solution.py:527
  50.8 1.0 collective-permute-start.4
  51.7 1.3 %collective-permute-start.5 = (bf16[64,256]{1,0:T(8,128)(2,1)}, bf16[64,256]{1,0:T(8,128)(2,1)S(1)}, u32[]{:S(2)}, u32[]{:S(2)}) collective-permute-start(bf16[64,256]{1,0:T(8,128)(2,1)} %get-tuple-element.38), channel_id=1, source_target_pairs={{64,120},{68,124},{72,112},{76,116},{80,104},{84,108},{88,96},{92,... | collective-permute-start | bytes 98312 | tf_op jit(solution)/shard_map/ppermute | solution.py:567
  53.0 1.3 %collective-permute-start.6 = (bf16[64,256]{1,0:T(8,128)(2,1)}, bf16[64,256]{1,0:T(8,128)(2,1)S(1)}, u32[]{:S(2)}, u32[]{:S(2)}) collective-permute-start(bf16[64,256]{1,0:T(8,128)(2,1)} %get-tuple-element.39), channel_id=1, source_target_pairs={{64,124},{68,120},{72,116},{76,112},{80,108},{84,104},{88,100},{92... | collective-permute-start | bytes 98312 | tf_op jit(solution)/shard_map/ppermute | solution.py:568
  54.3 10.5 %all-to-all-start.1 = ((bf16[32,80,256]{2,1,0:T(8,128)(2,1)}), bf16[32,80,256]{2,1,0:T(8,128)(2,1)S(1)}, u32[]{:S(2)}, u32[]{:S(2)}) async-start(bf16[32,80,256]{2,1,0:T(8,128)(2,1)} %get-tuple-element.42), calls=%async_computation.1 | async-start | bytes 2621440 | tf_op jit(solution)/shard_map/all_to_all | solution.py:569
  64.9 1.2 %collective-permute-done.5.near_hbm.near_ref = bf16[64,256]{1,0:T(8,128)(2,1)S(1)} collective-permute-done((bf16[64,256]{1,0:T(8,128)(2,1)}, bf16[64,256]{1,0:T(8,128)(2,1)S(1)}, u32[]{:S(2)}, u32[]{:S(2)}) %collective-permute-start.5) | collective-permute-done | bytes 32800 | tf_op jit(solution)/shard_map/ppermute | solution.py:567
  66.0 1.1 %join.1 = (bf16[2,64,1792]{2,1,0:T(8,128)(2,1)}, bf16[2,64,1792]{2,1,0:T(8,128)(2,1)}, bf16[64,256]{1,0:T(8,128)(2,1)S(1)}, bf16[64,256]{1,0:T(8,128)(2,1)S(1)}) custom-call(s32[1]{0:T(128)} %bitcast.me_ref, bf16[30,64,128]{2,1,0:T(8,128)(2,1)S(1)} %copy-done.7, bf16[30,64,128]{2,1,0:T(8,128)(2,1)S(1)} %collective-permute-done.4.theirs_ref, ...), custom_call_target="tpu_custom_call" | custom-call | flops 40000000000 | bytes 4000000 | tf_op jit(solution)/shard_map/join/pallas_call | solution.py:572
  67.2 13.8 %all-to-all-done.1.got_ref = bf16[32,80,256]{2,1,0:T(8,128)(2,1)S(1)} async-done(((bf16[32,80,256]{2,1,0:T(8,128)(2,1)}), bf16[32,80,256]{2,1,0:T(8,128)(2,1)S(1)}, u32[]{:S(2)}, u32[]{:S(2)}) %all-to-all-start.1) | async-done | bytes 1310752 | tf_op jit(solution)/shard_map/all_to_all | solution.py:569
  81.4 1.4 %collective-permute-start.9 = (f32[16,128]{1,0:T(8,128)S(1)}, f32[16,128]{1,0:T(8,128)S(1)}, u32[]{:S(2)}, u32[]{:S(2)}) collective-permute-start(f32[16,128]{1,0:T(8,128)S(1)} %get-tuple-element.49.own_ref), channel_id=1, source_target_pairs={{0,2},{1,3},{2,0},{3,1},{4,6},{5,7},{6,4},{7,5},{8,10},{9,11},{10,... | collective-permute-start | bytes 24584 | tf_op jit(solution)/shard_map/ppermute | solution.py:600
  82.8 1.9 %collective-permute-start.8 = (f32[16,128]{1,0:T(8,128)S(1)}, f32[16,128]{1,0:T(8,128)S(1)}, u32[]{:S(2)}, u32[]{:S(2)}) collective-permute-start(f32[16,128]{1,0:T(8,128)S(1)} %get-tuple-element.49.own_ref), channel_id=1, source_target_pairs={{0,1},{1,0},{2,3},{3,2},{4,5},{5,4},{6,7},{7,6},{8,9},{9,8},{10,11... | collective-permute-start | bytes 24584 | tf_op jit(solution)/shard_map/ppermute | solution.py:600
  84.7 1.3 %collective-permute-start.7 = (bf16[2,64,256]{2,1,0:T(8,128)(2,1)S(1)}, bf16[2,64,256]{2,1,0:T(8,128)(2,1)S(1)}, u32[]{:S(2)}, u32[]{:S(2)}) collective-permute-start(bf16[2,64,256]{2,1,0:T(8,128)(2,1)S(1)} %get-tuple-element.46), channel_id=1, source_target_pairs={{28,96},{24,100},{20,104},{16,108},{12,112},{8,116},{4,120},{0,124... | collective-permute-start | bytes 196616 | tf_op jit(solution)/shard_map/ppermute | solution.py:596
  87.8 7.3 %collective-permute-done.7.relay_ref = bf16[2,64,256]{2,1,0:T(8,128)(2,1)S(1)} collective-permute-done((bf16[2,64,256]{2,1,0:T(8,128)(2,1)S(1)}, bf16[2,64,256]{2,1,0:T(8,128)(2,1)S(1)}, u32[]{:S(2)}, u32[]{:S(2)}) %collective-permute-start.7) | collective-permute-done | bytes 65568 | tf_op jit(solution)/shard_map/ppermute | solution.py:596
  (39 shorter events, 5.1 us)
Async XLA Ops:
  2.2 11.2 %copy-start.2 = (bf16[2,64,256]{2,1,0:T(8,128)(2,1)S(1)}, bf16[2,64,256]{2,1,0:T(8,128)(2,1)}, u32[]{:S(2)}) copy-start(bf16[2,64,256]{2,1,0:T(8,128)(2,1)} %get-tuple-element.29.late_hbm.late_ref) | copy-start | bytes 196612
  2.2 11.2 %copy-start.3 = (bf16[2,64,256]{2,1,0:T(8,128)(2,1)S(1)}, bf16[2,64,256]{2,1,0:T(8,128)(2,1)}, u32[]{:S(2)}) copy-start(bf16[2,64,256]{2,1,0:T(8,128)(2,1)} %get-tuple-element.33.early_ref) | copy-start | bytes 196612
  2.3 11.2 %collective-permute-start.1 = (bf16[2,64,256]{2,1,0:T(8,128)(2,1)}, bf16[2,64,256]{2,1,0:T(8,128)(2,1)S(1)}, u32[]{:S(2)}, u32[]{:S(2)}) collective-permute-start(bf16[2,64,256]{2,1,0:T(8,128)(2,1)} %get-tuple-element.33.early_ref), channel_id=1, source_target_pairs={{96,28},{100,24},{104,20},{108,16},{112,12},{116,8},{120,4},{124,0... | collective-permute-start | bytes 196616 | tf_op jit(solution)/shard_map/ppermute | solution.py:480
  8.1 5.4 %collective-permute-start.2 = (bf16[64,256]{1,0:T(8,128)(2,1)}, bf16[64,256]{1,0:T(8,128)(2,1)S(1)}, u32[]{:S(2)}, u32[]{:S(2)}) collective-permute-start(bf16[64,256]{1,0:T(8,128)(2,1)} %get-tuple-element.34), channel_id=1, source_target_pairs={{120,64},{124,68},{112,72},{116,76},{104,80},{108,84},{96,88},{100... | collective-permute-start | bytes 98312 | tf_op jit(solution)/shard_map/ppermute | solution.py:481
  9.5 3.9 %collective-permute-start.3 = (bf16[64,256]{1,0:T(8,128)(2,1)}, bf16[64,256]{1,0:T(8,128)(2,1)S(1)}, u32[]{:S(2)}, u32[]{:S(2)}) collective-permute-start(bf16[64,256]{1,0:T(8,128)(2,1)} %get-tuple-element.35), channel_id=1, source_target_pairs={{124,64},{120,68},{116,72},{112,76},{108,80},{104,84},{100,88},{96... | collective-permute-start | bytes 98312 | tf_op jit(solution)/shard_map/ppermute | solution.py:482
  12.8 14.3 %collective-permute-start = (bf16[30,64,128]{2,1,0:T(8,128)(2,1)}, bf16[30,64,128]{2,1,0:T(8,128)(2,1)S(1)}, u32[]{:S(2)}, u32[]{:S(2)}) collective-permute-start(bf16[30,64,128]{2,1,0:T(8,128)(2,1)} %swap.1), channel_id=1, source_target_pairs={{0,4},{4,0},{8,12},{12,8},{16,20},{20,16},{24,28},{28,24},{32,36},... | collective-permute-start | bytes 1474568 | tf_op jit(solution)/shard_map/ppermute | solution.py:500
  13.4 1.4 %copy-start.4 = (bf16[64,256]{1,0:T(8,128)(2,1)}, bf16[64,256]{1,0:T(8,128)(2,1)S(1)}, u32[]{:S(2)}) copy-start(bf16[64,256]{1,0:T(8,128)(2,1)S(1)} %collective-permute-done.2.near_hbm) | copy-start | bytes 98308
  13.5 1.4 %copy-start.5 = (bf16[64,256]{1,0:T(8,128)(2,1)}, bf16[64,256]{1,0:T(8,128)(2,1)S(1)}, u32[]{:S(2)}) copy-start(bf16[64,256]{1,0:T(8,128)(2,1)S(1)} %collective-permute-done.3.far_hbm) | copy-start | bytes 98308
  14.8 8.8 %copy-start.12 = (f32[1792]{0:T(1024)S(1)}, f32[1792]{0:T(1024)}, u32[]{:S(2)}) copy-start(f32[1792]{0:T(1024)} %param.10) | copy-start | bytes 21508
  14.8 12.3 %copy-start = (bf16[1,2,64,1792]{3,2,1,0:T(8,128)(2,1)S(1)}, bf16[1,2,64,1792]{3,2,1,0:T(8,128)(2,1)}, u32[]{:S(2)}) copy-start(bf16[1,2,64,1792]{3,2,1,0:T(8,128)(2,1)} %param.7) | copy-start | bytes 1376260
  14.8 12.3 %copy-start.1 = (bf16[1,2,64,1792]{3,2,1,0:T(8,128)(2,1)S(1)}, bf16[1,2,64,1792]{3,2,1,0:T(8,128)(2,1)}, u32[]{:S(2)}) copy-start(bf16[1,2,64,1792]{3,2,1,0:T(8,128)(2,1)} %param.12) | copy-start | bytes 1376260
  14.8 23.0 %all-to-all-start = ((bf16[32,64,256]{2,1,0:T(8,128)(2,1)}), bf16[32,64,256]{2,1,0:T(8,128)(2,1)S(1)}, u32[]{:S(2)}, u32[]{:S(2)}) async-start(bf16[32,64,256]{2,1,0:T(8,128)(2,1)} %send.1), calls=%async_computation | async-start | bytes 2097152 | tf_op jit(solution)/shard_map/all_to_all | solution.py:513
  27.1 0.8 copy-start.6
  29.4 0.8 copy-start.10
  37.9 1.0 %copy-start.11 = (bf16[32,64,256]{2,1,0:T(8,128)(2,1)}, bf16[32,64,256]{2,1,0:T(8,128)(2,1)S(1)}, u32[]{:S(2)}) copy-start(bf16[32,64,256]{2,1,0:T(8,128)(2,1)S(1)} %all-to-all-done.kv_hbm) | copy-start | bytes 3145732
  50.8 15.3 %collective-permute-start.4 = (bf16[30,64,128]{2,1,0:T(8,128)(2,1)}, bf16[30,64,128]{2,1,0:T(8,128)(2,1)S(1)}, u32[]{:S(2)}, u32[]{:S(2)}) collective-permute-start(bf16[30,64,128]{2,1,0:T(8,128)(2,1)} %get-tuple-element.37), channel_id=1, source_target_pairs={{0,4},{4,0},{8,12},{12,8},{16,20},{20,16},{24,28},{28,24},{32,36},... | collective-permute-start | bytes 1474568 | tf_op jit(solution)/shard_map/ppermute | solution.py:566
  51.7 14.3 %collective-permute-start.5 = (bf16[64,256]{1,0:T(8,128)(2,1)}, bf16[64,256]{1,0:T(8,128)(2,1)S(1)}, u32[]{:S(2)}, u32[]{:S(2)}) collective-permute-start(bf16[64,256]{1,0:T(8,128)(2,1)} %get-tuple-element.38), channel_id=1, source_target_pairs={{64,120},{68,124},{72,112},{76,116},{80,104},{84,108},{88,96},{92,... | collective-permute-start | bytes 98312 | tf_op jit(solution)/shard_map/ppermute | solution.py:567
  53.0 13.0 %collective-permute-start.6 = (bf16[64,256]{1,0:T(8,128)(2,1)}, bf16[64,256]{1,0:T(8,128)(2,1)S(1)}, u32[]{:S(2)}, u32[]{:S(2)}) collective-permute-start(bf16[64,256]{1,0:T(8,128)(2,1)} %get-tuple-element.39), channel_id=1, source_target_pairs={{64,124},{68,120},{72,116},{76,112},{80,108},{84,104},{88,100},{92... | collective-permute-start | bytes 98312 | tf_op jit(solution)/shard_map/ppermute | solution.py:568
  54.3 11.7 %copy-start.7 = (bf16[30,64,128]{2,1,0:T(8,128)(2,1)S(1)}, bf16[30,64,128]{2,1,0:T(8,128)(2,1)}, u32[]{:S(2)}) copy-start(bf16[30,64,128]{2,1,0:T(8,128)(2,1)} %get-tuple-element.36.mine_ref) | copy-start | bytes 1474564
  54.3 26.6 %all-to-all-start.1 = ((bf16[32,80,256]{2,1,0:T(8,128)(2,1)}), bf16[32,80,256]{2,1,0:T(8,128)(2,1)S(1)}, u32[]{:S(2)}, u32[]{:S(2)}) async-start(bf16[32,80,256]{2,1,0:T(8,128)(2,1)} %get-tuple-element.42), calls=%async_computation.1 | async-start | bytes 2621440 | tf_op jit(solution)/shard_map/all_to_all | solution.py:569
  81.3 4.7 %collective-permute-start.10 = (f32[16,128]{1,0:T(8,128)S(1)}, f32[16,128]{1,0:T(8,128)S(1)}, u32[]{:S(2)}, u32[]{:S(2)}) collective-permute-start(f32[16,128]{1,0:T(8,128)S(1)} %get-tuple-element.49.own_ref), channel_id=1, source_target_pairs={{0,3},{1,2},{2,1},{3,0},{4,7},{5,6},{6,5},{7,4},{8,11},{9,10},{10,... | collective-permute-start | bytes 24584 | tf_op jit(solution)/shard_map/ppermute | solution.py:600
  81.4 5.2 %collective-permute-start.9 = (f32[16,128]{1,0:T(8,128)S(1)}, f32[16,128]{1,0:T(8,128)S(1)}, u32[]{:S(2)}, u32[]{:S(2)}) collective-permute-start(f32[16,128]{1,0:T(8,128)S(1)} %get-tuple-element.49.own_ref), channel_id=1, source_target_pairs={{0,2},{1,3},{2,0},{3,1},{4,6},{5,7},{6,4},{7,5},{8,10},{9,11},{10,... | collective-permute-start | bytes 24584 | tf_op jit(solution)/shard_map/ppermute | solution.py:600
  82.8 3.8 %collective-permute-start.8 = (f32[16,128]{1,0:T(8,128)S(1)}, f32[16,128]{1,0:T(8,128)S(1)}, u32[]{:S(2)}, u32[]{:S(2)}) collective-permute-start(f32[16,128]{1,0:T(8,128)S(1)} %get-tuple-element.49.own_ref), channel_id=1, source_target_pairs={{0,1},{1,0},{2,3},{3,2},{4,5},{5,4},{6,7},{7,6},{8,9},{9,8},{10,11... | collective-permute-start | bytes 24584 | tf_op jit(solution)/shard_map/ppermute | solution.py:600
  84.7 10.4 %collective-permute-start.7 = (bf16[2,64,256]{2,1,0:T(8,128)(2,1)S(1)}, bf16[2,64,256]{2,1,0:T(8,128)(2,1)S(1)}, u32[]{:S(2)}, u32[]{:S(2)}) collective-permute-start(bf16[2,64,256]{2,1,0:T(8,128)(2,1)S(1)} %get-tuple-element.46), channel_id=1, source_target_pairs={{28,96},{24,100},{20,104},{16,108},{12,112},{8,116},{4,120},{0,124... | collective-permute-start | bytes 196616 | tf_op jit(solution)/shard_map/ppermute | solution.py:596
  (2 other events, 1.5 us)

commit v6 on v5

--- a/solution.py
+++ b/solution.py
@@ -26,7 +26,7 @@
 BIAS_FLOPS = 10_000_000_000
 VMEM_BYTES = 59 * 1024 * 1024
 SMALL_BYTES = 16 * 1024 * 1024
-BLOCKS_PER_CHUNK = 4
+BLOCKS_PER_CHUNK = 9
 
 NT = (((1,), (1,)), ((), ()))
 NN = (((1,), (0,)), ((), ()))
@@ -168,6 +168,7 @@
     sum_ref,
     in_sems,
     out_sems,
+    tile_sems,
 ):
     block_len = mine_ref.shape[1]
     pair_len = 2 * block_len
@@ -212,6 +213,13 @@
         late = jnp.where(c == me, own_late, jnp.where(c == pair + 1 - head, other_late, c))
         return jnp.where(block < group_size, early, late)
 
+    def tile_copies(first, count, sem):
+        at = pl.ds(first, count)
+        return [
+            pltpu.make_async_copy(ref.at[at], hbm.at[at], tile_sems.at[i, sem])
+            for i, (ref, hbm) in enumerate(((back_ref, back_hbm), (mine_ref, mine_hbm)))
+        ]
+
     stage_ref[...] = jnp.zeros_like(stage_ref)
     sum_ref[...] = jnp.zeros_like(sum_ref)
     for load in loads:
@@ -285,6 +293,8 @@
                 pl.ds(t * pair_len + partner_at, block_len), :
             ].astype(jnp.bfloat16)
 
+        for copy in tile_copies(h * GROUP, GROUP, h):
+            copy.start()
         acc_ref[...] = jnp.zeros_like(acc_ref)
 
         def grad_step(i, value_total):
@@ -311,6 +321,9 @@
             sum_ref[t : t + 1, :] += jnp.sum(
                 row_ref[t * pair_len : (t + 1) * pair_len, :], axis=0, keepdims=True
             )
+
+        for copy in tile_copies((2 + h) * GROUP, GROUP, 2 + h):
+            copy.start()
 
         def store(i, carry):
             slot = place(low + i)
@@ -345,16 +358,16 @@
         pltpu.make_async_copy(source, into, out_sems.at[i])
         for i, (source, into) in enumerate(
             (
-                (back_ref, back_hbm),
                 (stage_ref.at[near, :block_len], near_grad_hbm),
                 (stage_ref.at[far, :block_len], far_grad_hbm),
                 (stage_ref.at[:group_size], parts_hbm),
-                (mine_ref, mine_hbm),
             )
         )
-    ]
+    ] + tile_copies(4 * GROUP, 2, 4)
     for store in stores:
         store.start()
+    for i in range(4):
+        stores += tile_copies(i * GROUP, GROUP, i)
     for store in stores:
         store.wait()
 
@@ -551,7 +564,8 @@
             pltpu.VMEM((rows, HD), f32),
             pltpu.VMEM((SUM_ROWS // 2, HD), f32),
             pltpu.SemaphoreType.DMA((8,)),
-            pltpu.SemaphoreType.DMA((5,)),
+            pltpu.SemaphoreType.DMA((3,)),
+            pltpu.SemaphoreType.DMA((2, 5)),
         ],
         compiler_params=large,
         cost_estimate=pl.CostEstimate(

time: 95.9 us -> 97.3 us (1.015); the launches traced: 95.8 us -> 95.8 us
  waiting for transfers between devices: 34 us -> 32.8 us
    ppermute x1, waiting for transfers between devices: 1.17 us -> 0.01 us  [on_device(): near_grad = lax.ppermute(near_grad, 'ctx', back_along(to_near))]
    ppermute x3, waiting for transfers between devices: 0.59 us -> 1.63 us  [on_device(): lax.ppermute(sums, 'dp', [(i, i ^ step) for i in range(dp_size)])]
  transfers between devices with their start and end apart: 13 -> 13, of which waited for: 6 -> 5; matrix products, arithmetic and copies ran while one was open for 1% -> 1% of each run, Pallas kernels for 4% -> 4%
where the time goes in v6:
time: 97.3 us; the launch traced here: 95.8 us
  starting transfers between devices  37.7 us (39%)
  waiting for transfers between devices  32.8 us (34%)
  Pallas kernels  20 us (21%)
  local copies, waits for them, and re-layouts  3.83 us (4%)
    all_to_all x1, waiting for transfers between devices, on_device(): got = lax.all_to_all(parts, 'ctx', 0, 0)  13.6 us
    pallas_call x1, Pallas kernels, on_device(): pl.pallas_call(functools.partial(attention_kernel, group_size, reach), ou...  12.2 us
    all_to_all x1, starting transfers between devices, on_device(): got = lax.all_to_all(parts, 'ctx', 0, 0)  10.5 us
    all_to_all x1, starting transfers between devices, on_device(): gathered = lax.all_to_all(sent, 'ctx', 0, 0)  8.76 us
    all_to_all x1, waiting for transfers between devices, on_device(): gathered = lax.all_to_all(sent, 'ctx', 0, 0)  7.71 us
    ppermute x1, waiting for transfers between devices, on_device(): relay_grad = lax.ppermute(relay_total, 'ctx', back_along(relays))  6.45 us
    ppermute x1, starting transfers between devices, on_device(): relayed = lax.ppermute(early, 'ctx', relays)  5.81 us
    ppermute x3, starting transfers between devices, on_device(): lax.ppermute(sums, 'dp', [(i, i ^ step) for i in range(dp_size)])  4.34 us
  transfers between devices with their start and end apart: 13, of which 5 were waited for; matrix products, arithmetic and copies ran while one was open for 1% of the time, Pallas kernels for 4%

profile of v6, /device:TPU:24, one launch (start us, length us, event | category | flops | bytes accessed | tf_op | source)
XLA Modules:
  0.0 95.8 jit_solution(14365779148398260056)
XLA Ops:
  0.6 1.6 %blocks.1 = (bf16[2,64,256]{2,1,0:T(8,128)(2,1)}, bf16[2,64,256]{2,1,0:T(8,128)(2,1)}, bf16[64,256]{1,0:T(8,128)(2,1)}, bf16[64,256]{1,0:T(8,128)(2,1)}) custom-call(s32[1]{0:T(128)} %bitcast.me_ref, bf16[2,64,256]{2,1,0:T(8,128)(2,1)} %bitcast.16, bf16[2,64,256]{2,1,0:T(8,128)(2,1)} %bitcast.17, f32[1,256]{1,0:T(1,128)} %bitcast.18), custom_call_target="tpu_custom_call" | custom-call | tf_op jit(solution)/shard_map/blocks/pallas_call | solution.py:479
  2.3 5.8 %collective-permute-start.1 = (bf16[2,64,256]{2,1,0:T(8,128)(2,1)}, bf16[2,64,256]{2,1,0:T(8,128)(2,1)S(1)}, u32[]{:S(2)}, u32[]{:S(2)}) collective-permute-start(bf16[2,64,256]{2,1,0:T(8,128)(2,1)} %get-tuple-element.33.early_ref), channel_id=1, source_target_pairs={{96,28},{100,24},{104,20},{108,16},{112,12},{116,8},{120,4},{124,0... | collective-permute-start | bytes 196616 | tf_op jit(solution)/shard_map/ppermute | solution.py:493
  8.1 1.4 %collective-permute-start.2 = (bf16[64,256]{1,0:T(8,128)(2,1)}, bf16[64,256]{1,0:T(8,128)(2,1)S(1)}, u32[]{:S(2)}, u32[]{:S(2)}) collective-permute-start(bf16[64,256]{1,0:T(8,128)(2,1)} %get-tuple-element.34), channel_id=1, source_target_pairs={{120,64},{124,68},{112,72},{116,76},{104,80},{108,84},{96,88},{100... | collective-permute-start | bytes 98312 | tf_op jit(solution)/shard_map/ppermute | solution.py:494
  9.5 1.3 %collective-permute-start.3 = (bf16[64,256]{1,0:T(8,128)(2,1)}, bf16[64,256]{1,0:T(8,128)(2,1)S(1)}, u32[]{:S(2)}, u32[]{:S(2)}) collective-permute-start(bf16[64,256]{1,0:T(8,128)(2,1)} %get-tuple-element.35), channel_id=1, source_target_pairs={{124,64},{120,68},{116,72},{112,76},{108,80},{104,84},{100,88},{96... | collective-permute-start | bytes 98312 | tf_op jit(solution)/shard_map/ppermute | solution.py:495
  10.8 1.9 %swap.1 = bf16[30,64,128]{2,1,0:T(8,128)(2,1)} custom-call(s32[1]{0:T(128)} %bitcast.me_ref, bf16[2,64,1792]{2,1,0:T(8,128)(2,1)} %bitcast.12, bf16[2,64,1792]{2,1,0:T(8,128)(2,1)} %bitcast.14, bf16[2,64,256]{2,1,0:T(8,128)(2,1)} %get-tuple-element.29.late_hbm.late_ref), custom_call_target="tpu_custom_call" | custom-call | flops 1000000 | bytes 2000000 | tf_op jit(solution)/shard_map/swap/pallas_call | solution.py:496
  13.5 1.3 %send.1 = bf16[32,64,256]{2,1,0:T(8,128)(2,1)} custom-call(s32[1]{0:T(128)} %bitcast.me_ref, bf16[2,64,256]{2,1,0:T(8,128)(2,1)S(1)} %copy-done.3, bf16[2,64,256]{2,1,0:T(8,128)(2,1)S(1)} %copy-done.2, bf16[2,64,256]{2,1,0:T(8,128)(2,1)S(1)} %collective-permute-done.1.relay_ref, bf16[64,256]{1,0:T(8,128)(2,1)S(1)} %collective-permute-done.2.near_hbm, ...), custom_call_target="tpu_custom_call" | custom-call | tf_op jit(solution)/shard_map/send/pallas_call | solution.py:514
  14.8 8.8 %all-to-all-start = ((bf16[32,64,256]{2,1,0:T(8,128)(2,1)}), bf16[32,64,256]{2,1,0:T(8,128)(2,1)S(1)}, u32[]{:S(2)}, u32[]{:S(2)}) async-start(bf16[32,64,256]{2,1,0:T(8,128)(2,1)} %send.1), calls=%async_computation | async-start | bytes 2097152 | tf_op jit(solution)/shard_map/all_to_all | solution.py:526
  23.6 3.4 %collective-permute-done.other_ref.other_hbm = bf16[30,64,128]{2,1,0:T(8,128)(2,1)S(1)} collective-permute-done((bf16[30,64,128]{2,1,0:T(8,128)(2,1)}, bf16[30,64,128]{2,1,0:T(8,128)(2,1)S(1)}, u32[]{:S(2)}, u32[]{:S(2)}) %collective-permute-start) | collective-permute-done | bytes 491552 | tf_op jit(solution)/shard_map/ppermute | solution.py:513
  27.9 0.8 copy-done.8
  29.4 0.8 copy-done.10
  30.2 7.7 %all-to-all-done.kv_hbm = bf16[32,64,256]{2,1,0:T(8,128)(2,1)S(1)} async-done(((bf16[32,64,256]{2,1,0:T(8,128)(2,1)}), bf16[32,64,256]{2,1,0:T(8,128)(2,1)S(1)}, u32[]{:S(2)}, u32[]{:S(2)}) %all-to-all-start) | async-done | bytes 1048608 | tf_op jit(solution)/shard_map/all_to_all | solution.py:526
  37.9 1.0 %copy-done.11 = bf16[32,64,256]{2,1,0:T(8,128)(2,1)} copy-done((bf16[32,64,256]{2,1,0:T(8,128)(2,1)}, bf16[32,64,256]{2,1,0:T(8,128)(2,1)S(1)}, u32[]{:S(2)}) %copy-start.11) | copy-done | bytes 1048600
  38.9 12.2 %attention.1 = (bf16[30,64,128]{2,1,0:T(8,128)(2,1)}, bf16[30,64,128]{2,1,0:T(8,128)(2,1)}, bf16[32,80,256]{2,1,0:T(8,128)(2,1)}, bf16[64,256]{1,0:T(8,128)(2,1)}, bf16[64,256]{1,0:T(8,128)(2,1)}) custom-call(s32[1]{0:T(128)} %bitcast.me_ref, s32[1,16]{1,0:T(1,128)} %len_ref.1, bf16[2,896,128]{2,1,0:T(8,128)(2,1)} %copy-done.8, ...), custom_call_target="tpu_custom_call" | custom-call | flops 3000000000 | bytes 10000000 | tf_op jit(solution)/shard_map/attention/pallas_call | solution.py:540
  51.1 1.0 %collective-permute-start.4 = (bf16[30,64,128]{2,1,0:T(8,128)(2,1)}, bf16[30,64,128]{2,1,0:T(8,128)(2,1)S(1)}, u32[]{:S(2)}, u32[]{:S(2)}) collective-permute-start(bf16[30,64,128]{2,1,0:T(8,128)(2,1)} %get-tuple-element.37), channel_id=1, source_target_pairs={{0,4},{4,0},{8,12},{12,8},{16,20},{20,16},{24,28},{28,24},{32,36},... | collective-permute-start | bytes 1474568 | tf_op jit(solution)/shard_map/ppermute | solution.py:580
  52.0 1.3 %collective-permute-start.5 = (bf16[64,256]{1,0:T(8,128)(2,1)}, bf16[64,256]{1,0:T(8,128)(2,1)S(1)}, u32[]{:S(2)}, u32[]{:S(2)}) collective-permute-start(bf16[64,256]{1,0:T(8,128)(2,1)} %get-tuple-element.38), channel_id=1, source_target_pairs={{64,120},{68,124},{72,112},{76,116},{80,104},{84,108},{88,96},{92,... | collective-permute-start | bytes 98312 | tf_op jit(solution)/shard_map/ppermute | solution.py:581
  53.3 1.3 %collective-permute-start.6 = (bf16[64,256]{1,0:T(8,128)(2,1)}, bf16[64,256]{1,0:T(8,128)(2,1)S(1)}, u32[]{:S(2)}, u32[]{:S(2)}) collective-permute-start(bf16[64,256]{1,0:T(8,128)(2,1)} %get-tuple-element.39), channel_id=1, source_target_pairs={{64,124},{68,120},{72,116},{76,112},{80,108},{84,104},{88,100},{92... | collective-permute-start | bytes 98312 | tf_op jit(solution)/shard_map/ppermute | solution.py:582
  54.6 10.5 %all-to-all-start.1 = ((bf16[32,80,256]{2,1,0:T(8,128)(2,1)}), bf16[32,80,256]{2,1,0:T(8,128)(2,1)S(1)}, u32[]{:S(2)}, u32[]{:S(2)}) async-start(bf16[32,80,256]{2,1,0:T(8,128)(2,1)} %get-tuple-element.42), calls=%async_computation.1 | async-start | bytes 2621440 | tf_op jit(solution)/shard_map/all_to_all | solution.py:583
  65.2 1.1 %join.1 = (bf16[2,64,1792]{2,1,0:T(8,128)(2,1)}, bf16[2,64,1792]{2,1,0:T(8,128)(2,1)}, bf16[64,256]{1,0:T(8,128)(2,1)S(1)}, bf16[64,256]{1,0:T(8,128)(2,1)S(1)}) custom-call(s32[1]{0:T(128)} %bitcast.me_ref, bf16[30,64,128]{2,1,0:T(8,128)(2,1)S(1)} %copy-done.7, bf16[30,64,128]{2,1,0:T(8,128)(2,1)S(1)} %collective-permute-done.4.theirs_ref, ...), custom_call_target="tpu_custom_call" | custom-call | flops 40000000000 | bytes 4000000 | tf_op jit(solution)/shard_map/join/pallas_call | solution.py:586
  66.3 13.6 %all-to-all-done.1.got_ref = bf16[32,80,256]{2,1,0:T(8,128)(2,1)S(1)} async-done(((bf16[32,80,256]{2,1,0:T(8,128)(2,1)}), bf16[32,80,256]{2,1,0:T(8,128)(2,1)S(1)}, u32[]{:S(2)}, u32[]{:S(2)}) %all-to-all-start.1) | async-done | bytes 1310752 | tf_op jit(solution)/shard_map/all_to_all | solution.py:583
  80.2 2.1 %collective-permute-start.10 = (f32[16,128]{1,0:T(8,128)S(1)}, f32[16,128]{1,0:T(8,128)S(1)}, u32[]{:S(2)}, u32[]{:S(2)}) collective-permute-start(f32[16,128]{1,0:T(8,128)S(1)} %get-tuple-element.49.own_ref), channel_id=1, source_target_pairs={{0,3},{1,2},{2,1},{3,0},{4,7},{5,6},{6,5},{7,4},{8,11},{9,10},{10,... | collective-permute-start | bytes 24584 | tf_op jit(solution)/shard_map/ppermute | solution.py:614
  82.3 2.2 %collective-permute-start.9 = (f32[16,128]{1,0:T(8,128)S(1)}, f32[16,128]{1,0:T(8,128)S(1)}, u32[]{:S(2)}, u32[]{:S(2)}) collective-permute-start(f32[16,128]{1,0:T(8,128)S(1)} %get-tuple-element.49.own_ref), channel_id=1, source_target_pairs={{0,2},{1,3},{2,0},{3,1},{4,6},{5,7},{6,4},{7,5},{8,10},{9,11},{10,... | collective-permute-start | bytes 24584 | tf_op jit(solution)/shard_map/ppermute | solution.py:614
  84.5 1.3 %collective-permute-start.7 = (bf16[2,64,256]{2,1,0:T(8,128)(2,1)S(1)}, bf16[2,64,256]{2,1,0:T(8,128)(2,1)S(1)}, u32[]{:S(2)}, u32[]{:S(2)}) collective-permute-start(bf16[2,64,256]{2,1,0:T(8,128)(2,1)S(1)} %get-tuple-element.46), channel_id=1, source_target_pairs={{28,96},{24,100},{20,104},{16,108},{12,112},{8,116},{4,120},{0,124... | collective-permute-start | bytes 196616 | tf_op jit(solution)/shard_map/ppermute | solution.py:610
  85.8 1.6 %collective-permute-done.9.refs_1_ = f32[16,128]{1,0:T(8,128)S(1)} collective-permute-done((f32[16,128]{1,0:T(8,128)S(1)}, f32[16,128]{1,0:T(8,128)S(1)}, u32[]{:S(2)}, u32[]{:S(2)}) %collective-permute-start.9) | collective-permute-done | bytes 8224 | tf_op jit(solution)/shard_map/ppermute | solution.py:614
  88.7 6.5 %collective-permute-done.7.relay_ref = bf16[2,64,256]{2,1,0:T(8,128)(2,1)S(1)} collective-permute-done((bf16[2,64,256]{2,1,0:T(8,128)(2,1)S(1)}, bf16[2,64,256]{2,1,0:T(8,128)(2,1)S(1)}, u32[]{:S(2)}, u32[]{:S(2)}) %collective-permute-start.7) | collective-permute-done | bytes 65568 | tf_op jit(solution)/shard_map/ppermute | solution.py:610
  (39 shorter events, 4.5 us)
Async XLA Ops:
  2.2 11.2 %copy-start.2 = (bf16[2,64,256]{2,1,0:T(8,128)(2,1)S(1)}, bf16[2,64,256]{2,1,0:T(8,128)(2,1)}, u32[]{:S(2)}) copy-start(bf16[2,64,256]{2,1,0:T(8,128)(2,1)} %get-tuple-element.29.late_hbm.late_ref) | copy-start | bytes 196612
  2.2 11.2 %copy-start.3 = (bf16[2,64,256]{2,1,0:T(8,128)(2,1)S(1)}, bf16[2,64,256]{2,1,0:T(8,128)(2,1)}, u32[]{:S(2)}) copy-start(bf16[2,64,256]{2,1,0:T(8,128)(2,1)} %get-tuple-element.33.early_ref) | copy-start | bytes 196612
  2.3 11.2 %collective-permute-start.1 = (bf16[2,64,256]{2,1,0:T(8,128)(2,1)}, bf16[2,64,256]{2,1,0:T(8,128)(2,1)S(1)}, u32[]{:S(2)}, u32[]{:S(2)}) collective-permute-start(bf16[2,64,256]{2,1,0:T(8,128)(2,1)} %get-tuple-element.33.early_ref), channel_id=1, source_target_pairs={{96,28},{100,24},{104,20},{108,16},{112,12},{116,8},{120,4},{124,0... | collective-permute-start | bytes 196616 | tf_op jit(solution)/shard_map/ppermute | solution.py:493
  8.1 5.4 %collective-permute-start.2 = (bf16[64,256]{1,0:T(8,128)(2,1)}, bf16[64,256]{1,0:T(8,128)(2,1)S(1)}, u32[]{:S(2)}, u32[]{:S(2)}) collective-permute-start(bf16[64,256]{1,0:T(8,128)(2,1)} %get-tuple-element.34), channel_id=1, source_target_pairs={{120,64},{124,68},{112,72},{116,76},{104,80},{108,84},{96,88},{100... | collective-permute-start | bytes 98312 | tf_op jit(solution)/shard_map/ppermute | solution.py:494
  9.5 3.9 %collective-permute-start.3 = (bf16[64,256]{1,0:T(8,128)(2,1)}, bf16[64,256]{1,0:T(8,128)(2,1)S(1)}, u32[]{:S(2)}, u32[]{:S(2)}) collective-permute-start(bf16[64,256]{1,0:T(8,128)(2,1)} %get-tuple-element.35), channel_id=1, source_target_pairs={{124,64},{120,68},{116,72},{112,76},{108,80},{104,84},{100,88},{96... | collective-permute-start | bytes 98312 | tf_op jit(solution)/shard_map/ppermute | solution.py:495
  12.8 14.3 %collective-permute-start = (bf16[30,64,128]{2,1,0:T(8,128)(2,1)}, bf16[30,64,128]{2,1,0:T(8,128)(2,1)S(1)}, u32[]{:S(2)}, u32[]{:S(2)}) collective-permute-start(bf16[30,64,128]{2,1,0:T(8,128)(2,1)} %swap.1), channel_id=1, source_target_pairs={{0,4},{4,0},{8,12},{12,8},{16,20},{20,16},{24,28},{28,24},{32,36},... | collective-permute-start | bytes 1474568 | tf_op jit(solution)/shard_map/ppermute | solution.py:513
  13.4 1.4 %copy-start.4 = (bf16[64,256]{1,0:T(8,128)(2,1)}, bf16[64,256]{1,0:T(8,128)(2,1)S(1)}, u32[]{:S(2)}) copy-start(bf16[64,256]{1,0:T(8,128)(2,1)S(1)} %collective-permute-done.2.near_hbm) | copy-start | bytes 98308
  13.5 1.4 %copy-start.5 = (bf16[64,256]{1,0:T(8,128)(2,1)}, bf16[64,256]{1,0:T(8,128)(2,1)S(1)}, u32[]{:S(2)}) copy-start(bf16[64,256]{1,0:T(8,128)(2,1)S(1)} %collective-permute-done.3.far_hbm) | copy-start | bytes 98308
  14.8 8.8 %copy-start.12 = (f32[1792]{0:T(1024)S(1)}, f32[1792]{0:T(1024)}, u32[]{:S(2)}) copy-start(f32[1792]{0:T(1024)} %param.10) | copy-start | bytes 21508
  14.8 12.3 %copy-start = (bf16[1,2,64,1792]{3,2,1,0:T(8,128)(2,1)S(1)}, bf16[1,2,64,1792]{3,2,1,0:T(8,128)(2,1)}, u32[]{:S(2)}) copy-start(bf16[1,2,64,1792]{3,2,1,0:T(8,128)(2,1)} %param.7) | copy-start | bytes 1376260
  14.8 12.3 %copy-start.1 = (bf16[1,2,64,1792]{3,2,1,0:T(8,128)(2,1)S(1)}, bf16[1,2,64,1792]{3,2,1,0:T(8,128)(2,1)}, u32[]{:S(2)}) copy-start(bf16[1,2,64,1792]{3,2,1,0:T(8,128)(2,1)} %param.12) | copy-start | bytes 1376260
  14.8 23.0 %all-to-all-start = ((bf16[32,64,256]{2,1,0:T(8,128)(2,1)}), bf16[32,64,256]{2,1,0:T(8,128)(2,1)S(1)}, u32[]{:S(2)}, u32[]{:S(2)}) async-start(bf16[32,64,256]{2,1,0:T(8,128)(2,1)} %send.1), calls=%async_computation | async-start | bytes 2097152 | tf_op jit(solution)/shard_map/all_to_all | solution.py:526
  27.1 0.8 copy-start.6
  29.4 0.8 copy-start.10
  37.9 1.0 %copy-start.11 = (bf16[32,64,256]{2,1,0:T(8,128)(2,1)}, bf16[32,64,256]{2,1,0:T(8,128)(2,1)S(1)}, u32[]{:S(2)}) copy-start(bf16[32,64,256]{2,1,0:T(8,128)(2,1)S(1)} %all-to-all-done.kv_hbm) | copy-start | bytes 3145732
  51.1 14.1 %collective-permute-start.4 = (bf16[30,64,128]{2,1,0:T(8,128)(2,1)}, bf16[30,64,128]{2,1,0:T(8,128)(2,1)S(1)}, u32[]{:S(2)}, u32[]{:S(2)}) collective-permute-start(bf16[30,64,128]{2,1,0:T(8,128)(2,1)} %get-tuple-element.37), channel_id=1, source_target_pairs={{0,4},{4,0},{8,12},{12,8},{16,20},{20,16},{24,28},{28,24},{32,36},... | collective-permute-start | bytes 1474568 | tf_op jit(solution)/shard_map/ppermute | solution.py:580
  52.0 13.1 %collective-permute-start.5 = (bf16[64,256]{1,0:T(8,128)(2,1)}, bf16[64,256]{1,0:T(8,128)(2,1)S(1)}, u32[]{:S(2)}, u32[]{:S(2)}) collective-permute-start(bf16[64,256]{1,0:T(8,128)(2,1)} %get-tuple-element.38), channel_id=1, source_target_pairs={{64,120},{68,124},{72,112},{76,116},{80,104},{84,108},{88,96},{92,... | collective-permute-start | bytes 98312 | tf_op jit(solution)/shard_map/ppermute | solution.py:581
  53.3 11.9 %collective-permute-start.6 = (bf16[64,256]{1,0:T(8,128)(2,1)}, bf16[64,256]{1,0:T(8,128)(2,1)S(1)}, u32[]{:S(2)}, u32[]{:S(2)}) collective-permute-start(bf16[64,256]{1,0:T(8,128)(2,1)} %get-tuple-element.39), channel_id=1, source_target_pairs={{64,124},{68,120},{72,116},{76,112},{80,108},{84,104},{88,100},{92... | collective-permute-start | bytes 98312 | tf_op jit(solution)/shard_map/ppermute | solution.py:582
  54.6 10.6 %copy-start.7 = (bf16[30,64,128]{2,1,0:T(8,128)(2,1)S(1)}, bf16[30,64,128]{2,1,0:T(8,128)(2,1)}, u32[]{:S(2)}) copy-start(bf16[30,64,128]{2,1,0:T(8,128)(2,1)} %get-tuple-element.36.mine_ref) | copy-start | bytes 1474564
  54.6 25.3 %all-to-all-start.1 = ((bf16[32,80,256]{2,1,0:T(8,128)(2,1)}), bf16[32,80,256]{2,1,0:T(8,128)(2,1)S(1)}, u32[]{:S(2)}, u32[]{:S(2)}) async-start(bf16[32,80,256]{2,1,0:T(8,128)(2,1)} %get-tuple-element.42), calls=%async_computation.1 | async-start | bytes 2621440 | tf_op jit(solution)/shard_map/all_to_all | solution.py:583
  80.2 5.6 %collective-permute-start.10 = (f32[16,128]{1,0:T(8,128)S(1)}, f32[16,128]{1,0:T(8,128)S(1)}, u32[]{:S(2)}, u32[]{:S(2)}) collective-permute-start(f32[16,128]{1,0:T(8,128)S(1)} %get-tuple-element.49.own_ref), channel_id=1, source_target_pairs={{0,3},{1,2},{2,1},{3,0},{4,7},{5,6},{6,5},{7,4},{8,11},{9,10},{10,... | collective-permute-start | bytes 24584 | tf_op jit(solution)/shard_map/ppermute | solution.py:614
  82.3 5.2 %collective-permute-start.9 = (f32[16,128]{1,0:T(8,128)S(1)}, f32[16,128]{1,0:T(8,128)S(1)}, u32[]{:S(2)}, u32[]{:S(2)}) collective-permute-start(f32[16,128]{1,0:T(8,128)S(1)} %get-tuple-element.49.own_ref), channel_id=1, source_target_pairs={{0,2},{1,3},{2,0},{3,1},{4,6},{5,7},{6,4},{7,5},{8,10},{9,11},{10,... | collective-permute-start | bytes 24584 | tf_op jit(solution)/shard_map/ppermute | solution.py:614
  84.5 3.0 %collective-permute-start.8 = (f32[16,128]{1,0:T(8,128)S(1)}, f32[16,128]{1,0:T(8,128)S(1)}, u32[]{:S(2)}, u32[]{:S(2)}) collective-permute-start(f32[16,128]{1,0:T(8,128)S(1)} %get-tuple-element.49.own_ref), channel_id=1, source_target_pairs={{0,1},{1,0},{2,3},{3,2},{4,5},{5,4},{6,7},{7,6},{8,9},{9,8},{10,11... | collective-permute-start | bytes 24584 | tf_op jit(solution)/shard_map/ppermute | solution.py:614
  84.5 10.6 %collective-permute-start.7 = (bf16[2,64,256]{2,1,0:T(8,128)(2,1)S(1)}, bf16[2,64,256]{2,1,0:T(8,128)(2,1)S(1)}, u32[]{:S(2)}, u32[]{:S(2)}) collective-permute-start(bf16[2,64,256]{2,1,0:T(8,128)(2,1)S(1)} %get-tuple-element.46), channel_id=1, source_target_pairs={{28,96},{24,100},{20,104},{16,108},{12,112},{8,116},{4,120},{0,124... | collective-permute-start | bytes 196616 | tf_op jit(solution)/shard_map/ppermute | solution.py:610
  (2 other events, 1.5 us)

commit v7 on v6

--- a/solution.py
+++ b/solution.py
@@ -188,13 +188,13 @@
         for i, (source, into) in enumerate(
             (
                 (other_hbm.at[4 * GROUP :], other_ref),
-                (q_hbm, q_both),
-                (d_hbm, d_both),
-                (dt_hbm, dt_both),
                 (kv_hbm, all_ref.at[:group_size]),
                 (late_hbm.at[head], all_ref.at[own_late]),
                 (near_hbm, all_ref.at[near]),
                 (far_hbm, all_ref.at[far]),
+                (q_hbm, q_both),
+                (d_hbm, d_both),
+                (dt_hbm, dt_both),
             )
         )
     ]
@@ -222,7 +222,7 @@
 
     stage_ref[...] = jnp.zeros_like(stage_ref)
     sum_ref[...] = jnp.zeros_like(sum_ref)
-    for load in loads:
+    for load in loads[:6]:
         load.wait()
     all_ref[other_late, :, :HD] = other_ref[0]
     all_ref[other_late, :, HD:] = other_ref[1]
@@ -282,6 +282,12 @@
 
         total = lax.fori_loop(0, n_chunks, out_step, jnp.zeros((1, rows), jnp.float32))
         inverse = 1.0 / total
+
+        @pl.when(h == 0)
+        def _():
+            for late_load in loads[6:]:
+                late_load.wait()
+
         summed = acc_ref[...] * inverse
         delta = jnp.sum(summed * dt_both[h].astype(jnp.float32), axis=0, keepdims=True)
         row_ref[...] = jnp.transpose(summed)

time: 97.3 us -> 96.4 us (level); the launches traced: 95.8 us -> 96.3 us
  waiting for transfers between devices: 32.8 us -> 34.5 us
    all_to_all x1, waiting for transfers between devices: 13.6 us -> 15.5 us  [on_device(): got = lax.all_to_all(parts, 'ctx', 0, 0)]
    ppermute x3, waiting for transfers between devices: 1.63 us -> 0.59 us  [on_device(): lax.ppermute(sums, 'dp', [(i, i ^ step) for i in range(dp_size)])]
where the time goes in v7:
time: 96.4 us; the launch traced here: 96.3 us
  starting transfers between devices  36.8 us (38%)
  waiting for transfers between devices  34.5 us (36%)
  Pallas kernels  19.7 us (20%)
  local copies, waits for them, and re-layouts  3.83 us (4%)
    all_to_all x1, waiting for transfers between devices, on_device(): got = lax.all_to_all(parts, 'ctx', 0, 0)  15.5 us
    pallas_call x1, Pallas kernels, on_device(): pl.pallas_call(functools.partial(attention_kernel, group_size, reach), ou...  11.9 us
    all_to_all x1, starting transfers between devices, on_device(): got = lax.all_to_all(parts, 'ctx', 0, 0)  10.5 us
    all_to_all x1, starting transfers between devices, on_device(): gathered = lax.all_to_all(sent, 'ctx', 0, 0)  8.76 us
    all_to_all x1, waiting for transfers between devices, on_device(): gathered = lax.all_to_all(sent, 'ctx', 0, 0)  7.71 us
    ppermute x1, waiting for transfers between devices, on_device(): relay_grad = lax.ppermute(relay_total, 'ctx', back_along(relays))  7.28 us
    ppermute x1, starting transfers between devices, on_device(): relayed = lax.ppermute(early, 'ctx', relays)  5.81 us
    unnamed x26, local copies, waits for them, and re-layouts  3.82 us
  transfers between devices with their start and end apart: 13, of which 5 were waited for; matrix products, arithmetic and copies ran while one was open for 1% of the time, Pallas kernels for 4%

profile of v7, /device:TPU:24, one launch (start us, length us, event | category | flops | bytes accessed | tf_op | source)
XLA Modules:
  0.0 96.3 jit_solution(17749302379057483006)
XLA Ops:
  0.6 1.6 %blocks.1 = (bf16[2,64,256]{2,1,0:T(8,128)(2,1)}, bf16[2,64,256]{2,1,0:T(8,128)(2,1)}, bf16[64,256]{1,0:T(8,128)(2,1)}, bf16[64,256]{1,0:T(8,128)(2,1)}) custom-call(s32[1]{0:T(128)} %bitcast.me_ref, bf16[2,64,256]{2,1,0:T(8,128)(2,1)} %bitcast.16, bf16[2,64,256]{2,1,0:T(8,128)(2,1)} %bitcast.17, f32[1,256]{1,0:T(1,128)} %bitcast.18), custom_call_target="tpu_custom_call" | custom-call | tf_op jit(solution)/shard_map/blocks/pallas_call | solution.py:485
  2.3 5.8 %collective-permute-start.1 = (bf16[2,64,256]{2,1,0:T(8,128)(2,1)}, bf16[2,64,256]{2,1,0:T(8,128)(2,1)S(1)}, u32[]{:S(2)}, u32[]{:S(2)}) collective-permute-start(bf16[2,64,256]{2,1,0:T(8,128)(2,1)} %get-tuple-element.33.early_ref), channel_id=1, source_target_pairs={{96,28},{100,24},{104,20},{108,16},{112,12},{116,8},{120,4},{124,0... | collective-permute-start | bytes 196616 | tf_op jit(solution)/shard_map/ppermute | solution.py:499
  8.1 1.4 %collective-permute-start.2 = (bf16[64,256]{1,0:T(8,128)(2,1)}, bf16[64,256]{1,0:T(8,128)(2,1)S(1)}, u32[]{:S(2)}, u32[]{:S(2)}) collective-permute-start(bf16[64,256]{1,0:T(8,128)(2,1)} %get-tuple-element.34), channel_id=1, source_target_pairs={{120,64},{124,68},{112,72},{116,76},{104,80},{108,84},{96,88},{100... | collective-permute-start | bytes 98312 | tf_op jit(solution)/shard_map/ppermute | solution.py:500
  9.5 1.3 %collective-permute-start.3 = (bf16[64,256]{1,0:T(8,128)(2,1)}, bf16[64,256]{1,0:T(8,128)(2,1)S(1)}, u32[]{:S(2)}, u32[]{:S(2)}) collective-permute-start(bf16[64,256]{1,0:T(8,128)(2,1)} %get-tuple-element.35), channel_id=1, source_target_pairs={{124,64},{120,68},{116,72},{112,76},{108,80},{104,84},{100,88},{96... | collective-permute-start | bytes 98312 | tf_op jit(solution)/shard_map/ppermute | solution.py:501
  10.8 1.9 %swap.1 = bf16[30,64,128]{2,1,0:T(8,128)(2,1)} custom-call(s32[1]{0:T(128)} %bitcast.me_ref, bf16[2,64,1792]{2,1,0:T(8,128)(2,1)} %bitcast.12, bf16[2,64,1792]{2,1,0:T(8,128)(2,1)} %bitcast.14, bf16[2,64,256]{2,1,0:T(8,128)(2,1)} %get-tuple-element.29.late_hbm.late_ref), custom_call_target="tpu_custom_call" | custom-call | flops 1000000 | bytes 2000000 | tf_op jit(solution)/shard_map/swap/pallas_call | solution.py:502
  13.5 1.3 %send.1 = bf16[32,64,256]{2,1,0:T(8,128)(2,1)} custom-call(s32[1]{0:T(128)} %bitcast.me_ref, bf16[2,64,256]{2,1,0:T(8,128)(2,1)S(1)} %copy-done.3, bf16[2,64,256]{2,1,0:T(8,128)(2,1)S(1)} %copy-done.2, bf16[2,64,256]{2,1,0:T(8,128)(2,1)S(1)} %collective-permute-done.1.relay_ref, bf16[64,256]{1,0:T(8,128)(2,1)S(1)} %collective-permute-done.2.near_hbm, ...), custom_call_target="tpu_custom_call" | custom-call | tf_op jit(solution)/shard_map/send/pallas_call | solution.py:520
  14.8 8.8 %all-to-all-start = ((bf16[32,64,256]{2,1,0:T(8,128)(2,1)}), bf16[32,64,256]{2,1,0:T(8,128)(2,1)S(1)}, u32[]{:S(2)}, u32[]{:S(2)}) async-start(bf16[32,64,256]{2,1,0:T(8,128)(2,1)} %send.1), calls=%async_computation | async-start | bytes 2097152 | tf_op jit(solution)/shard_map/all_to_all | solution.py:532
  23.6 3.4 %collective-permute-done.other_ref.other_hbm = bf16[30,64,128]{2,1,0:T(8,128)(2,1)S(1)} collective-permute-done((bf16[30,64,128]{2,1,0:T(8,128)(2,1)}, bf16[30,64,128]{2,1,0:T(8,128)(2,1)S(1)}, u32[]{:S(2)}, u32[]{:S(2)}) %collective-permute-start) | collective-permute-done | bytes 491552 | tf_op jit(solution)/shard_map/ppermute | solution.py:519
  27.9 0.8 copy-done.8
  28.6 0.8 copy-done.9
  29.4 0.8 copy-done.10
  30.2 7.7 %all-to-all-done.kv_hbm = bf16[32,64,256]{2,1,0:T(8,128)(2,1)S(1)} async-done(((bf16[32,64,256]{2,1,0:T(8,128)(2,1)}), bf16[32,64,256]{2,1,0:T(8,128)(2,1)S(1)}, u32[]{:S(2)}, u32[]{:S(2)}) %all-to-all-start) | async-done | bytes 1048608 | tf_op jit(solution)/shard_map/all_to_all | solution.py:532
  37.9 1.0 %copy-done.11 = bf16[32,64,256]{2,1,0:T(8,128)(2,1)} copy-done((bf16[32,64,256]{2,1,0:T(8,128)(2,1)}, bf16[32,64,256]{2,1,0:T(8,128)(2,1)S(1)}, u32[]{:S(2)}) %copy-start.11) | copy-done | bytes 1048600
  38.9 11.9 %attention.1 = (bf16[30,64,128]{2,1,0:T(8,128)(2,1)}, bf16[30,64,128]{2,1,0:T(8,128)(2,1)}, bf16[32,80,256]{2,1,0:T(8,128)(2,1)}, bf16[64,256]{1,0:T(8,128)(2,1)}, bf16[64,256]{1,0:T(8,128)(2,1)}) custom-call(s32[1]{0:T(128)} %bitcast.me_ref, s32[1,16]{1,0:T(1,128)} %len_ref.1, bf16[2,896,128]{2,1,0:T(8,128)(2,1)} %copy-done.8, ...), custom_call_target="tpu_custom_call" | custom-call | flops 3000000000 | bytes 10000000 | tf_op jit(solution)/shard_map/attention/pallas_call | solution.py:546
  50.8 1.0 collective-permute-start.4
  51.7 1.3 %collective-permute-start.5 = (bf16[64,256]{1,0:T(8,128)(2,1)}, bf16[64,256]{1,0:T(8,128)(2,1)S(1)}, u32[]{:S(2)}, u32[]{:S(2)}) collective-permute-start(bf16[64,256]{1,0:T(8,128)(2,1)} %get-tuple-element.38), channel_id=1, source_target_pairs={{64,120},{68,124},{72,112},{76,116},{80,104},{84,108},{88,96},{92,... | collective-permute-start | bytes 98312 | tf_op jit(solution)/shard_map/ppermute | solution.py:587
  53.0 1.3 %collective-permute-start.6 = (bf16[64,256]{1,0:T(8,128)(2,1)}, bf16[64,256]{1,0:T(8,128)(2,1)S(1)}, u32[]{:S(2)}, u32[]{:S(2)}) collective-permute-start(bf16[64,256]{1,0:T(8,128)(2,1)} %get-tuple-element.39), channel_id=1, source_target_pairs={{64,124},{68,120},{72,116},{76,112},{80,108},{84,104},{88,100},{92... | collective-permute-start | bytes 98312 | tf_op jit(solution)/shard_map/ppermute | solution.py:588
  54.3 10.5 %all-to-all-start.1 = ((bf16[32,80,256]{2,1,0:T(8,128)(2,1)}), bf16[32,80,256]{2,1,0:T(8,128)(2,1)S(1)}, u32[]{:S(2)}, u32[]{:S(2)}) async-start(bf16[32,80,256]{2,1,0:T(8,128)(2,1)} %get-tuple-element.42), calls=%async_computation.1 | async-start | bytes 2621440 | tf_op jit(solution)/shard_map/all_to_all | solution.py:589
  64.9 1.1 %join.1 = (bf16[2,64,1792]{2,1,0:T(8,128)(2,1)}, bf16[2,64,1792]{2,1,0:T(8,128)(2,1)}, bf16[64,256]{1,0:T(8,128)(2,1)S(1)}, bf16[64,256]{1,0:T(8,128)(2,1)S(1)}) custom-call(s32[1]{0:T(128)} %bitcast.me_ref, bf16[30,64,128]{2,1,0:T(8,128)(2,1)S(1)} %copy-done.7, bf16[30,64,128]{2,1,0:T(8,128)(2,1)S(1)} %collective-permute-done.4.theirs_ref, ...), custom_call_target="tpu_custom_call" | custom-call | flops 40000000000 | bytes 4000000 | tf_op jit(solution)/shard_map/join/pallas_call | solution.py:592
  66.0 15.5 %all-to-all-done.1.got_ref = bf16[32,80,256]{2,1,0:T(8,128)(2,1)S(1)} async-done(((bf16[32,80,256]{2,1,0:T(8,128)(2,1)}), bf16[32,80,256]{2,1,0:T(8,128)(2,1)S(1)}, u32[]{:S(2)}, u32[]{:S(2)}) %all-to-all-start.1) | async-done | bytes 1310752 | tf_op jit(solution)/shard_map/all_to_all | solution.py:589
  81.9 0.7 collective-permute-start.9
  82.6 2.6 %collective-permute-start.8 = (f32[16,128]{1,0:T(8,128)S(1)}, f32[16,128]{1,0:T(8,128)S(1)}, u32[]{:S(2)}, u32[]{:S(2)}) collective-permute-start(f32[16,128]{1,0:T(8,128)S(1)} %get-tuple-element.49.own_ref), channel_id=1, source_target_pairs={{0,1},{1,0},{2,3},{3,2},{4,5},{5,4},{6,7},{7,6},{8,9},{9,8},{10,11... | collective-permute-start | bytes 24584 | tf_op jit(solution)/shard_map/ppermute | solution.py:620
  85.2 1.3 %collective-permute-start.7 = (bf16[2,64,256]{2,1,0:T(8,128)(2,1)S(1)}, bf16[2,64,256]{2,1,0:T(8,128)(2,1)S(1)}, u32[]{:S(2)}, u32[]{:S(2)}) collective-permute-start(bf16[2,64,256]{2,1,0:T(8,128)(2,1)S(1)} %get-tuple-element.46), channel_id=1, source_target_pairs={{28,96},{24,100},{20,104},{16,108},{12,112},{8,116},{4,120},{0,124... | collective-permute-start | bytes 196616 | tf_op jit(solution)/shard_map/ppermute | solution.py:616
  88.3 7.3 %collective-permute-done.7.relay_ref = bf16[2,64,256]{2,1,0:T(8,128)(2,1)S(1)} collective-permute-done((bf16[2,64,256]{2,1,0:T(8,128)(2,1)S(1)}, bf16[2,64,256]{2,1,0:T(8,128)(2,1)S(1)}, u32[]{:S(2)}, u32[]{:S(2)}) %collective-permute-start.7) | collective-permute-done | bytes 65568 | tf_op jit(solution)/shard_map/ppermute | solution.py:616
  (39 shorter events, 4.4 us)
Async XLA Ops:
  2.2 11.2 %copy-start.2 = (bf16[2,64,256]{2,1,0:T(8,128)(2,1)S(1)}, bf16[2,64,256]{2,1,0:T(8,128)(2,1)}, u32[]{:S(2)}) copy-start(bf16[2,64,256]{2,1,0:T(8,128)(2,1)} %get-tuple-element.29.late_hbm.late_ref) | copy-start | bytes 196612
  2.2 11.2 %copy-start.3 = (bf16[2,64,256]{2,1,0:T(8,128)(2,1)S(1)}, bf16[2,64,256]{2,1,0:T(8,128)(2,1)}, u32[]{:S(2)}) copy-start(bf16[2,64,256]{2,1,0:T(8,128)(2,1)} %get-tuple-element.33.early_ref) | copy-start | bytes 196612
  2.3 11.2 %collective-permute-start.1 = (bf16[2,64,256]{2,1,0:T(8,128)(2,1)}, bf16[2,64,256]{2,1,0:T(8,128)(2,1)S(1)}, u32[]{:S(2)}, u32[]{:S(2)}) collective-permute-start(bf16[2,64,256]{2,1,0:T(8,128)(2,1)} %get-tuple-element.33.early_ref), channel_id=1, source_target_pairs={{96,28},{100,24},{104,20},{108,16},{112,12},{116,8},{120,4},{124,0... | collective-permute-start | bytes 196616 | tf_op jit(solution)/shard_map/ppermute | solution.py:499
  8.1 5.4 %collective-permute-start.2 = (bf16[64,256]{1,0:T(8,128)(2,1)}, bf16[64,256]{1,0:T(8,128)(2,1)S(1)}, u32[]{:S(2)}, u32[]{:S(2)}) collective-permute-start(bf16[64,256]{1,0:T(8,128)(2,1)} %get-tuple-element.34), channel_id=1, source_target_pairs={{120,64},{124,68},{112,72},{116,76},{104,80},{108,84},{96,88},{100... | collective-permute-start | bytes 98312 | tf_op jit(solution)/shard_map/ppermute | solution.py:500
  9.5 3.9 %collective-permute-start.3 = (bf16[64,256]{1,0:T(8,128)(2,1)}, bf16[64,256]{1,0:T(8,128)(2,1)S(1)}, u32[]{:S(2)}, u32[]{:S(2)}) collective-permute-start(bf16[64,256]{1,0:T(8,128)(2,1)} %get-tuple-element.35), channel_id=1, source_target_pairs={{124,64},{120,68},{116,72},{112,76},{108,80},{104,84},{100,88},{96... | collective-permute-start | bytes 98312 | tf_op jit(solution)/shard_map/ppermute | solution.py:501
  12.8 14.3 %collective-permute-start = (bf16[30,64,128]{2,1,0:T(8,128)(2,1)}, bf16[30,64,128]{2,1,0:T(8,128)(2,1)S(1)}, u32[]{:S(2)}, u32[]{:S(2)}) collective-permute-start(bf16[30,64,128]{2,1,0:T(8,128)(2,1)} %swap.1), channel_id=1, source_target_pairs={{0,4},{4,0},{8,12},{12,8},{16,20},{20,16},{24,28},{28,24},{32,36},... | collective-permute-start | bytes 1474568 | tf_op jit(solution)/shard_map/ppermute | solution.py:519
  13.4 1.4 %copy-start.4 = (bf16[64,256]{1,0:T(8,128)(2,1)}, bf16[64,256]{1,0:T(8,128)(2,1)S(1)}, u32[]{:S(2)}) copy-start(bf16[64,256]{1,0:T(8,128)(2,1)S(1)} %collective-permute-done.2.near_hbm) | copy-start | bytes 98308
  13.5 1.4 %copy-start.5 = (bf16[64,256]{1,0:T(8,128)(2,1)}, bf16[64,256]{1,0:T(8,128)(2,1)S(1)}, u32[]{:S(2)}) copy-start(bf16[64,256]{1,0:T(8,128)(2,1)S(1)} %collective-permute-done.3.far_hbm) | copy-start | bytes 98308
  14.8 8.8 %copy-start.12 = (f32[1792]{0:T(1024)S(1)}, f32[1792]{0:T(1024)}, u32[]{:S(2)}) copy-start(f32[1792]{0:T(1024)} %param.10) | copy-start | bytes 21508
  14.8 12.3 %copy-start = (bf16[1,2,64,1792]{3,2,1,0:T(8,128)(2,1)S(1)}, bf16[1,2,64,1792]{3,2,1,0:T(8,128)(2,1)}, u32[]{:S(2)}) copy-start(bf16[1,2,64,1792]{3,2,1,0:T(8,128)(2,1)} %param.7) | copy-start | bytes 1376260
  14.8 12.3 %copy-start.1 = (bf16[1,2,64,1792]{3,2,1,0:T(8,128)(2,1)S(1)}, bf16[1,2,64,1792]{3,2,1,0:T(8,128)(2,1)}, u32[]{:S(2)}) copy-start(bf16[1,2,64,1792]{3,2,1,0:T(8,128)(2,1)} %param.12) | copy-start | bytes 1376260
  14.8 23.0 %all-to-all-start = ((bf16[32,64,256]{2,1,0:T(8,128)(2,1)}), bf16[32,64,256]{2,1,0:T(8,128)(2,1)S(1)}, u32[]{:S(2)}, u32[]{:S(2)}) async-start(bf16[32,64,256]{2,1,0:T(8,128)(2,1)} %send.1), calls=%async_computation | async-start | bytes 2097152 | tf_op jit(solution)/shard_map/all_to_all | solution.py:532
  27.1 0.8 copy-start.6
  29.4 0.8 copy-start.10
  37.9 1.0 %copy-start.11 = (bf16[32,64,256]{2,1,0:T(8,128)(2,1)}, bf16[32,64,256]{2,1,0:T(8,128)(2,1)S(1)}, u32[]{:S(2)}) copy-start(bf16[32,64,256]{2,1,0:T(8,128)(2,1)S(1)} %all-to-all-done.kv_hbm) | copy-start | bytes 3145732
  50.8 14.1 %collective-permute-start.4 = (bf16[30,64,128]{2,1,0:T(8,128)(2,1)}, bf16[30,64,128]{2,1,0:T(8,128)(2,1)S(1)}, u32[]{:S(2)}, u32[]{:S(2)}) collective-permute-start(bf16[30,64,128]{2,1,0:T(8,128)(2,1)} %get-tuple-element.37), channel_id=1, source_target_pairs={{0,4},{4,0},{8,12},{12,8},{16,20},{20,16},{24,28},{28,24},{32,36},... | collective-permute-start | bytes 1474568 | tf_op jit(solution)/shard_map/ppermute | solution.py:586
  51.7 13.1 %collective-permute-start.5 = (bf16[64,256]{1,0:T(8,128)(2,1)}, bf16[64,256]{1,0:T(8,128)(2,1)S(1)}, u32[]{:S(2)}, u32[]{:S(2)}) collective-permute-start(bf16[64,256]{1,0:T(8,128)(2,1)} %get-tuple-element.38), channel_id=1, source_target_pairs={{64,120},{68,124},{72,112},{76,116},{80,104},{84,108},{88,96},{92,... | collective-permute-start | bytes 98312 | tf_op jit(solution)/shard_map/ppermute | solution.py:587
  53.0 11.9 %collective-permute-start.6 = (bf16[64,256]{1,0:T(8,128)(2,1)}, bf16[64,256]{1,0:T(8,128)(2,1)S(1)}, u32[]{:S(2)}, u32[]{:S(2)}) collective-permute-start(bf16[64,256]{1,0:T(8,128)(2,1)} %get-tuple-element.39), channel_id=1, source_target_pairs={{64,124},{68,120},{72,116},{76,112},{80,108},{84,104},{88,100},{92... | collective-permute-start | bytes 98312 | tf_op jit(solution)/shard_map/ppermute | solution.py:588
  54.3 10.6 %copy-start.7 = (bf16[30,64,128]{2,1,0:T(8,128)(2,1)S(1)}, bf16[30,64,128]{2,1,0:T(8,128)(2,1)}, u32[]{:S(2)}) copy-start(bf16[30,64,128]{2,1,0:T(8,128)(2,1)} %get-tuple-element.36.mine_ref) | copy-start | bytes 1474564
  54.3 27.2 %all-to-all-start.1 = ((bf16[32,80,256]{2,1,0:T(8,128)(2,1)}), bf16[32,80,256]{2,1,0:T(8,128)(2,1)S(1)}, u32[]{:S(2)}, u32[]{:S(2)}) async-start(bf16[32,80,256]{2,1,0:T(8,128)(2,1)} %get-tuple-element.42), calls=%async_computation.1 | async-start | bytes 2621440 | tf_op jit(solution)/shard_map/all_to_all | solution.py:589
  81.8 4.7 %collective-permute-start.10 = (f32[16,128]{1,0:T(8,128)S(1)}, f32[16,128]{1,0:T(8,128)S(1)}, u32[]{:S(2)}, u32[]{:S(2)}) collective-permute-start(f32[16,128]{1,0:T(8,128)S(1)} %get-tuple-element.49.own_ref), channel_id=1, source_target_pairs={{0,3},{1,2},{2,1},{3,0},{4,7},{5,6},{6,5},{7,4},{8,11},{9,10},{10,... | collective-permute-start | bytes 24584 | tf_op jit(solution)/shard_map/ppermute | solution.py:620
  81.9 5.2 %collective-permute-start.9 = (f32[16,128]{1,0:T(8,128)S(1)}, f32[16,128]{1,0:T(8,128)S(1)}, u32[]{:S(2)}, u32[]{:S(2)}) collective-permute-start(f32[16,128]{1,0:T(8,128)S(1)} %get-tuple-element.49.own_ref), channel_id=1, source_target_pairs={{0,2},{1,3},{2,0},{3,1},{4,6},{5,7},{6,4},{7,5},{8,10},{9,11},{10,... | collective-permute-start | bytes 24584 | tf_op jit(solution)/shard_map/ppermute | solution.py:620
  82.6 4.5 %collective-permute-start.8 = (f32[16,128]{1,0:T(8,128)S(1)}, f32[16,128]{1,0:T(8,128)S(1)}, u32[]{:S(2)}, u32[]{:S(2)}) collective-permute-start(f32[16,128]{1,0:T(8,128)S(1)} %get-tuple-element.49.own_ref), channel_id=1, source_target_pairs={{0,1},{1,0},{2,3},{3,2},{4,5},{5,4},{6,7},{7,6},{8,9},{9,8},{10,11... | collective-permute-start | bytes 24584 | tf_op jit(solution)/shard_map/ppermute | solution.py:620
  85.2 10.4 %collective-permute-start.7 = (bf16[2,64,256]{2,1,0:T(8,128)(2,1)S(1)}, bf16[2,64,256]{2,1,0:T(8,128)(2,1)S(1)}, u32[]{:S(2)}, u32[]{:S(2)}) collective-permute-start(bf16[2,64,256]{2,1,0:T(8,128)(2,1)S(1)} %get-tuple-element.46), channel_id=1, source_target_pairs={{28,96},{24,100},{20,104},{16,108},{12,112},{8,116},{4,120},{0,124... | collective-permute-start | bytes 196616 | tf_op jit(solution)/shard_map/ppermute | solution.py:616
  (2 other events, 1.5 us)
